TPU v7x, 32 devices: a whole 2x2x4 slice. The times are simulated.
32 devices in a mesh: row: 4 (over y, core), col: 8 (over z, x).
Axes of the slice: x: 2, y: 2, z: 4, core: 2. Of those that a mesh axis runs over, the one named last changes fastest.
Arguments:
- features: bfloat16 [8192, 128], P(('col', 'row')), may hold values from -6 to 6
- weight: bfloat16 [128, 128], replicated, may hold values from -0.5 to 0.5
- tiles: bfloat16 [4, 8, 44, 128, 128], P('row', 'col'), may hold values from -0.15625 to 0.15625
- tile_slots: int32 [4, 8, 44], P('row', 'col'), may hold values from 0 to 127, as said below
- tile_counts: int32 [4, 8], P('row', 'col'), may hold values from 5 to 44, as said below
- cotangent: bfloat16 [8192, 128], P(('row', 'col')), may hold values from -6 to 6
Outputs:
- hidden: bfloat16 [8192, 128], P(('row', 'col'))
- feature_grad: bfloat16 [8192, 128], P(('col', 'row'))
- weight_grad: float32 [128, 128], replicated
Inputs may be any that keep to these rules, and one draw needn't show every extreme that they name: `tile_slots`: the slots of one block are distinct. `tile_counts`: some block has all 44 slots live.
All inputs are finite; a program needn't handle non-finite values.
Results may differ from a plain program's by a relative error of at most 0.006.
Values may be sent and summed in bfloat16 or wider, within the bound.
No kernel may reach another device: no remote copies, remote signals or barrier semaphores. Data moves between devices by JAX's collectives and lax.ppermute only.
A program may use at most 128 MiB of HBM per device.

v0:
```python
import math

import jax
import jax.numpy as jnp
from jax import lax
from jax.sharding import PartitionSpec as P


def silu_grad(values):
    sig = jax.nn.sigmoid(values)
    return sig * (1.0 + values * (1.0 - sig))


def body(features, weight, tiles, tile_slots, tile_counts, cotangent):
    tile_vals = tiles[0, 0]
    slot_ids = tile_slots[0, 0]
    live_count = tile_counts[0, 0]
    tile_size = tile_vals.shape[-1]
    share_rows = features.shape[0]
    width = features.shape[1]
    slot_total = slot_ids.shape[0]
    row_count = lax.axis_size("row")
    col_count = lax.axis_size("col")
    tile_rows = share_rows * col_count // tile_size
    tile_cols = share_rows * row_count // tile_size
    col_index = lax.axis_index("col")
    projected = jnp.dot(features, weight, preferred_element_type=jnp.float32).astype(jnp.bfloat16)
    proj_block = lax.all_gather(projected, "row", axis=0, tiled=True)
    is_live = jnp.arange(slot_total, dtype=jnp.int32) < live_count
    gathered = proj_block.reshape(tile_cols, tile_size, width)[slot_ids % tile_cols]
    products = jnp.einsum("tij,tjf->tif", tile_vals, gathered, preferred_element_type=jnp.float32)
    fwd_targets = jnp.where(is_live, slot_ids // tile_cols, tile_rows)
    partial_value = jax.ops.segment_sum(products, fwd_targets, tile_rows + 1)[:tile_rows].reshape(
        tile_rows * tile_size, width
    )
    summed = lax.psum(partial_value, "col")
    own_rows = lax.dynamic_slice_in_dim(summed, col_index * share_rows, share_rows, 0)
    hidden = jax.nn.silu(own_rows).astype(jnp.bfloat16)
    cot_block = lax.all_gather(cotangent, "col", axis=0, tiled=True)
    grad_block = (cot_block.astype(jnp.float32) * silu_grad(summed)).astype(jnp.bfloat16)
    grad_tiles = grad_block.reshape(tile_rows, tile_size, width)[slot_ids // tile_cols]
    back_products = jnp.einsum(
        "tji,tjf->tif", tile_vals, grad_tiles, preferred_element_type=jnp.float32
    )
    back_targets = jnp.where(is_live, slot_ids % tile_cols, tile_cols)
    back_partial = jax.ops.segment_sum(back_products, back_targets, tile_cols + 1)[
        :tile_cols
    ].reshape(tile_cols * tile_size, width)
    grad_proj = lax.psum_scatter(back_partial, "row", scatter_dimension=0, tiled=True).astype(
        jnp.bfloat16
    )
    feature_grad = jnp.dot(grad_proj, weight.T, preferred_element_type=jnp.float32).astype(
        jnp.bfloat16
    )
    weight_term = jnp.dot(features.T, grad_proj, preferred_element_type=jnp.float32)
    node_total = share_rows * row_count * col_count
    weight_grad = lax.psum(weight_term, ("row", "col")) / math.sqrt(node_total)
    return (hidden, feature_grad, weight_grad)


def solution(mesh):
    placed = (
        P(("col", "row"), None),
        P(),
        P("row", "col", None, None, None),
        P("row", "col", None),
        P("row", "col"),
        P(("row", "col"), None),
    )
    return jax.shard_map(
        body,
        mesh=mesh,
        in_specs=placed,
        out_specs=(P(("row", "col"), None), P(("col", "row"), None), P()),
        check_vma=False,
    )
```

profile of v0, /device:TPU:0, one launch (start us, length us, event | category | flops | bytes accessed | tf_op | source)
XLA Modules:
  0.0 282.8 jit_solution(3687551441933391329)
XLA Ops:
  7.2 0.0 copy-start
  7.2 0.0 all-reduce.3.cloned.1.call-start
  7.2 0.8 fusion.7
  8.7 1.0 convolution_convert_fusion.1
  9.7 7.2 %all_gather.6 = bf16[1024,128]{1,0:T(8,128)(2,1)S(1)} all-gather(bf16[256,128]{1,0:T(8,128)(2,1)S(1)} %convolution_convert_fusion.1), channel_id=1, replica_groups=mesh['row'=4,'col'=8] {'row'}, dimensions={0}, use_global_device_ids=true | all-gather | bytes 327680 | tf_op jit(solution)/shard_map/all_gather | solution.py:28
  16.9 0.8 gather_fusion
  17.7 0.0 copy-done
  17.7 2.7 convolution_bitcast_fusion.1
  20.5 3.4 %copy.13 = f32[44,128,128]{2,1,0:T(8,128)} copy(f32[44,128,128]{1,2,0:T(8,128)} %convolution_bitcast_fusion.1) | data formatting | bytes 5767168 | tf_op jit(solution)/shard_map/tij,tjf->tif/dot_general | solution.py:31
  23.9 0.1 broadcast_in_dim.15
  24.0 6.6 %scatter_fusion = f32[17,128,128]{2,1,0:T(8,128)S(1)} fusion(f32[17,128,128]{2,1,0:T(8,128)S(1)} %broadcast_in_dim.15, s32[44]{0:T(128)S(1)} %get-tuple-element.14, f32[44,128,128]{2,1,0:T(8,128)} %copy.13), kind=kCustom, calls=%fused_computation.2 | custom fusion | flops 720896 | bytes 8650928 | tf_op jit(solution)/shard_map/scatter-add | solution.py:33
  30.6 0.0 copy-start.3
  30.6 1.1 slice.12
  31.7 0.0 all-reduce.3.cloned.1.call-update
  31.7 0.0 reduce-scatter.2.cloned.1.call-start
  31.8 0.0 copy-done.3
  31.8 33.1 %all_gather.7 = bf16[2048,128]{1,0:T(8,128)(2,1)S(1)} all-gather(bf16[256,128]{1,0:T(8,128)(2,1)S(1)} %copy-done.3), channel_id=1, replica_groups=mesh['row'=4,'col'=8] {'col'}, dimensions={0}, use_global_device_ids=true | all-gather | bytes 589824 | tf_op jit(solution)/shard_map/all_gather | solution.py:39
  64.9 49.1 %all-reduce.3.cloned.1.call-done = f32[2048,128]{1,0:T(8,128)} async-done(((f32[2048,128]{1,0:T(8,128)}), f32[2048,128]{1,0:T(8,128)}) %all-reduce.3.cloned.1.call-update) | async-done | bytes 1048592 | tf_op jit(solution)/shard_map/psum | solution.py:36
  113.9 1.6 multiply_convert_fusion
  115.6 0.8 gather_fusion.1
  116.4 2.2 convolution_bitcast_fusion
  118.6 3.4 %copy.15 = f32[44,128,128]{2,1,0:T(8,128)} copy(f32[44,128,128]{1,2,0:T(8,128)} %convolution_bitcast_fusion) | data formatting | bytes 5767168 | tf_op jit(solution)/shard_map/tji,tjf->tif/dot_general | solution.py:42
  122.1 6.6 %scatter_fusion.1 = f32[9,128,128]{2,1,0:T(8,128)S(1)} fusion(f32[9,128,128]{2,1,0:T(8,128)S(1)} %broadcast_in_dim.17, s32[44]{0:T(128)S(1)} %get-tuple-element.12, f32[44,128,128]{2,1,0:T(8,128)} %copy.15), kind=kCustom, calls=%fused_computation.3 | custom fusion | flops 720896 | bytes 8650928 | tf_op jit(solution)/shard_map/scatter-add | solution.py:46
  128.7 0.0 copy-start.1
  128.7 0.0 copy-start.2
  128.8 0.8 slice.13
  129.6 0.0 reduce-scatter.2.cloned.1.call-update
  129.6 0.0 all-reduce.5.cloned.1.call-start
  129.7 1.6 multiply_convert_fusion.1
  131.2 19.7 %reduce-scatter.2.cloned.1.call-done = f32[256,128]{1,0:T(8,128)} async-done(((f32[1024,128]{1,0:T(8,128)}), f32[256,128]{1,0:T(8,128)}) %reduce-scatter.2.cloned.1.call-update) | async-done | bytes 131088 | tf_op jit(solution)/shard_map/reduce_scatter | solution.py:49
  151.0 0.0 copy-done.1
  151.0 1.7 convolution_bitcast_fusion.2
  152.7 0.0 all-reduce.5.cloned.1.call-update
  152.7 0.0 copy-done.2
  152.8 1.7 convolution_convert_fusion
  154.5 120.2 %all-reduce.5.cloned.1.call-done = f32[128,128]{0,1:T(8,128)} async-done(((f32[128,128]{0,1:T(8,128)}), f32[128,128]{0,1:T(8,128)}) %all-reduce.5.cloned.1.call-update) | async-done | bytes 65552 | tf_op jit(solution)/shard_map/psum | solution.py:57
  274.7 0.8 broadcast_multiply_fusion
  275.5 0.7 copy.16
  (4 shorter events, 0.1 us)
Async XLA Ops:
  7.2 10.6 %copy-start = (bf16[1,1,44,128,128]{4,3,2,1,0:T(8,128)(2,1)S(1)}, bf16[1,1,44,128,128]{4,3,2,1,0:T(8,128)(2,1)}, u32[]{:S(2)}) copy-start(bf16[1,1,44,128,128]{4,3,2,1,0:T(8,128)(2,1)} %param.8) | copy-start | bytes 4325380
  7.2 106.8 %all-reduce.3.cloned.1.call-start = ((), (), s32[]{:S(2)}) async-start(), calls=%async_computation.1 | async-start | bytes 2097152 | tf_op jit(solution)/shard_map/psum | solution.py:36
  30.6 1.2 copy-start.3
  31.7 119.3 %reduce-scatter.2.cloned.1.call-start = ((), (), s32[]{:S(2)}) async-start(), calls=%async_computation.2 | async-start | bytes 655360 | tf_op jit(solution)/shard_map/reduce_scatter | solution.py:49
  128.7 22.3 %copy-start.1 = (bf16[256,128]{1,0:T(8,128)(2,1)S(1)}, bf16[256,128]{1,0:T(8,128)(2,1)}, u32[]{:S(2)}) copy-start(bf16[256,128]{1,0:T(8,128)(2,1)} %param.6) | copy-start | bytes 196612
  128.7 24.0 %copy-start.2 = (bf16[128,128]{1,0:T(8,128)(2,1)S(1)}, bf16[128,128]{1,0:T(8,128)(2,1)}, u32[]{:S(2)}) copy-start(bf16[128,128]{1,0:T(8,128)(2,1)} %param.7) | copy-start | bytes 98308
  129.6 145.1 %all-reduce.5.cloned.1.call-start = ((), (), s32[]{:S(2)}) async-start(), calls=%async_computation.3 | async-start | bytes 131072 | tf_op jit(solution)/shard_map/psum | solution.py:57
Sparse Core Ops, SparseCore 0:
  31.9 82.0 all-reduce.2
  129.7 21.2 reduce-scatter.1
  157.1 117.4 all-reduce.4
where the time goes:
time: 285 us; the launch traced here: 283 us
  waiting for transfers between devices  189 us (66%)
  blocking collectives  40.3 us (14%)
  other arithmetic  18.1 us (6%)
  between operations  14.5 us (5%)
  local copies, waits for them, and re-layouts  11.3 us (4%)
  matrix products  9.38 us (3%)
    psum x1, waiting for transfers between devices, body(): weight_grad = lax.psum(weight_term, ('row', 'col')) / math.sqrt(node_total)  120 us
    psum x1, waiting for transfers between devices, body(): summed = lax.psum(partial_value, 'col')  49.1 us
    all_gather x1, blocking collectives, body(): cot_block = lax.all_gather(cotangent, 'col', axis=0, tiled=True)  33.1 us
    reduce_scatter x1, waiting for transfers between devices, body(): lax.psum_scatter(back_partial, 'row', scatter_dimension=0, tiled=True)  19.7 us
    all_gather x1, blocking collectives, body(): proj_block = lax.all_gather(projected, 'row', axis=0, tiled=True)  7.22 us
    scatter-add x1, other arithmetic, body(): jax.ops.segment_sum(products, fwd_targets, tile_rows + 1)[:tile_rows]  6.63 us
    scatter-add x1, other arithmetic, body(): jax.ops.segment_sum(back_products, back_targets, tile_cols + 1)[:tile_cols]  6.62 us
  transfers between devices with their start and end apart: 3, of which 3 were waited for; matrix products, arithmetic and copies ran while one was open for 1% of the time, Pallas kernels for 0%

commit v1 on v0

v1 whole, which is shorter than its diff:
```python
import functools
import math

import jax
import jax.numpy as jnp
from jax import lax
from jax.experimental import pallas as pl
from jax.experimental.pallas import tpu as pltpu
from jax.sharding import PartitionSpec as P

F32 = jnp.float32
BF16 = jnp.bfloat16
VMEM_LIMIT = 24 * 1024 * 1024
DENSE_LIMIT = 12 * 1024 * 1024


def in_vmem(x):
    return pltpu.with_memory_space_constraint(x, pltpu.VMEM)


def in_hbm(x):
    return pltpu.with_memory_space_constraint(x, pltpu.HBM)


def kernel_call(kernel, outs, flops, name, in_specs, scratch=(), limit=VMEM_LIMIT):
    shapes = [pltpu.VMEM(s, d) if keep else jax.ShapeDtypeStruct(s, d) for s, d, keep in outs]
    moved = sum(math.prod(s) * jnp.dtype(d).itemsize for s, d, _ in outs)
    return pl.pallas_call(
        kernel,
        out_shape=shapes,
        in_specs=in_specs,
        out_specs=[pl.BlockSpec(memory_space=pltpu.VMEM)] * len(outs),
        scratch_shapes=list(scratch),
        compiler_params=pltpu.CompilerParams(vmem_limit_bytes=limit),
        cost_estimate=pl.CostEstimate(flops=flops, bytes_accessed=moved, transcendentals=0),
        name=name,
    )


VM = pl.BlockSpec(memory_space=pltpu.VMEM)
ANY = pl.BlockSpec(memory_space=pl.ANY)


def bit_reverse(value, bits):
    out = 0
    for b in range(bits):
        out = out | (((value >> b) & 1) << (bits - 1 - b))
    return out


def slot_masks(near):
    return {0: [], 1: [(1, 1)], 2: [(2, 2), (1, 1), (3, 3)]}[near]


def sum_mask(bit, near):
    return 3 << (bit - 1) if bit == near and near else 1 << bit


def place_of(slot, row_bits, near, share_tiles, group_tiles):
    my_row = lax.axis_index("row")
    my_col = lax.axis_index("col")
    tile_cols = share_tiles << row_bits
    tile_row = lax.div(slot, tile_cols)
    tile_col = lax.rem(slot, tile_cols)
    row_share = lax.div(tile_row, share_tiles)
    apart = row_share ^ my_col
    if near:
        apart = apart ^ (((apart >> near) & 1) << (near - 1))
    mask = apart & ((1 << near) - 1)
    group = mask * 0
    for at, (even, odd) in enumerate(slot_masks(near)):
        group = jnp.where(mask == jnp.where((my_row & 1) == 1, odd, even), at + 1, group)
    row_at = group * group_tiles + (row_share >> near) * share_tiles + lax.rem(tile_row, share_tiles)
    col_share = bit_reverse(lax.div(tile_col, share_tiles) ^ my_row, row_bits)
    return row_at, col_share * share_tiles + lax.rem(tile_col, share_tiles)


def densify(place, tiles_ref, slots_ref, count_ref, dense_ref, held, slots, count, sems):
    copies = [
        pltpu.make_async_copy(count_ref, count, sems.at[0]),
        pltpu.make_async_copy(slots_ref, slots, sems.at[1]),
        pltpu.make_async_copy(tiles_ref.at[0, 0], held, sems.at[2]),
    ]
    for copy in copies:
        copy.start()
    dense_ref[...] = jnp.zeros_like(dense_ref)
    size = held.shape[-1]
    for copy in copies:
        copy.wait()

    def step(k, carry):
        row_at, col_at = place(slots[0, 0, k])
        rows = pl.ds(pl.multiple_of(row_at * size, size), size)
        cols = pl.ds(pl.multiple_of(col_at * size, size), size)
        dense_ref[rows, cols] = held[k]
        return carry

    lax.fori_loop(0, count[0, 0], step, 0)


def forward(parts, *refs):
    dense_ref, pieces, outs = refs[0], refs[1 : 1 + parts], refs[1 + parts :]
    group = outs[0].shape[0]
    for m in [*range(1, len(outs)), 0]:
        total, at = None, 0
        for piece in pieces:
            depth = piece.shape[0]
            term = jnp.dot(
                dense_ref[m * group : (m + 1) * group, at : at + depth], piece[...], preferred_element_type=F32
            )
            total = term if total is None else total + term
            at += depth
        outs[m][...] = total.astype(outs[m].dtype)


def middle(near, share, left_ref, right_ref, weight_ref, *refs):
    cot_refs, (send_ref, hidden_ref, high_ref, low_ref) = refs[:-4], refs[-4:]
    group = high_ref.shape[0]
    place = lax.axis_index("col") >> near
    weight = weight_ref[...]
    at = 0
    for cot_ref in cot_refs:
        for start in range(0, cot_ref.shape[0], share):
            rows = pl.ds(pl.multiple_of((place ^ at) * share, share), share)
            agg = left_ref[rows, :].astype(F32) + right_ref[rows, :].astype(F32)
            high = agg.astype(BF16)
            low = (agg - high.astype(F32)).astype(BF16)
            high_ref[rows, :] = high
            low_ref[rows, :] = low
            summed = jnp.dot(high, weight, preferred_element_type=F32)
            summed += jnp.dot(low, weight, preferred_element_type=F32)
            gate = 1.0 / (1.0 + jnp.exp(-summed))
            if at == 0:
                hidden_ref[...] = (summed * gate).astype(BF16)
            slope = gate * (1.0 + summed * (1.0 - gate))
            send_ref[rows, :] = (cot_ref[start : start + share, :].astype(F32) * slope).astype(BF16)
            at += 1
    dims = (((0,), (0,)), ((), ()))
    grad = send_ref[:group, :]
    term = lax.dot_general(high_ref[...], grad, dims, preferred_element_type=F32)
    term += lax.dot_general(low_ref[...], grad, dims, preferred_element_type=F32)
    send_ref[group:, :] = term.astype(BF16)


def pair_sums(terms):
    while len(terms) > 1:
        terms = [a + b for a, b in zip(terms[::2], terms[1::2])]
    return terms[0]


def backward(dense_ref, *refs):
    grads, (send_ref, keep_ref) = refs[:-2], refs[-2:]
    kept = keep_ref.shape[0]
    group = dense_ref.shape[0] // len(grads)
    dims = (((0,), (0,)), ((), ()))

    def product(cols):
        total = None
        for m, grad in enumerate(grads):
            term = lax.dot_general(
                grad[:group, :], dense_ref[m * group : (m + 1) * group, cols], dims, preferred_element_type=F32
            )
            total = term if total is None else total + term
        return total.T

    send_ref[:kept, :] = product(slice(kept, 2 * kept)).astype(BF16)
    send_ref[kept:, :] = pair_sums([grad[group:, :].astype(F32) for grad in grads]).astype(BF16)
    keep_ref[...] = product(slice(0, kept))


def finish(scale, keep_ref, own_ref, other_ref, weight_ref, grad_ref, wgrad_ref):
    share = keep_ref.shape[0]
    grad_proj = (keep_ref[...] + other_ref[:share, :].astype(F32)).astype(BF16)
    grad_ref[...] = lax.dot_general(
        grad_proj, weight_ref[...], (((1,), (1,)), ((), ())), preferred_element_type=F32
    ).astype(BF16)
    wgrad_ref[...] = (own_ref[share:, :].astype(F32) + other_ref[share:, :].astype(F32)) * scale


def swap(x, axis, mask):
    n = lax.axis_size(axis)
    return lax.ppermute(x, axis, [(i, i ^ mask) for i in range(n)])


def swap_by_row(x, masks):
    row_count, col_count = lax.axis_size("row"), lax.axis_size("col")
    pairs = [
        (r * col_count + c, r * col_count + (c ^ masks[r & 1])) for r in range(row_count) for c in range(col_count)
    ]
    return lax.ppermute(x, ("row", "col"), pairs)


class DenseBlock:
    def __init__(self, place, rows, cols, tiles, tile_slots, tile_counts):
        (self.dense,) = kernel_call(
            functools.partial(densify, place),
            [((rows, cols), BF16, True)],
            0,
            "densify",
            [ANY] * 3,
            [
                pltpu.VMEM(tiles.shape[2:], BF16),
                pltpu.SMEM(tile_slots.shape, jnp.int32),
                pltpu.SMEM(tile_counts.shape, jnp.int32),
                pltpu.SemaphoreType.DMA((3,)),
            ],
        )(in_hbm(tiles), tile_slots, tile_counts)

    def after(self, x):
        x, self.dense = lax.optimization_barrier((x, self.dense))
        return x

    def forward(self, pieces, groups):
        rows, cols = self.dense.shape
        width = pieces[0].shape[-1]
        return kernel_call(
            functools.partial(forward, len(pieces)),
            [((rows // groups, width), BF16 if m else F32, True) for m in range(groups)],
            2 * rows * cols * width,
            "forward",
            [VM] * (1 + len(pieces)),
        )(in_vmem(self.dense), *pieces)

    def backward(self, grads):
        rows, cols = self.dense.shape
        width = grads[0].shape[-1]
        return kernel_call(
            backward,
            [((cols // 2 + width, width), BF16, True), ((cols // 2, width), F32, True)],
            2 * rows * cols * width,
            "backward",
            [VM] * (1 + len(grads)),
        )(in_vmem(self.dense), *grads)


class TiledBlock:
    def __init__(self, place, rows, cols, tiles, tile_slots, tile_counts):
        self.tiles, slots = tiles[0, 0], tile_slots[0, 0]
        self.size = self.tiles.shape[-1]
        self.row_count, self.col_count = rows // self.size, cols // self.size
        self.row_at, self.col_at = place(slots)
        self.live = jnp.arange(slots.shape[0], dtype=jnp.int32) < tile_counts[0, 0]

    def after(self, x):
        return x

    def forward(self, pieces, groups):
        given = jnp.concatenate(pieces).reshape(self.col_count, self.size, -1)[self.col_at]
        terms = jnp.einsum("tij,tjf->tif", self.tiles, given, preferred_element_type=F32)
        at = jnp.where(self.live, self.row_at, self.row_count)
        sums = jax.ops.segment_sum(terms, at, self.row_count + 1)[: self.row_count]
        parts = jnp.split(sums.reshape(-1, given.shape[-1]), groups)
        return [parts[0], *[part.astype(BF16) for part in parts[1:]]]

    def backward(self, grads):
        group = self.row_count * self.size // len(grads)
        given = jnp.concatenate([grad[:group] for grad in grads])
        given = given.reshape(self.row_count, self.size, -1)[self.row_at]
        terms = jnp.einsum("tji,tjf->tif", self.tiles, given, preferred_element_type=F32)
        at = jnp.where(self.live, self.col_at, self.col_count)
        sums = jax.ops.segment_sum(terms, at, self.col_count + 1)[: self.col_count]
        keep, send = jnp.split(sums.reshape(-1, given.shape[-1]), 2)
        wsum = pair_sums([grad[group:].astype(F32) for grad in grads])
        return lax.optimization_barrier(jnp.concatenate([send, wsum]).astype(BF16)), keep


def body(features, weight, tiles, tile_slots, tile_counts, cotangent):
    size = tiles.shape[-1]
    share, width = features.shape
    row_count, col_count = lax.axis_size("row"), lax.axis_size("col")
    row_bits, col_bits = row_count.bit_length() - 1, col_count.bit_length() - 1
    near = min(2, col_bits)
    rows, cols = share * col_count, share * row_count
    group = rows >> near
    place = functools.partial(
        place_of, row_bits=row_bits, near=near, share_tiles=share // size, group_tiles=group // size
    )
    block_type = DenseBlock if 2 * rows * cols <= DENSE_LIMIT else TiledBlock
    block = block_type(place, rows, cols, tiles, tile_slots, tile_counts)

    pieces = [features]
    for bit in reversed(range(row_bits)):
        pieces += [swap(piece, "row", 1 << bit) for piece in pieces]
        if bit == row_bits - 1:
            pieces[1] = block.after(pieces[1])
    total, *sends = block.forward(pieces, 1 << near)

    sends, cotangent = lax.optimization_barrier((sends, cotangent))
    cots = [cotangent]
    for bit in range(near, col_bits):
        cots += [swap(piece, "col", sum_mask(bit, near)) for piece in cots]

    for send, masks in zip(sends, slot_masks(near)):
        total = total + swap_by_row(send, masks).astype(F32)
    left, cots = lax.optimization_barrier((total.astype(BF16), cots))
    right = jnp.zeros_like(left)
    for bit in range(near, col_bits):
        if bit > near:
            left = lax.optimization_barrier((left.astype(F32) + right.astype(F32)).astype(BF16))
        right = swap(left, "col", sum_mask(bit, near))

    grads, hidden = kernel_call(
        functools.partial(middle, near, share),
        [((group + width, width), BF16, True), ((share, width), BF16, False)],
        8 * group * width * width,
        "middle",
        [VM] * (3 + len(cots)),
        [pltpu.VMEM((group, width), BF16)] * 2,
    )(left, right, weight, *cots)
    send, keep = block.backward([grads, *[swap_by_row(grads, masks) for masks in slot_masks(near)]])

    kept = cols // 2
    for bit in range(row_bits):
        other = swap(send, "row", 1 << bit)
        if bit == row_bits - 1:
            break
        keep = keep + other[:kept].astype(F32)
        wsum = send[kept:].astype(F32) + other[kept:].astype(F32)
        kept //= 2
        send = lax.optimization_barrier(jnp.concatenate([keep[kept:].astype(BF16), wsum.astype(BF16)]))
        keep = keep[:kept]

    feature_grad, weight_grad = kernel_call(
        functools.partial(finish, 1.0 / math.sqrt(share * row_count * col_count)),
        [((share, width), BF16, False), ((width, width), F32, False)],
        2 * share * width * width,
        "finish",
        [VM] * 4,
    )(keep, send, other, weight)
    return hidden, feature_grad, weight_grad


def solution(mesh):
    placed = (
        P(("col", "row"), None),
        P(),
        P("row", "col", None, None, None),
        P("row", "col", None),
        P("row", "col"),
        P(("row", "col"), None),
    )
    return jax.shard_map(
        body,
        mesh=mesh,
        in_specs=placed,
        out_specs=(P(("row", "col"), None), P(("col", "row"), None), P()),
        check_vma=False,
    )
```

time: 285 us -> 46.9 us (0.16)
  waiting for transfers between devices: 189 us -> 21.4 us
  blocking collectives: 40.3 us -> 0 us
  other arithmetic: 18.1 us -> 0.11 us
  starting transfers between devices: 0.12 us -> 17.9 us
  between operations: 14.5 us -> 1.4 us
  local copies, waits for them, and re-layouts: 11.3 us -> 0.68 us
  matrix products: 9.38 us -> 0 us
  Pallas kernels: 0 us -> 5.63 us
    psum x2 -> x0, waiting for transfers between devices: 169 us -> none  [the longest x1 120 us: body(): weight_grad = lax.psum(weight_term, ('row', 'col')) / math.sqrt(node_total)]
    all_gather x2 -> x0, blocking collectives: 40.3 us -> none  [the longest x1 33.1 us: body(): cot_block = lax.all_gather(cotangent, 'col', axis=0, tiled=True)]
    ppermute x0 -> x13, waiting for transfers between devices: none -> 21.4 us  [the longest x7 13 us: swap(): return lax.ppermute(x, axis, [(i, i ^ mask) for i in range(n)])]
    reduce_scatter x1 -> x0, waiting for transfers between devices: 19.7 us -> none  [body(): lax.psum_scatter(back_partial, 'row', scatter_dimension=0, tiled=True)]
    ppermute x0 -> x13, starting transfers between devices: none -> 17.9 us  [the longest x7 10.9 us: swap(): return lax.ppermute(x, axis, [(i, i ^ mask) for i in range(n)])]
    scatter-add x2 -> x0, other arithmetic: 13.3 us -> none  [the longest x1 6.63 us: body(): jax.ops.segment_sum(products, fwd_targets, tile_rows + 1)[:tile_rows]]
    dot_general x5 -> x0, matrix products: 9.38 us -> none  [the longest x1 2.73 us: body(): jnp.einsum('tij,tjf->tif', tile_vals, gathered, preferred_element_type=jn...]
    dot_general x2 -> x0, local copies, waits for them, and re-layouts: 6.86 us -> none  [the longest x1 3.43 us: body(): jnp.einsum('tij,tjf->tif', tile_vals, gathered, preferred_element_type=jn...]
  transfers between devices with their start and end apart: 3 -> 13, of which waited for: 3 -> 9; matrix products, arithmetic and copies ran while one was open for 1% -> 0% of each run, Pallas kernels for 0% -> 4%
where the time goes in v1:
time: 46.9 us; the launch traced here: 47.1 us
  waiting for transfers between devices  21.4 us (46%)
  starting transfers between devices  17.9 us (38%)
  Pallas kernels  5.63 us (12%)
  between operations  1.4 us (3%)
  local copies, waits for them, and re-layouts  0.68 us (1%)
    ppermute x7, waiting for transfers between devices, swap(): return lax.ppermute(x, axis, [(i, i ^ mask) for i in range(n)])  13 us
    ppermute x7, starting transfers between devices, swap(): return lax.ppermute(x, axis, [(i, i ^ mask) for i in range(n)])  10.9 us
    ppermute x6, waiting for transfers between devices, swap_by_row(): return lax.ppermute(x, ('row', 'col'), pairs)  8.41 us
    ppermute x6, starting transfers between devices, swap_by_row(): return lax.ppermute(x, ('row', 'col'), pairs)  7.04 us
    pallas_call x1, Pallas kernels, __init__(): kernel_call(functools.partial(densify, place), [((rows, cols), BF16, True...  1.8 us
    pallas_call x1, Pallas kernels, forward(): kernel_call(functools.partial(forward, len(pieces)), [((rows // groups, w...  1.25 us
    pallas_call x1, Pallas kernels, body(): kernel_call(functools.partial(middle, near, share), [((group + width, wid...  0.95 us
  transfers between devices with their start and end apart: 13, of which 9 were waited for; matrix products, arithmetic and copies ran while one was open for 0% of the time, Pallas kernels for 4%

profile of v1, /device:TPU:0, one launch (start us, length us, event | category | flops | bytes accessed | tf_op | source)
XLA Modules:
  0.0 47.1 jit_solution(8404781627029130455)
XLA Ops:
  0.6 0.0 copy-start.1
  0.6 3.0 %collective-permute-start = (bf16[256,128]{1,0:T(8,128)(2,1)}, bf16[256,128]{1,0:T(8,128)(2,1)S(1)}, u32[]{:S(2)}, u32[]{:S(2)}) collective-permute-start(bf16[256,128]{1,0:T(8,128)(2,1)} %refs_1_.1), channel_id=1, source_target_pairs={{0,16},{8,24},{16,0},{24,8},{1,17},{9,25},{17,1},{25,9},{2,18},{10... | collective-permute-start | bytes 196616 | tf_op jit(solution)/shard_map/ppermute | solution.py:182
  3.7 0.0 collective-permute-start.1
  4.3 0.0 copy-start.3
  4.3 0.6 %copy-done.3 = s32[1,1,44]{2,1,0:T(1,128)S(1)} copy-done((s32[1,1,44]{2,1,0:T(1,128)S(1)}, s32[1,1,44]{2,1,0:T(1,128)}, u32[]{:S(2)}) %copy-start.3) | copy-done | bytes 200
  5.0 0.0 copy-start.2
  5.0 0.0 copy-start
  5.0 1.8 %densify.1.refs_0_.dense_ref = bf16[2048,1024]{1,0:T(8,128)(2,1)S(1)} custom-call(bf16[1,1,44,128,128]{4,3,2,1,0:T(8,128)(2,1)} %tiles_ref.1, s32[1,1,44]{2,1,0:T(1,128)S(1)} %copy-done.3, s32[1,1]{1,0:T(1,128)S(6)} %copy.9.count_ref), custom_call_target="tpu_custom_call" | custom-call | bytes 4194304 | tf_op jit(solution)/shard_map/densify/pallas_call | solution.py:195
  6.8 0.0 collective-permute-done.refs_2_
  6.8 1.6 %collective-permute-start.2 = (bf16[256,128]{1,0:T(8,128)(2,1)S(1)}, bf16[256,128]{1,0:T(8,128)(2,1)S(1)}, u32[]{:S(2)}, u32[]{:S(2)}) collective-permute-start(bf16[256,128]{1,0:T(8,128)(2,1)S(1)} %collective-permute-done.refs_2_), channel_id=1, source_target_pairs={{0,8},{8,0},{16,24},{24,16},{1,9},{9,1},{17,25},{25,17},{2,10},{10... | collective-permute-start | bytes 196616 | tf_op jit(solution)/shard_map/ppermute | solution.py:182
  8.4 0.0 collective-permute-done.1.refs_3_
  8.4 0.9 %collective-permute-done.2.refs_4_ = bf16[256,128]{1,0:T(8,128)(2,1)S(1)} collective-permute-done((bf16[256,128]{1,0:T(8,128)(2,1)S(1)}, bf16[256,128]{1,0:T(8,128)(2,1)S(1)}, u32[]{:S(2)}, u32[]{:S(2)}) %collective-permute-start.2) | collective-permute-done | bytes 65568 | tf_op jit(solution)/shard_map/ppermute | solution.py:182
  9.3 0.0 copy-done.1
  9.3 1.2 %forward.1 = (f32[512,128]{1,0:T(8,128)S(1)}, bf16[512,128]{1,0:T(8,128)(2,1)S(1)}, bf16[512,128]{1,0:T(8,128)(2,1)S(1)}, bf16[512,128]{1,0:T(8,128)(2,1)S(1)}) custom-call(bf16[2048,1024]{1,0:T(8,128)(2,1)S(1)} %densify.1.refs_0_.dense_ref, bf16[256,128]{1,0:T(8,128)(2,1)S(1)} %copy-done.1, bf16[256,128]{1,0:T(8,128)(2,1)S(1)} %collective-permute-done.refs_2_, ...), custom_call_target="tpu_custom_call" | custom-call | flops 536870912 | bytes 655360 | tf_op jit(solution)/shard_map/forward/pallas_call | solution.py:216
  10.5 1.4 %collective-permute-start.3 = (bf16[512,128]{1,0:T(8,128)(2,1)S(1)}, bf16[512,128]{1,0:T(8,128)(2,1)S(1)}, u32[]{:S(2)}, u32[]{:S(2)}) collective-permute-start(bf16[512,128]{1,0:T(8,128)(2,1)S(1)} %get-tuple-element.28), channel_id=1, source_target_pairs={{0,2},{1,3},{2,0},{3,1},{4,6},{5,7},{6,4},{7,5},{8,10},{9,11},{10,... | collective-permute-start | bytes 393224 | tf_op jit(solution)/shard_map/ppermute | solution.py:190
  11.9 0.7 %collective-permute-start.4 = (bf16[512,128]{1,0:T(8,128)(2,1)S(1)}, bf16[512,128]{1,0:T(8,128)(2,1)S(1)}, u32[]{:S(2)}, u32[]{:S(2)}) collective-permute-start(bf16[512,128]{1,0:T(8,128)(2,1)S(1)} %get-tuple-element.29), channel_id=1, source_target_pairs={{0,1},{1,0},{2,3},{3,2},{4,5},{5,4},{6,7},{7,6},{8,9},{9,8},{10,11... | collective-permute-start | bytes 393224 | tf_op jit(solution)/shard_map/ppermute | solution.py:190
  12.6 1.5 %collective-permute-start.5 = (bf16[512,128]{1,0:T(8,128)(2,1)S(1)}, bf16[512,128]{1,0:T(8,128)(2,1)S(1)}, u32[]{:S(2)}, u32[]{:S(2)}) collective-permute-start(bf16[512,128]{1,0:T(8,128)(2,1)S(1)} %get-tuple-element.30), channel_id=1, source_target_pairs={{0,3},{1,2},{2,1},{3,0},{4,7},{5,6},{6,5},{7,4},{8,11},{9,10},{10,... | collective-permute-start | bytes 393224 | tf_op jit(solution)/shard_map/ppermute | solution.py:190
  14.1 0.0 copy-done.2
  14.1 3.1 %collective-permute-start.6 = (bf16[256,128]{1,0:T(8,128)(2,1)S(1)}, bf16[256,128]{1,0:T(8,128)(2,1)S(1)}, u32[]{:S(2)}, u32[]{:S(2)}) collective-permute-start(bf16[256,128]{1,0:T(8,128)(2,1)S(1)} %copy-done.2), channel_id=1, source_target_pairs={{0,6},{1,7},{2,4},{3,5},{4,2},{5,3},{6,0},{7,1},{8,14},{9,15},{10,... | collective-permute-start | bytes 196616 | tf_op jit(solution)/shard_map/ppermute | solution.py:182
  17.2 0.0 collective-permute-done.3
  17.2 3.0 %collective-permute-done.4 = bf16[512,128]{1,0:T(8,128)(2,1)S(1)} collective-permute-done((bf16[512,128]{1,0:T(8,128)(2,1)S(1)}, bf16[512,128]{1,0:T(8,128)(2,1)S(1)}, u32[]{:S(2)}, u32[]{:S(2)}) %collective-permute-start.4) | collective-permute-done | bytes 131104 | tf_op jit(solution)/shard_map/ppermute | solution.py:190
  20.2 0.0 collective-permute-done.5
  20.2 0.1 add_convert_fusion.left_ref
  20.3 2.0 %collective-permute-done.6.refs_1_ = bf16[256,128]{1,0:T(8,128)(2,1)S(1)} collective-permute-done((bf16[256,128]{1,0:T(8,128)(2,1)S(1)}, bf16[256,128]{1,0:T(8,128)(2,1)S(1)}, u32[]{:S(2)}, u32[]{:S(2)}) %collective-permute-start.6) | collective-permute-done | bytes 65568 | tf_op jit(solution)/shard_map/ppermute | solution.py:182
  22.3 3.0 %collective-permute-start.7 = (bf16[512,128]{1,0:T(8,128)(2,1)S(1)}, bf16[512,128]{1,0:T(8,128)(2,1)S(1)}, u32[]{:S(2)}, u32[]{:S(2)}) collective-permute-start(bf16[512,128]{1,0:T(8,128)(2,1)S(1)} %add_convert_fusion.left_ref), channel_id=1, source_target_pairs={{0,6},{1,7},{2,4},{3,5},{4,2},{5,3},{6,0},{7,1},{8,14},{9,15},{10,... | collective-permute-start | bytes 393224 | tf_op jit(solution)/shard_map/ppermute | solution.py:182
  25.3 3.9 %collective-permute-done.7.right_ref = bf16[512,128]{1,0:T(8,128)(2,1)S(1)} collective-permute-done((bf16[512,128]{1,0:T(8,128)(2,1)S(1)}, bf16[512,128]{1,0:T(8,128)(2,1)S(1)}, u32[]{:S(2)}, u32[]{:S(2)}) %collective-permute-start.7) | collective-permute-done | bytes 131104 | tf_op jit(solution)/shard_map/ppermute | solution.py:182
  29.2 0.0 copy-done
  29.2 0.9 %middle.1 = (bf16[640,128]{1,0:T(8,128)(2,1)S(1)}, bf16[256,128]{1,0:T(8,128)(2,1)}) custom-call(bf16[512,128]{1,0:T(8,128)(2,1)S(1)} %add_convert_fusion.left_ref, bf16[512,128]{1,0:T(8,128)(2,1)S(1)} %collective-permute-done.7.right_ref, bf16[128,128]{1,0:T(8,128)(2,1)S(1)} %copy-done, bf16[256,128]{1,0:T(8,128)(2,1)S(1)} %copy-done.2, ...), custom_call_target="tpu_custom_call" | custom-call | flops 67108864 | bytes 229376 | tf_op jit(solution)/shard_map/middle/pallas_call | solution.py:302
  30.1 0.5 %collective-permute-start.10 = (bf16[640,128]{1,0:T(8,128)(2,1)S(1)}, bf16[640,128]{1,0:T(8,128)(2,1)S(1)}, u32[]{:S(2)}, u32[]{:S(2)}) collective-permute-start(bf16[640,128]{1,0:T(8,128)(2,1)S(1)} %get-tuple-element.36.refs_0_), channel_id=1, source_target_pairs={{0,3},{1,2},{2,1},{3,0},{4,7},{5,6},{6,5},{7,4},{8,11},{9,10},{10,... | collective-permute-start | bytes 491528 | tf_op jit(solution)/shard_map/ppermute | solution.py:190
  30.6 1.8 %collective-permute-start.9 = (bf16[640,128]{1,0:T(8,128)(2,1)S(1)}, bf16[640,128]{1,0:T(8,128)(2,1)S(1)}, u32[]{:S(2)}, u32[]{:S(2)}) collective-permute-start(bf16[640,128]{1,0:T(8,128)(2,1)S(1)} %get-tuple-element.36.refs_0_), channel_id=1, source_target_pairs={{0,1},{1,0},{2,3},{3,2},{4,5},{5,4},{6,7},{7,6},{8,9},{9,8},{10,11... | collective-permute-start | bytes 491528 | tf_op jit(solution)/shard_map/ppermute | solution.py:190
  32.4 1.2 %collective-permute-start.8 = (bf16[640,128]{1,0:T(8,128)(2,1)S(1)}, bf16[640,128]{1,0:T(8,128)(2,1)S(1)}, u32[]{:S(2)}, u32[]{:S(2)}) collective-permute-start(bf16[640,128]{1,0:T(8,128)(2,1)S(1)} %get-tuple-element.36.refs_0_), channel_id=1, source_target_pairs={{0,2},{1,3},{2,0},{3,1},{4,6},{5,7},{6,4},{7,5},{8,10},{9,11},{10,... | collective-permute-start | bytes 491528 | tf_op jit(solution)/shard_map/ppermute | solution.py:190
  33.6 3.7 %collective-permute-done.10.refs_3_ = bf16[640,128]{1,0:T(8,128)(2,1)S(1)} collective-permute-done((bf16[640,128]{1,0:T(8,128)(2,1)S(1)}, bf16[640,128]{1,0:T(8,128)(2,1)S(1)}, u32[]{:S(2)}, u32[]{:S(2)}) %collective-permute-start.10) | collective-permute-done | bytes 163872 | tf_op jit(solution)/shard_map/ppermute | solution.py:190
  37.3 0.7 %collective-permute-done.9.refs_2_ = bf16[640,128]{1,0:T(8,128)(2,1)S(1)} collective-permute-done((bf16[640,128]{1,0:T(8,128)(2,1)S(1)}, bf16[640,128]{1,0:T(8,128)(2,1)S(1)}, u32[]{:S(2)}, u32[]{:S(2)}) %collective-permute-start.9) | collective-permute-done | bytes 163872 | tf_op jit(solution)/shard_map/ppermute | solution.py:190
  38.0 1.0 %collective-permute-done.8.refs_1_ = bf16[640,128]{1,0:T(8,128)(2,1)S(1)} collective-permute-done((bf16[640,128]{1,0:T(8,128)(2,1)S(1)}, bf16[640,128]{1,0:T(8,128)(2,1)S(1)}, u32[]{:S(2)}, u32[]{:S(2)}) %collective-permute-start.8) | collective-permute-done | bytes 163872 | tf_op jit(solution)/shard_map/ppermute | solution.py:190
  39.0 0.8 %backward.1 = (bf16[640,128]{1,0:T(8,128)(2,1)S(1)}, f32[512,128]{1,0:T(8,128)S(1)}) custom-call(bf16[2048,1024]{1,0:T(8,128)(2,1)S(1)} %densify.1.refs_0_.dense_ref, bf16[640,128]{1,0:T(8,128)(2,1)S(1)} %get-tuple-element.36.refs_0_, bf16[640,128]{1,0:T(8,128)(2,1)S(1)} %collective-permute-done.8.refs_1_, ...), custom_call_target="tpu_custom_call" | custom-call | flops 536870912 | bytes 425984 | tf_op jit(solution)/shard_map/backward/pallas_call | solution.py:227
  39.9 0.1 collective-permute-start.11
  39.9 1.4 %collective-permute-done.11 = bf16[640,128]{1,0:T(8,128)(2,1)S(1)} collective-permute-done((bf16[640,128]{1,0:T(8,128)(2,1)S(1)}, bf16[640,128]{1,0:T(8,128)(2,1)S(1)}, u32[]{:S(2)}, u32[]{:S(2)}) %collective-permute-start.11) | collective-permute-done | bytes 163872 | tf_op jit(solution)/shard_map/ppermute | solution.py:182
  41.4 0.1 collective-permute-start.12
  41.5 4.8 %collective-permute-done.12.other_ref = bf16[384,128]{1,0:T(8,128)(2,1)S(1)} collective-permute-done((bf16[384,128]{1,0:T(8,128)(2,1)S(1)}, bf16[384,128]{1,0:T(8,128)(2,1)S(1)}, u32[]{:S(2)}, u32[]{:S(2)}) %collective-permute-start.12) | collective-permute-done | bytes 98336 | tf_op jit(solution)/shard_map/ppermute | solution.py:182
  46.3 0.8 %finish.1 = (bf16[256,128]{1,0:T(8,128)(2,1)}, f32[128,128]{1,0:T(8,128)}) custom-call(f32[256,128]{1,0:T(8,128)S(1)} %slice.22.keep_ref, bf16[384,128]{1,0:T(8,128)(2,1)S(1)} %pad_maximum_fusion.own_ref, bf16[384,128]{1,0:T(8,128)(2,1)S(1)} %collective-permute-done.12.other_ref, bf16[128,128]{1,0:T(8,128)(2,1)S(1)} %copy-done), custom_call_target="tpu_custom_call" | custom-call | flops 8388608 | bytes 131072 | tf_op jit(solution)/shard_map/finish/pallas_call | solution.py:323
  (5 shorter events, 0.1 us)
Async XLA Ops:
  0.6 8.7 %copy-start.1 = (bf16[256,128]{1,0:T(8,128)(2,1)S(1)}, bf16[256,128]{1,0:T(8,128)(2,1)}, u32[]{:S(2)}) copy-start(bf16[256,128]{1,0:T(8,128)(2,1)} %refs_1_.1) | copy-start | bytes 196612
  0.6 6.2 %collective-permute-start = (bf16[256,128]{1,0:T(8,128)(2,1)}, bf16[256,128]{1,0:T(8,128)(2,1)S(1)}, u32[]{:S(2)}, u32[]{:S(2)}) collective-permute-start(bf16[256,128]{1,0:T(8,128)(2,1)} %refs_1_.1), channel_id=1, source_target_pairs={{0,16},{8,24},{16,0},{24,8},{1,17},{9,25},{17,1},{25,9},{2,18},{10... | collective-permute-start | bytes 196616 | tf_op jit(solution)/shard_map/ppermute | solution.py:182
  3.7 4.7 %collective-permute-start.1 = (bf16[256,128]{1,0:T(8,128)(2,1)}, bf16[256,128]{1,0:T(8,128)(2,1)S(1)}, u32[]{:S(2)}, u32[]{:S(2)}) collective-permute-start(bf16[256,128]{1,0:T(8,128)(2,1)} %refs_1_.1), channel_id=1, source_target_pairs={{0,8},{8,0},{16,24},{24,16},{1,9},{9,1},{17,25},{25,17},{2,10},{10... | collective-permute-start | bytes 196616 | tf_op jit(solution)/shard_map/ppermute | solution.py:182
  4.3 0.7 %copy-start.3 = (s32[1,1,44]{2,1,0:T(1,128)S(1)}, s32[1,1,44]{2,1,0:T(1,128)}, u32[]{:S(2)}) copy-start(s32[1,1,44]{2,1,0:T(1,128)} %slots_ref.1) | copy-start | bytes 532
  5.0 9.1 %copy-start.2 = (bf16[256,128]{1,0:T(8,128)(2,1)S(1)}, bf16[256,128]{1,0:T(8,128)(2,1)}, u32[]{:S(2)}) copy-start(bf16[256,128]{1,0:T(8,128)(2,1)} %refs_0_) | copy-start | bytes 196612
  5.0 24.2 %copy-start = (bf16[128,128]{1,0:T(8,128)(2,1)S(1)}, bf16[128,128]{1,0:T(8,128)(2,1)}, u32[]{:S(2)}) copy-start(bf16[128,128]{1,0:T(8,128)(2,1)} %weight_ref.3) | copy-start | bytes 98308
  6.8 2.5 %collective-permute-start.2 = (bf16[256,128]{1,0:T(8,128)(2,1)S(1)}, bf16[256,128]{1,0:T(8,128)(2,1)S(1)}, u32[]{:S(2)}, u32[]{:S(2)}) collective-permute-start(bf16[256,128]{1,0:T(8,128)(2,1)S(1)} %collective-permute-done.refs_2_), channel_id=1, source_target_pairs={{0,8},{8,0},{16,24},{24,16},{1,9},{9,1},{17,25},{25,17},{2,10},{10... | collective-permute-start | bytes 196616 | tf_op jit(solution)/shard_map/ppermute | solution.py:182
  10.5 6.7 %collective-permute-start.3 = (bf16[512,128]{1,0:T(8,128)(2,1)S(1)}, bf16[512,128]{1,0:T(8,128)(2,1)S(1)}, u32[]{:S(2)}, u32[]{:S(2)}) collective-permute-start(bf16[512,128]{1,0:T(8,128)(2,1)S(1)} %get-tuple-element.28), channel_id=1, source_target_pairs={{0,2},{1,3},{2,0},{3,1},{4,6},{5,7},{6,4},{7,5},{8,10},{9,11},{10,... | collective-permute-start | bytes 393224 | tf_op jit(solution)/shard_map/ppermute | solution.py:190
  11.9 8.3 %collective-permute-start.4 = (bf16[512,128]{1,0:T(8,128)(2,1)S(1)}, bf16[512,128]{1,0:T(8,128)(2,1)S(1)}, u32[]{:S(2)}, u32[]{:S(2)}) collective-permute-start(bf16[512,128]{1,0:T(8,128)(2,1)S(1)} %get-tuple-element.29), channel_id=1, source_target_pairs={{0,1},{1,0},{2,3},{3,2},{4,5},{5,4},{6,7},{7,6},{8,9},{9,8},{10,11... | collective-permute-start | bytes 393224 | tf_op jit(solution)/shard_map/ppermute | solution.py:190
  12.6 7.6 %collective-permute-start.5 = (bf16[512,128]{1,0:T(8,128)(2,1)S(1)}, bf16[512,128]{1,0:T(8,128)(2,1)S(1)}, u32[]{:S(2)}, u32[]{:S(2)}) collective-permute-start(bf16[512,128]{1,0:T(8,128)(2,1)S(1)} %get-tuple-element.30), channel_id=1, source_target_pairs={{0,3},{1,2},{2,1},{3,0},{4,7},{5,6},{6,5},{7,4},{8,11},{9,10},{10,... | collective-permute-start | bytes 393224 | tf_op jit(solution)/shard_map/ppermute | solution.py:190
  14.1 8.2 %collective-permute-start.6 = (bf16[256,128]{1,0:T(8,128)(2,1)S(1)}, bf16[256,128]{1,0:T(8,128)(2,1)S(1)}, u32[]{:S(2)}, u32[]{:S(2)}) collective-permute-start(bf16[256,128]{1,0:T(8,128)(2,1)S(1)} %copy-done.2), channel_id=1, source_target_pairs={{0,6},{1,7},{2,4},{3,5},{4,2},{5,3},{6,0},{7,1},{8,14},{9,15},{10,... | collective-permute-start | bytes 196616 | tf_op jit(solution)/shard_map/ppermute | solution.py:182
  22.3 6.8 %collective-permute-start.7 = (bf16[512,128]{1,0:T(8,128)(2,1)S(1)}, bf16[512,128]{1,0:T(8,128)(2,1)S(1)}, u32[]{:S(2)}, u32[]{:S(2)}) collective-permute-start(bf16[512,128]{1,0:T(8,128)(2,1)S(1)} %add_convert_fusion.left_ref), channel_id=1, source_target_pairs={{0,6},{1,7},{2,4},{3,5},{4,2},{5,3},{6,0},{7,1},{8,14},{9,15},{10,... | collective-permute-start | bytes 393224 | tf_op jit(solution)/shard_map/ppermute | solution.py:182
  30.1 7.2 %collective-permute-start.10 = (bf16[640,128]{1,0:T(8,128)(2,1)S(1)}, bf16[640,128]{1,0:T(8,128)(2,1)S(1)}, u32[]{:S(2)}, u32[]{:S(2)}) collective-permute-start(bf16[640,128]{1,0:T(8,128)(2,1)S(1)} %get-tuple-element.36.refs_0_), channel_id=1, source_target_pairs={{0,3},{1,2},{2,1},{3,0},{4,7},{5,6},{6,5},{7,4},{8,11},{9,10},{10,... | collective-permute-start | bytes 491528 | tf_op jit(solution)/shard_map/ppermute | solution.py:190
  30.6 7.4 %collective-permute-start.9 = (bf16[640,128]{1,0:T(8,128)(2,1)S(1)}, bf16[640,128]{1,0:T(8,128)(2,1)S(1)}, u32[]{:S(2)}, u32[]{:S(2)}) collective-permute-start(bf16[640,128]{1,0:T(8,128)(2,1)S(1)} %get-tuple-element.36.refs_0_), channel_id=1, source_target_pairs={{0,1},{1,0},{2,3},{3,2},{4,5},{5,4},{6,7},{7,6},{8,9},{9,8},{10,11... | collective-permute-start | bytes 491528 | tf_op jit(solution)/shard_map/ppermute | solution.py:190
  32.4 6.6 %collective-permute-start.8 = (bf16[640,128]{1,0:T(8,128)(2,1)S(1)}, bf16[640,128]{1,0:T(8,128)(2,1)S(1)}, u32[]{:S(2)}, u32[]{:S(2)}) collective-permute-start(bf16[640,128]{1,0:T(8,128)(2,1)S(1)} %get-tuple-element.36.refs_0_), channel_id=1, source_target_pairs={{0,2},{1,3},{2,0},{3,1},{4,6},{5,7},{6,4},{7,5},{8,10},{9,11},{10,... | collective-permute-start | bytes 491528 | tf_op jit(solution)/shard_map/ppermute | solution.py:190
  39.9 1.5 %collective-permute-start.11 = (bf16[640,128]{1,0:T(8,128)(2,1)S(1)}, bf16[640,128]{1,0:T(8,128)(2,1)S(1)}, u32[]{:S(2)}, u32[]{:S(2)}) collective-permute-start(bf16[640,128]{1,0:T(8,128)(2,1)S(1)} %get-tuple-element.38), channel_id=1, source_target_pairs={{0,8},{8,0},{16,24},{24,16},{1,9},{9,1},{17,25},{25,17},{2,10},{10... | collective-permute-start | bytes 491528 | tf_op jit(solution)/shard_map/ppermute | solution.py:182
  41.4 4.9 %collective-permute-start.12 = (bf16[384,128]{1,0:T(8,128)(2,1)S(1)}, bf16[384,128]{1,0:T(8,128)(2,1)S(1)}, u32[]{:S(2)}, u32[]{:S(2)}) collective-permute-start(bf16[384,128]{1,0:T(8,128)(2,1)S(1)} %pad_maximum_fusion.own_ref), channel_id=1, source_target_pairs={{0,16},{8,24},{16,0},{24,8},{1,17},{9,25},{17,1},{25,9},{2,18},{10... | collective-permute-start | bytes 294920 | tf_op jit(solution)/shard_map/ppermute | solution.py:182

commit v2 on v1

--- a/solution.py
+++ b/solution.py
@@ -37,6 +37,7 @@
     )
 
 
+SPLIT = True
 VM = pl.BlockSpec(memory_space=pltpu.VMEM)
 ANY = pl.BlockSpec(memory_space=pl.ANY)
 
@@ -48,61 +49,68 @@
     return out
 
 
-def slot_masks(near):
-    return {0: [], 1: [(1, 1)], 2: [(2, 2), (1, 1), (3, 3)]}[near]
+PARTNERS = {0: [], 1: [1], 2: [2, 1, 3]}
 
 
 def sum_mask(bit, near):
     return 3 << (bit - 1) if bit == near and near else 1 << bit
 
 
-def place_of(slot, row_bits, near, share_tiles, group_tiles):
-    my_row = lax.axis_index("row")
-    my_col = lax.axis_index("col")
-    tile_cols = share_tiles << row_bits
-    tile_row = lax.div(slot, tile_cols)
-    tile_col = lax.rem(slot, tile_cols)
-    row_share = lax.div(tile_row, share_tiles)
+def quotient(value, by):
+    if by & (by - 1):
+        return lax.div(value, by), lax.rem(value, by)
+    return value >> (by.bit_length() - 1), value & (by - 1)
+
+
+def place_of(slot, my_row, my_col, row_bits, near, share_tiles, group_tiles):
+    tile_row, tile_col = quotient(slot, share_tiles << row_bits)
+    row_share, row_rest = quotient(tile_row, share_tiles)
+    col_share, col_rest = quotient(tile_col, share_tiles)
     apart = row_share ^ my_col
     if near:
         apart = apart ^ (((apart >> near) & 1) << (near - 1))
     mask = apart & ((1 << near) - 1)
     group = mask * 0
-    for at, (even, odd) in enumerate(slot_masks(near)):
-        group = jnp.where(mask == jnp.where((my_row & 1) == 1, odd, even), at + 1, group)
-    row_at = group * group_tiles + (row_share >> near) * share_tiles + lax.rem(tile_row, share_tiles)
-    col_share = bit_reverse(lax.div(tile_col, share_tiles) ^ my_row, row_bits)
-    return row_at, col_share * share_tiles + lax.rem(tile_col, share_tiles)
-
-
-def densify(place, tiles_ref, slots_ref, count_ref, dense_ref, held, slots, count, sems):
-    copies = [
-        pltpu.make_async_copy(count_ref, count, sems.at[0]),
-        pltpu.make_async_copy(slots_ref, slots, sems.at[1]),
-        pltpu.make_async_copy(tiles_ref.at[0, 0], held, sems.at[2]),
-    ]
+    for at, partner in enumerate(PARTNERS[near]):
+        group = jnp.where(mask == partner, at + 1, group)
+    row_at = group * group_tiles + (row_share >> near) * share_tiles + row_rest
+    return row_at, bit_reverse(col_share ^ my_row, row_bits) * share_tiles + col_rest
+
+
+def densify(place, parts, tiles_ref, slots_ref, count_ref, dense_ref, held, slots, sems):
+    total, size, _ = held.shape
+    step = -(-total // parts)
+    copies = [pltpu.make_async_copy(slots_ref, slots, sems.at[parts])]
+    for part, start in enumerate(range(0, total, step)):
+        some = pl.ds(start, min(step, total - start))
+        copies.append(pltpu.make_async_copy(tiles_ref.at[0, 0, some], held.at[some], sems.at[part]))
     for copy in copies:
         copy.start()
     dense_ref[...] = jnp.zeros_like(dense_ref)
-    size = held.shape[-1]
+    my_row, my_col = lax.axis_index("row"), lax.axis_index("col")
+    dead = dense_ref.shape[0] // size - 1
+    count = count_ref[0, 0]
     for copy in copies:
         copy.wait()
-
-    def step(k, carry):
-        row_at, col_at = place(slots[0, 0, k])
-        rows = pl.ds(pl.multiple_of(row_at * size, size), size)
-        cols = pl.ds(pl.multiple_of(col_at * size, size), size)
-        dense_ref[rows, cols] = held[k]
+    unroll = 4
+
+    def some_tiles(first, carry):
+        for inner in range(unroll):
+            k = jnp.minimum(first * unroll + inner, total - 1)
+            row_at, col_at = place(slots[0, 0, k], my_row, my_col)
+            row_at = jnp.where(first * unroll + inner < count, row_at, dead)
+            rows = pl.ds(pl.multiple_of(row_at * size, size), size)
+            cols = pl.ds(pl.multiple_of(col_at * size, size), size)
+            dense_ref[rows, cols] = held[k]
         return carry
 
-    lax.fori_loop(0, count[0, 0], step, 0)
-
-
-def forward(parts, *refs):
+    lax.fori_loop(0, (count + unroll - 1) // unroll, some_tiles, 0)
+
+
+def forward(parts, groups, *refs):
     dense_ref, pieces, outs = refs[0], refs[1 : 1 + parts], refs[1 + parts :]
-    group = outs[0].shape[0]
-    for m in [*range(1, len(outs)), 0]:
-        total, at = None, 0
+    for m, ref in zip(groups, outs):
+        group, total, at = ref.shape[0], None, 0
         for piece in pieces:
             depth = piece.shape[0]
             term = jnp.dot(
@@ -110,36 +118,37 @@
             )
             total = term if total is None else total + term
             at += depth
-        outs[m][...] = total.astype(outs[m].dtype)
+        ref[...] = total.astype(ref.dtype)
 
 
 def middle(near, share, left_ref, right_ref, weight_ref, *refs):
-    cot_refs, (send_ref, hidden_ref, high_ref, low_ref) = refs[:-4], refs[-4:]
-    group = high_ref.shape[0]
+    cot_refs, (send_ref, hidden_ref, agg_ref) = refs[:-3], refs[-3:]
+    group, width = agg_ref.shape[0], left_ref.shape[1]
     place = lax.axis_index("col") >> near
-    weight = weight_ref[...]
+    weight = jnp.concatenate([weight_ref[...]] * 2)
     at = 0
     for cot_ref in cot_refs:
         for start in range(0, cot_ref.shape[0], share):
             rows = pl.ds(pl.multiple_of((place ^ at) * share, share), share)
             agg = left_ref[rows, :].astype(F32) + right_ref[rows, :].astype(F32)
             high = agg.astype(BF16)
-            low = (agg - high.astype(F32)).astype(BF16)
-            high_ref[rows, :] = high
-            low_ref[rows, :] = low
-            summed = jnp.dot(high, weight, preferred_element_type=F32)
-            summed += jnp.dot(low, weight, preferred_element_type=F32)
+            both = jnp.concatenate([high, (agg - high.astype(F32)).astype(BF16)], axis=1)
+            agg_ref[rows, :] = both
+            summed = jnp.dot(both, weight, preferred_element_type=F32)
             gate = 1.0 / (1.0 + jnp.exp(-summed))
             if at == 0:
                 hidden_ref[...] = (summed * gate).astype(BF16)
             slope = gate * (1.0 + summed * (1.0 - gate))
             send_ref[rows, :] = (cot_ref[start : start + share, :].astype(F32) * slope).astype(BF16)
             at += 1
-    dims = (((0,), (0,)), ((), ()))
-    grad = send_ref[:group, :]
-    term = lax.dot_general(high_ref[...], grad, dims, preferred_element_type=F32)
-    term += lax.dot_general(low_ref[...], grad, dims, preferred_element_type=F32)
-    send_ref[group:, :] = term.astype(BF16)
+    term = lax.dot_general(
+        send_ref[:group, :], agg_ref[...], (((0,), (0,)), ((), ())), preferred_element_type=F32
+    )
+    send_ref[group:, :] = (term[:, :width] + term[:, width:]).T.astype(BF16)
+
+
+def emit(given_ref, out_ref):
+    out_ref[...] = given_ref[...]
 
 
 def pair_sums(terms):
@@ -148,24 +157,36 @@
     return terms[0]
 
 
-def backward(dense_ref, *refs):
-    grads, (send_ref, keep_ref) = refs[:-2], refs[-2:]
-    kept = keep_ref.shape[0]
-    group = dense_ref.shape[0] // len(grads)
-    dims = (((0,), (0,)), ((), ()))
-
-    def product(cols):
-        total = None
-        for m, grad in enumerate(grads):
-            term = lax.dot_general(
-                grad[:group, :], dense_ref[m * group : (m + 1) * group, cols], dims, preferred_element_type=F32
-            )
-            total = term if total is None else total + term
-        return total.T
-
-    send_ref[:kept, :] = product(slice(kept, 2 * kept)).astype(BF16)
-    send_ref[kept:, :] = pair_sums([grad[group:, :].astype(F32) for grad in grads]).astype(BF16)
-    keep_ref[...] = product(slice(0, kept))
+def columns_of(dense_ref, grads, first, columns):
+    total = None
+    for m, grad in enumerate(grads, first):
+        group = grad.shape[0] - grad.shape[1]
+        term = lax.dot_general(
+            grad[:group, :],
+            dense_ref[m * group : (m + 1) * group, columns],
+            (((0,), (0,)), ((), ())),
+            preferred_element_type=F32,
+        )
+        total = term if total is None else total + term
+    return total
+
+
+def backward_own(dense_ref, grad_ref, total_ref):
+    total_ref[...] = columns_of(dense_ref, [grad_ref], 0, slice(0, total_ref.shape[1]))
+
+
+def backward_sent(dense_ref, total_ref, *refs):
+    grads, send_ref = refs[:-1], refs[-1]
+    kept = total_ref.shape[1] // 2
+    columns = slice(kept, 2 * kept)
+    send_ref[:kept, :] = (columns_of(dense_ref, grads[1:], 1, columns) + total_ref[:, columns]).T.astype(BF16)
+    send_ref[kept:, :] = pair_sums([grad[-grad.shape[1] :, :].astype(F32) for grad in grads]).astype(BF16)
+
+
+def backward_kept(dense_ref, total_ref, *refs):
+    grads, keep_ref = refs[:-1], refs[-1]
+    columns = slice(0, keep_ref.shape[0])
+    keep_ref[...] = (columns_of(dense_ref, grads, 1, columns) + total_ref[:, columns]).T
 
 
 def finish(scale, keep_ref, own_ref, other_ref, weight_ref, grad_ref, wgrad_ref):
@@ -182,55 +203,57 @@
     return lax.ppermute(x, axis, [(i, i ^ mask) for i in range(n)])
 
 
-def swap_by_row(x, masks):
-    row_count, col_count = lax.axis_size("row"), lax.axis_size("col")
-    pairs = [
-        (r * col_count + c, r * col_count + (c ^ masks[r & 1])) for r in range(row_count) for c in range(col_count)
-    ]
-    return lax.ppermute(x, ("row", "col"), pairs)
-
-
 class DenseBlock:
     def __init__(self, place, rows, cols, tiles, tile_slots, tile_counts):
         (self.dense,) = kernel_call(
-            functools.partial(densify, place),
-            [((rows, cols), BF16, True)],
+            functools.partial(densify, place, 4),
+            [((rows + tiles.shape[-1], cols), BF16, True)],
             0,
             "densify",
-            [ANY] * 3,
+            [ANY, ANY, pl.BlockSpec(memory_space=pltpu.SMEM)],
             [
                 pltpu.VMEM(tiles.shape[2:], BF16),
                 pltpu.SMEM(tile_slots.shape, jnp.int32),
-                pltpu.SMEM(tile_counts.shape, jnp.int32),
-                pltpu.SemaphoreType.DMA((3,)),
+                pltpu.SemaphoreType.DMA((5,)),
             ],
-        )(in_hbm(tiles), tile_slots, tile_counts)
+        )(in_hbm(tiles), in_hbm(tile_slots), tile_counts)
+        self.rows, self.cols = rows, cols
 
     def after(self, x):
         x, self.dense = lax.optimization_barrier((x, self.dense))
         return x
 
     def forward(self, pieces, groups):
-        rows, cols = self.dense.shape
-        width = pieces[0].shape[-1]
-        return kernel_call(
-            functools.partial(forward, len(pieces)),
-            [((rows // groups, width), BF16 if m else F32, True) for m in range(groups)],
-            2 * rows * cols * width,
-            "forward",
-            [VM] * (1 + len(pieces)),
-        )(in_vmem(self.dense), *pieces)
+        width, group = pieces[0].shape[-1], self.rows // groups
+
+        def some(name, which, dtype):
+            return kernel_call(
+                functools.partial(forward, len(pieces), which),
+                [((group, width), dtype, True) for _ in which],
+                2 * len(which) * group * self.cols * width,
+                name,
+                [VM] * (1 + len(pieces)),
+            )(in_vmem(self.dense), *pieces)
+
+        sends = some("forward_sent", range(1, groups), BF16) if groups > 1 else []
+        if SPLIT:
+            (self.dense, sends) = lax.optimization_barrier((self.dense, sends))
+        return [*some("forward_own", [0], F32), *sends]
 
     def backward(self, grads):
-        rows, cols = self.dense.shape
+        rows, cols = self.rows, self.cols
         width = grads[0].shape[-1]
-        return kernel_call(
-            backward,
-            [((cols // 2 + width, width), BF16, True), ((cols // 2, width), F32, True)],
-            2 * rows * cols * width,
-            "backward",
-            [VM] * (1 + len(grads)),
-        )(in_vmem(self.dense), *grads)
+        dense = in_vmem(self.dense)
+
+        def some(kernel, shape, dtype, flops, name, *given):
+            (out,) = kernel_call(kernel, [(shape, dtype, True)], flops, name, [VM] * (1 + len(given)))(dense, *given)
+            return out
+
+        flops = 2 * rows * cols * width // len(grads)
+        total = some(backward_own, (width, cols), F32, flops, "backward_own", grads[0])
+        flops = 2 * rows * cols * width // 2
+        send = some(backward_sent, (cols // 2 + width, width), BF16, flops, "backward_sent", total, *grads)
+        return send, some(backward_kept, (cols // 2, width), F32, flops, "backward_kept", total, *grads[1:])
 
 
 class TiledBlock:
@@ -238,7 +261,7 @@
         self.tiles, slots = tiles[0, 0], tile_slots[0, 0]
         self.size = self.tiles.shape[-1]
         self.row_count, self.col_count = rows // self.size, cols // self.size
-        self.row_at, self.col_at = place(slots)
+        self.row_at, self.col_at = place(slots, lax.axis_index("row"), lax.axis_index("col"))
         self.live = jnp.arange(slots.shape[0], dtype=jnp.int32) < tile_counts[0, 0]
 
     def after(self, x):
@@ -290,8 +313,8 @@
     for bit in range(near, col_bits):
         cots += [swap(piece, "col", sum_mask(bit, near)) for piece in cots]
 
-    for send, masks in zip(sends, slot_masks(near)):
-        total = total + swap_by_row(send, masks).astype(F32)
+    for send, mask in zip(sends, PARTNERS[near]):
+        total = total + swap(send, "col", mask).astype(F32)
     left, cots = lax.optimization_barrier((total.astype(BF16), cots))
     right = jnp.zeros_like(left)
     for bit in range(near, col_bits):
@@ -301,13 +324,14 @@
 
     grads, hidden = kernel_call(
         functools.partial(middle, near, share),
-        [((group + width, width), BF16, True), ((share, width), BF16, False)],
+        [((group + width, width), BF16, True), ((share, width), BF16, True)],
         8 * group * width * width,
         "middle",
         [VM] * (3 + len(cots)),
-        [pltpu.VMEM((group, width), BF16)] * 2,
+        [pltpu.VMEM((group, 2 * width), BF16)],
     )(left, right, weight, *cots)
-    send, keep = block.backward([grads, *[swap_by_row(grads, masks) for masks in slot_masks(near)]])
+    (hidden,) = kernel_call(emit, [((share, width), BF16, False)], 0, "emit", [VM])(hidden)
+    send, keep = block.backward([grads, *[swap(grads, "col", mask) for mask in PARTNERS[near]]])
 
     kept = cols // 2
     for bit in range(row_bits):

time: 46.9 us -> 44.4 us (0.947)
  waiting for transfers between devices: 21.4 us -> 17.5 us
  starting transfers between devices: 17.9 us -> 18.8 us
  Pallas kernels: 5.63 us -> 6.39 us
  local copies, waits for them, and re-layouts: 0.68 us -> 0.03 us
    ppermute x6 -> x0, waiting for transfers between devices: 8.41 us -> none  [swap_by_row(): return lax.ppermute(x, ('row', 'col'), pairs)]
    ppermute x7 -> x13, starting transfers between devices: 10.9 us -> 18.8 us  [swap(): return lax.ppermute(x, axis, [(i, i ^ mask) for i in range(n)])]
    ppermute x6 -> x0, starting transfers between devices: 7.04 us -> none  [swap_by_row(): return lax.ppermute(x, ('row', 'col'), pairs)]
    ppermute x7 -> x13, waiting for transfers between devices: 13 us -> 17.5 us  [swap(): return lax.ppermute(x, axis, [(i, i ^ mask) for i in range(n)])]
    pallas_call x3 -> x7, Pallas kernels: 3.88 us -> 5.01 us  [the longest x1 1.66 us: __init__(): kernel_call(functools.partial(densify, place, 4), [((rows + tiles.shape[-...]
    unnamed x8 -> x6, local copies, waits for them, and re-layouts: 0.66 us -> 0.01 us
  transfers between devices with their start and end apart: 13 -> 13, of which waited for: 9 -> 10; matrix products, arithmetic and copies ran while one was open for 0% -> 0% of each run, Pallas kernels for 4% -> 8%
where the time goes in v2:
time: 44.4 us; the launch traced here: 44.3 us
  starting transfers between devices  18.8 us (42%)
  waiting for transfers between devices  17.5 us (39%)
  Pallas kernels  6.39 us (14%)
  between operations  1.42 us (3%)
    ppermute x13, starting transfers between devices, swap(): return lax.ppermute(x, axis, [(i, i ^ mask) for i in range(n)])  18.8 us
    ppermute x13, waiting for transfers between devices, swap(): return lax.ppermute(x, axis, [(i, i ^ mask) for i in range(n)])  17.5 us
    pallas_call x1, Pallas kernels, __init__(): kernel_call(functools.partial(densify, place, 4), [((rows + tiles.shape[-...  1.66 us
    pallas_call x2, Pallas kernels, some(): kernel_call(functools.partial(forward, len(pieces), which), [((group, wid...  1.41 us
    pallas_call x3, Pallas kernels, some(): kernel_call(kernel, [(shape, dtype, True)], flops, name, [VM] * (1 + len(...  1.3 us
  transfers between devices with their start and end apart: 13, of which 10 were waited for; matrix products, arithmetic and copies ran while one was open for 0% of the time, Pallas kernels for 8%

profile of v2, /device:TPU:0, one launch (start us, length us, event | category | flops | bytes accessed | tf_op | source)
XLA Modules:
  0.0 44.3 jit_solution(11367777420835755831)
XLA Ops:
  0.6 0.0 copy-start
  0.6 3.0 %collective-permute-start = (bf16[256,128]{1,0:T(8,128)(2,1)}, bf16[256,128]{1,0:T(8,128)(2,1)S(1)}, u32[]{:S(2)}, u32[]{:S(2)}) collective-permute-start(bf16[256,128]{1,0:T(8,128)(2,1)} %refs_1_.3), channel_id=1, source_target_pairs={{0,16},{8,24},{16,0},{24,8},{1,17},{9,25},{17,1},{25,9},{2,18},{10... | collective-permute-start | bytes 196616 | tf_op jit(solution)/shard_map/ppermute | solution.py:203
  3.7 0.0 collective-permute-start.1
  4.3 0.0 copy-start.2
  4.3 1.7 %densify.1.refs_0_.dense_ref = bf16[2176,1024]{1,0:T(8,128)(2,1)S(1)} custom-call(bf16[1,1,44,128,128]{4,3,2,1,0:T(8,128)(2,1)} %tiles_ref.1, s32[1,1,44]{2,1,0:T(1,128)} %slots_ref.1, s32[1,1]{1,0:T(1,128)S(6)} %copy.9.count_ref), custom_call_target="tpu_custom_call" | custom-call | bytes 4456448 | tf_op jit(solution)/shard_map/densify/pallas_call | solution.py:208
  6.0 0.0 copy-start.1
  6.0 0.1 collective-permute-done.refs_2_
  6.1 0.3 collective-permute-start.2
  6.4 0.0 collective-permute-done.1.refs_3_
  6.4 0.9 %collective-permute-done.2.refs_4_ = bf16[256,128]{1,0:T(8,128)(2,1)S(1)} collective-permute-done((bf16[256,128]{1,0:T(8,128)(2,1)S(1)}, bf16[256,128]{1,0:T(8,128)(2,1)S(1)}, u32[]{:S(2)}, u32[]{:S(2)}) %collective-permute-start.2) | collective-permute-done | bytes 65568 | tf_op jit(solution)/shard_map/ppermute | solution.py:203
  7.4 0.0 copy-done
  7.4 1.0 %forward_sent.1 = (bf16[512,128]{1,0:T(8,128)(2,1)S(1)}, bf16[512,128]{1,0:T(8,128)(2,1)S(1)}, bf16[512,128]{1,0:T(8,128)(2,1)S(1)}) custom-call(bf16[2176,1024]{1,0:T(8,128)(2,1)S(1)} %densify.1.refs_0_.dense_ref, bf16[256,128]{1,0:T(8,128)(2,1)S(1)} %copy-done, bf16[256,128]{1,0:T(8,128)(2,1)S(1)} %collective-permute-done.refs_2_, ...), custom_call_target="tpu_custom_call" | custom-call | flops 402653184 | bytes 393216 | tf_op jit(solution)/shard_map/forward_sent/pallas_call | solution.py:230
  8.4 2.1 %collective-permute-start.3 = (bf16[512,128]{1,0:T(8,128)(2,1)S(1)}, bf16[512,128]{1,0:T(8,128)(2,1)S(1)}, u32[]{:S(2)}, u32[]{:S(2)}) collective-permute-start(bf16[512,128]{1,0:T(8,128)(2,1)S(1)} %get-tuple-element.32), channel_id=1, source_target_pairs={{0,2},{1,3},{2,0},{3,1},{4,6},{5,7},{6,4},{7,5},{8,10},{9,11},{10,... | collective-permute-start | bytes 393224 | tf_op jit(solution)/shard_map/ppermute | solution.py:203
  10.5 1.5 %collective-permute-start.4 = (bf16[512,128]{1,0:T(8,128)(2,1)S(1)}, bf16[512,128]{1,0:T(8,128)(2,1)S(1)}, u32[]{:S(2)}, u32[]{:S(2)}) collective-permute-start(bf16[512,128]{1,0:T(8,128)(2,1)S(1)} %get-tuple-element.33), channel_id=1, source_target_pairs={{0,1},{1,0},{2,3},{3,2},{4,5},{5,4},{6,7},{7,6},{8,9},{9,8},{10,11... | collective-permute-start | bytes 393224 | tf_op jit(solution)/shard_map/ppermute | solution.py:203
  12.0 0.0 collective-permute-start.5
  12.1 0.0 copy-done.2
  12.1 4.0 %collective-permute-start.6 = (bf16[256,128]{1,0:T(8,128)(2,1)S(1)}, bf16[256,128]{1,0:T(8,128)(2,1)S(1)}, u32[]{:S(2)}, u32[]{:S(2)}) collective-permute-start(bf16[256,128]{1,0:T(8,128)(2,1)S(1)} %copy-done.2), channel_id=1, source_target_pairs={{0,6},{1,7},{2,4},{3,5},{4,2},{5,3},{6,0},{7,1},{8,14},{9,15},{10,... | collective-permute-start | bytes 196616 | tf_op jit(solution)/shard_map/ppermute | solution.py:203
  16.0 0.4 forward_own.1
  16.5 0.0 collective-permute-done.3
  16.5 2.1 %collective-permute-done.4 = bf16[512,128]{1,0:T(8,128)(2,1)S(1)} collective-permute-done((bf16[512,128]{1,0:T(8,128)(2,1)S(1)}, bf16[512,128]{1,0:T(8,128)(2,1)S(1)}, u32[]{:S(2)}, u32[]{:S(2)}) %collective-permute-start.4) | collective-permute-done | bytes 131104 | tf_op jit(solution)/shard_map/ppermute | solution.py:203
  18.6 0.0 collective-permute-done.5
  18.6 0.1 add_convert_fusion.left_ref
  18.7 2.1 %collective-permute-done.6.refs_1_ = bf16[256,128]{1,0:T(8,128)(2,1)S(1)} collective-permute-done((bf16[256,128]{1,0:T(8,128)(2,1)S(1)}, bf16[256,128]{1,0:T(8,128)(2,1)S(1)}, u32[]{:S(2)}, u32[]{:S(2)}) %collective-permute-start.6) | collective-permute-done | bytes 65568 | tf_op jit(solution)/shard_map/ppermute | solution.py:203
  20.8 2.6 %collective-permute-start.7 = (bf16[512,128]{1,0:T(8,128)(2,1)S(1)}, bf16[512,128]{1,0:T(8,128)(2,1)S(1)}, u32[]{:S(2)}, u32[]{:S(2)}) collective-permute-start(bf16[512,128]{1,0:T(8,128)(2,1)S(1)} %add_convert_fusion.left_ref), channel_id=1, source_target_pairs={{0,6},{1,7},{2,4},{3,5},{4,2},{5,3},{6,0},{7,1},{8,14},{9,15},{10,... | collective-permute-start | bytes 393224 | tf_op jit(solution)/shard_map/ppermute | solution.py:203
  23.4 4.3 %collective-permute-done.7.right_ref = bf16[512,128]{1,0:T(8,128)(2,1)S(1)} collective-permute-done((bf16[512,128]{1,0:T(8,128)(2,1)S(1)}, bf16[512,128]{1,0:T(8,128)(2,1)S(1)}, u32[]{:S(2)}, u32[]{:S(2)}) %collective-permute-start.7) | collective-permute-done | bytes 131104 | tf_op jit(solution)/shard_map/ppermute | solution.py:203
  27.7 0.0 copy-done.1
  27.7 0.6 %middle.1 = (bf16[640,128]{1,0:T(8,128)(2,1)S(1)}, bf16[256,128]{1,0:T(8,128)(2,1)S(1)}) custom-call(bf16[512,128]{1,0:T(8,128)(2,1)S(1)} %add_convert_fusion.left_ref, bf16[512,128]{1,0:T(8,128)(2,1)S(1)} %collective-permute-done.7.right_ref, bf16[128,128]{1,0:T(8,128)(2,1)S(1)} %copy-done.1, bf16[256,128]{1,0:T(8,128)(2,1)S(1)} %copy-done.2, ...), custom_call_target="tpu_custom_call" | custom-call | flops 67108864 | bytes 229376 | tf_op jit(solution)/shard_map/middle/pallas_call | solution.py:325
  28.2 0.3 collective-permute-start.10
  28.5 2.0 %collective-permute-start.9 = (bf16[640,128]{1,0:T(8,128)(2,1)S(1)}, bf16[640,128]{1,0:T(8,128)(2,1)S(1)}, u32[]{:S(2)}, u32[]{:S(2)}) collective-permute-start(bf16[640,128]{1,0:T(8,128)(2,1)S(1)} %get-tuple-element.40.grad_ref.refs_0_), channel_id=1, source_target_pairs={{0,1},{1,0},{2,3},{3,2},{4,5},{5,4},{6,7},{7,6},{8,9},{9,8},{10,11... | collective-permute-start | bytes 491528 | tf_op jit(solution)/shard_map/ppermute | solution.py:203
  30.5 1.2 %collective-permute-start.8 = (bf16[640,128]{1,0:T(8,128)(2,1)S(1)}, bf16[640,128]{1,0:T(8,128)(2,1)S(1)}, u32[]{:S(2)}, u32[]{:S(2)}) collective-permute-start(bf16[640,128]{1,0:T(8,128)(2,1)S(1)} %get-tuple-element.40.grad_ref.refs_0_), channel_id=1, source_target_pairs={{0,2},{1,3},{2,0},{3,1},{4,6},{5,7},{6,4},{7,5},{8,10},{9,11},{10,... | collective-permute-start | bytes 491528 | tf_op jit(solution)/shard_map/ppermute | solution.py:203
  31.8 0.3 backward_own.1.total_ref
  32.1 2.7 %collective-permute-done.10.refs_2_.refs_3_ = bf16[640,128]{1,0:T(8,128)(2,1)S(1)} collective-permute-done((bf16[640,128]{1,0:T(8,128)(2,1)S(1)}, bf16[640,128]{1,0:T(8,128)(2,1)S(1)}, u32[]{:S(2)}, u32[]{:S(2)}) %collective-permute-start.10) | collective-permute-done | bytes 163872 | tf_op jit(solution)/shard_map/ppermute | solution.py:203
  34.8 0.8 %collective-permute-done.9.refs_1_.refs_2_ = bf16[640,128]{1,0:T(8,128)(2,1)S(1)} collective-permute-done((bf16[640,128]{1,0:T(8,128)(2,1)S(1)}, bf16[640,128]{1,0:T(8,128)(2,1)S(1)}, u32[]{:S(2)}, u32[]{:S(2)}) %collective-permute-start.9) | collective-permute-done | bytes 163872 | tf_op jit(solution)/shard_map/ppermute | solution.py:203
  35.6 0.9 %collective-permute-done.8.refs_0_.refs_1_ = bf16[640,128]{1,0:T(8,128)(2,1)S(1)} collective-permute-done((bf16[640,128]{1,0:T(8,128)(2,1)S(1)}, bf16[640,128]{1,0:T(8,128)(2,1)S(1)}, u32[]{:S(2)}, u32[]{:S(2)}) %collective-permute-start.8) | collective-permute-done | bytes 163872 | tf_op jit(solution)/shard_map/ppermute | solution.py:203
  36.5 0.5 %backward_sent.1 = bf16[640,128]{1,0:T(8,128)(2,1)S(1)} custom-call(bf16[2176,1024]{1,0:T(8,128)(2,1)S(1)} %densify.1.refs_0_.dense_ref, f32[128,1024]{1,0:T(8,128)S(1)} %backward_own.1.total_ref, bf16[640,128]{1,0:T(8,128)(2,1)S(1)} %get-tuple-element.40.grad_ref.refs_0_, bf16[640,128]{1,0:T(8,128)(2,1)S(1)} %collective-permute-done.8.refs_0_.refs_1_, ...), custom_call_target="tpu_custom_call" | custom-call | flops 268435456 | bytes 163840 | tf_op jit(solution)/shard_map/backward_sent/pallas_call | solution.py:249
  37.0 0.1 collective-permute-start.11
  37.1 0.5 %backward_kept.1 = f32[512,128]{1,0:T(8,128)S(1)} custom-call(bf16[2176,1024]{1,0:T(8,128)(2,1)S(1)} %densify.1.refs_0_.dense_ref, f32[128,1024]{1,0:T(8,128)S(1)} %backward_own.1.total_ref, bf16[640,128]{1,0:T(8,128)(2,1)S(1)} %collective-permute-done.8.refs_0_.refs_1_, bf16[640,128]{1,0:T(8,128)(2,1)S(1)} %collective-permute-done.9.refs_1_.refs_2_, ...), custom_call_target="tpu_custom_call" | custom-call | flops 268435456 | bytes 262144 | tf_op jit(solution)/shard_map/backward_kept/pallas_call | solution.py:249
  37.6 0.9 %collective-permute-done.11 = bf16[640,128]{1,0:T(8,128)(2,1)S(1)} collective-permute-done((bf16[640,128]{1,0:T(8,128)(2,1)S(1)}, bf16[640,128]{1,0:T(8,128)(2,1)S(1)}, u32[]{:S(2)}, u32[]{:S(2)}) %collective-permute-start.11) | collective-permute-done | bytes 163872 | tf_op jit(solution)/shard_map/ppermute | solution.py:203
  38.5 1.6 %collective-permute-start.12 = (bf16[384,128]{1,0:T(8,128)(2,1)S(1)}, bf16[384,128]{1,0:T(8,128)(2,1)S(1)}, u32[]{:S(2)}, u32[]{:S(2)}) collective-permute-start(bf16[384,128]{1,0:T(8,128)(2,1)S(1)} %pad_maximum_fusion.own_ref), channel_id=1, source_target_pairs={{0,16},{8,24},{16,0},{24,8},{1,17},{9,25},{17,1},{25,9},{2,18},{10... | collective-permute-start | bytes 294920 | tf_op jit(solution)/shard_map/ppermute | solution.py:203
  40.1 0.6 %emit.1 = bf16[256,128]{1,0:T(8,128)(2,1)} custom-call(bf16[256,128]{1,0:T(8,128)(2,1)S(1)} %get-tuple-element.39.given_ref), custom_call_target="tpu_custom_call" | custom-call | bytes 65536 | tf_op jit(solution)/shard_map/emit/pallas_call | solution.py:333
  40.8 2.7 %collective-permute-done.12.other_ref = bf16[384,128]{1,0:T(8,128)(2,1)S(1)} collective-permute-done((bf16[384,128]{1,0:T(8,128)(2,1)S(1)}, bf16[384,128]{1,0:T(8,128)(2,1)S(1)}, u32[]{:S(2)}, u32[]{:S(2)}) %collective-permute-start.12) | collective-permute-done | bytes 98336 | tf_op jit(solution)/shard_map/ppermute | solution.py:203
  43.5 0.8 %finish.1 = (bf16[256,128]{1,0:T(8,128)(2,1)}, f32[128,128]{1,0:T(8,128)}) custom-call(f32[256,128]{1,0:T(8,128)S(1)} %slice.22.keep_ref, bf16[384,128]{1,0:T(8,128)(2,1)S(1)} %pad_maximum_fusion.own_ref, bf16[384,128]{1,0:T(8,128)(2,1)S(1)} %collective-permute-done.12.other_ref, bf16[128,128]{1,0:T(8,128)(2,1)S(1)} %copy-done.1), custom_call_target="tpu_custom_call" | custom-call | flops 8388608 | bytes 131072 | tf_op jit(solution)/shard_map/finish/pallas_call | solution.py:347
  (5 shorter events, 0.1 us)
Async XLA Ops:
  0.6 6.8 %copy-start = (bf16[256,128]{1,0:T(8,128)(2,1)S(1)}, bf16[256,128]{1,0:T(8,128)(2,1)}, u32[]{:S(2)}) copy-start(bf16[256,128]{1,0:T(8,128)(2,1)} %refs_1_.3) | copy-start | bytes 196612
  0.6 5.5 %collective-permute-start = (bf16[256,128]{1,0:T(8,128)(2,1)}, bf16[256,128]{1,0:T(8,128)(2,1)S(1)}, u32[]{:S(2)}, u32[]{:S(2)}) collective-permute-start(bf16[256,128]{1,0:T(8,128)(2,1)} %refs_1_.3), channel_id=1, source_target_pairs={{0,16},{8,24},{16,0},{24,8},{1,17},{9,25},{17,1},{25,9},{2,18},{10... | collective-permute-start | bytes 196616 | tf_op jit(solution)/shard_map/ppermute | solution.py:203
  3.7 2.8 %collective-permute-start.1 = (bf16[256,128]{1,0:T(8,128)(2,1)}, bf16[256,128]{1,0:T(8,128)(2,1)S(1)}, u32[]{:S(2)}, u32[]{:S(2)}) collective-permute-start(bf16[256,128]{1,0:T(8,128)(2,1)} %refs_1_.3), channel_id=1, source_target_pairs={{0,8},{8,0},{16,24},{24,16},{1,9},{9,1},{17,25},{25,17},{2,10},{10... | collective-permute-start | bytes 196616 | tf_op jit(solution)/shard_map/ppermute | solution.py:203
  4.3 7.7 %copy-start.2 = (bf16[256,128]{1,0:T(8,128)(2,1)S(1)}, bf16[256,128]{1,0:T(8,128)(2,1)}, u32[]{:S(2)}) copy-start(bf16[256,128]{1,0:T(8,128)(2,1)} %refs_0_) | copy-start | bytes 196612
  6.0 21.7 %copy-start.1 = (bf16[128,128]{1,0:T(8,128)(2,1)S(1)}, bf16[128,128]{1,0:T(8,128)(2,1)}, u32[]{:S(2)}) copy-start(bf16[128,128]{1,0:T(8,128)(2,1)} %weight_ref.3) | copy-start | bytes 98308
  6.1 1.3 %collective-permute-start.2 = (bf16[256,128]{1,0:T(8,128)(2,1)S(1)}, bf16[256,128]{1,0:T(8,128)(2,1)S(1)}, u32[]{:S(2)}, u32[]{:S(2)}) collective-permute-start(bf16[256,128]{1,0:T(8,128)(2,1)S(1)} %collective-permute-done.refs_2_), channel_id=1, source_target_pairs={{0,8},{8,0},{16,24},{24,16},{1,9},{9,1},{17,25},{25,17},{2,10},{10... | collective-permute-start | bytes 196616 | tf_op jit(solution)/shard_map/ppermute | solution.py:203
  8.4 8.1 %collective-permute-start.3 = (bf16[512,128]{1,0:T(8,128)(2,1)S(1)}, bf16[512,128]{1,0:T(8,128)(2,1)S(1)}, u32[]{:S(2)}, u32[]{:S(2)}) collective-permute-start(bf16[512,128]{1,0:T(8,128)(2,1)S(1)} %get-tuple-element.32), channel_id=1, source_target_pairs={{0,2},{1,3},{2,0},{3,1},{4,6},{5,7},{6,4},{7,5},{8,10},{9,11},{10,... | collective-permute-start | bytes 393224 | tf_op jit(solution)/shard_map/ppermute | solution.py:203
  10.5 8.1 %collective-permute-start.4 = (bf16[512,128]{1,0:T(8,128)(2,1)S(1)}, bf16[512,128]{1,0:T(8,128)(2,1)S(1)}, u32[]{:S(2)}, u32[]{:S(2)}) collective-permute-start(bf16[512,128]{1,0:T(8,128)(2,1)S(1)} %get-tuple-element.33), channel_id=1, source_target_pairs={{0,1},{1,0},{2,3},{3,2},{4,5},{5,4},{6,7},{7,6},{8,9},{9,8},{10,11... | collective-permute-start | bytes 393224 | tf_op jit(solution)/shard_map/ppermute | solution.py:203
  12.0 6.6 %collective-permute-start.5 = (bf16[512,128]{1,0:T(8,128)(2,1)S(1)}, bf16[512,128]{1,0:T(8,128)(2,1)S(1)}, u32[]{:S(2)}, u32[]{:S(2)}) collective-permute-start(bf16[512,128]{1,0:T(8,128)(2,1)S(1)} %get-tuple-element.34), channel_id=1, source_target_pairs={{0,3},{1,2},{2,1},{3,0},{4,7},{5,6},{6,5},{7,4},{8,11},{9,10},{10,... | collective-permute-start | bytes 393224 | tf_op jit(solution)/shard_map/ppermute | solution.py:203
  12.1 8.7 %collective-permute-start.6 = (bf16[256,128]{1,0:T(8,128)(2,1)S(1)}, bf16[256,128]{1,0:T(8,128)(2,1)S(1)}, u32[]{:S(2)}, u32[]{:S(2)}) collective-permute-start(bf16[256,128]{1,0:T(8,128)(2,1)S(1)} %copy-done.2), channel_id=1, source_target_pairs={{0,6},{1,7},{2,4},{3,5},{4,2},{5,3},{6,0},{7,1},{8,14},{9,15},{10,... | collective-permute-start | bytes 196616 | tf_op jit(solution)/shard_map/ppermute | solution.py:203
  20.8 6.9 %collective-permute-start.7 = (bf16[512,128]{1,0:T(8,128)(2,1)S(1)}, bf16[512,128]{1,0:T(8,128)(2,1)S(1)}, u32[]{:S(2)}, u32[]{:S(2)}) collective-permute-start(bf16[512,128]{1,0:T(8,128)(2,1)S(1)} %add_convert_fusion.left_ref), channel_id=1, source_target_pairs={{0,6},{1,7},{2,4},{3,5},{4,2},{5,3},{6,0},{7,1},{8,14},{9,15},{10,... | collective-permute-start | bytes 393224 | tf_op jit(solution)/shard_map/ppermute | solution.py:203
  28.2 6.6 %collective-permute-start.10 = (bf16[640,128]{1,0:T(8,128)(2,1)S(1)}, bf16[640,128]{1,0:T(8,128)(2,1)S(1)}, u32[]{:S(2)}, u32[]{:S(2)}) collective-permute-start(bf16[640,128]{1,0:T(8,128)(2,1)S(1)} %get-tuple-element.40.grad_ref.refs_0_), channel_id=1, source_target_pairs={{0,3},{1,2},{2,1},{3,0},{4,7},{5,6},{6,5},{7,4},{8,11},{9,10},{10,... | collective-permute-start | bytes 491528 | tf_op jit(solution)/shard_map/ppermute | solution.py:203
  28.5 7.1 %collective-permute-start.9 = (bf16[640,128]{1,0:T(8,128)(2,1)S(1)}, bf16[640,128]{1,0:T(8,128)(2,1)S(1)}, u32[]{:S(2)}, u32[]{:S(2)}) collective-permute-start(bf16[640,128]{1,0:T(8,128)(2,1)S(1)} %get-tuple-element.40.grad_ref.refs_0_), channel_id=1, source_target_pairs={{0,1},{1,0},{2,3},{3,2},{4,5},{5,4},{6,7},{7,6},{8,9},{9,8},{10,11... | collective-permute-start | bytes 491528 | tf_op jit(solution)/shard_map/ppermute | solution.py:203
  30.5 6.0 %collective-permute-start.8 = (bf16[640,128]{1,0:T(8,128)(2,1)S(1)}, bf16[640,128]{1,0:T(8,128)(2,1)S(1)}, u32[]{:S(2)}, u32[]{:S(2)}) collective-permute-start(bf16[640,128]{1,0:T(8,128)(2,1)S(1)} %get-tuple-element.40.grad_ref.refs_0_), channel_id=1, source_target_pairs={{0,2},{1,3},{2,0},{3,1},{4,6},{5,7},{6,4},{7,5},{8,10},{9,11},{10,... | collective-permute-start | bytes 491528 | tf_op jit(solution)/shard_map/ppermute | solution.py:203
  37.0 1.5 %collective-permute-start.11 = (bf16[640,128]{1,0:T(8,128)(2,1)S(1)}, bf16[640,128]{1,0:T(8,128)(2,1)S(1)}, u32[]{:S(2)}, u32[]{:S(2)}) collective-permute-start(bf16[640,128]{1,0:T(8,128)(2,1)S(1)} %backward_sent.1), channel_id=1, source_target_pairs={{0,8},{8,0},{16,24},{24,16},{1,9},{9,1},{17,25},{25,17},{2,10},{10... | collective-permute-start | bytes 491528 | tf_op jit(solution)/shard_map/ppermute | solution.py:203
  38.5 4.9 %collective-permute-start.12 = (bf16[384,128]{1,0:T(8,128)(2,1)S(1)}, bf16[384,128]{1,0:T(8,128)(2,1)S(1)}, u32[]{:S(2)}, u32[]{:S(2)}) collective-permute-start(bf16[384,128]{1,0:T(8,128)(2,1)S(1)} %pad_maximum_fusion.own_ref), channel_id=1, source_target_pairs={{0,16},{8,24},{16,0},{24,8},{1,17},{9,25},{17,1},{25,9},{2,18},{10... | collective-permute-start | bytes 294920 | tf_op jit(solution)/shard_map/ppermute | solution.py:203

commit v3 on v2

--- a/solution.py
+++ b/solution.py
@@ -11,6 +11,7 @@
 F32 = jnp.float32
 BF16 = jnp.bfloat16
 VMEM_LIMIT = 24 * 1024 * 1024
+DENSIFY_PARTS = 6
 DENSE_LIMIT = 12 * 1024 * 1024
 
 
@@ -37,7 +38,6 @@
     )
 
 
-SPLIT = True
 VM = pl.BlockSpec(memory_space=pltpu.VMEM)
 ANY = pl.BlockSpec(memory_space=pl.ANY)
 
@@ -62,22 +62,24 @@
     return value >> (by.bit_length() - 1), value & (by - 1)
 
 
-def place_of(slot, my_row, my_col, row_bits, near, share_tiles, group_tiles):
-    tile_row, tile_col = quotient(slot, share_tiles << row_bits)
-    row_share, row_rest = quotient(tile_row, share_tiles)
-    col_share, col_rest = quotient(tile_col, share_tiles)
-    apart = row_share ^ my_col
+def row_place(tile_row, my_col, near, share_tiles, group_tiles):
+    share, rest = quotient(tile_row, share_tiles)
+    apart = share ^ my_col
     if near:
         apart = apart ^ (((apart >> near) & 1) << (near - 1))
     mask = apart & ((1 << near) - 1)
     group = mask * 0
     for at, partner in enumerate(PARTNERS[near]):
         group = jnp.where(mask == partner, at + 1, group)
-    row_at = group * group_tiles + (row_share >> near) * share_tiles + row_rest
-    return row_at, bit_reverse(col_share ^ my_row, row_bits) * share_tiles + col_rest
-
-
-def densify(place, parts, tiles_ref, slots_ref, count_ref, dense_ref, held, slots, sems):
+    return group * group_tiles + (share >> near) * share_tiles + rest
+
+
+def col_place(tile_col, my_row, row_bits, share_tiles):
+    share, rest = quotient(tile_col, share_tiles)
+    return bit_reverse(share ^ my_row, row_bits) * share_tiles + rest
+
+
+def densify(row_of, col_of, parts, tiles_ref, slots_ref, count_ref, dense_ref, held, slots, row_at, col_at, sems):
     total, size, _ = held.shape
     step = -(-total // parts)
     copies = [pltpu.make_async_copy(slots_ref, slots, sems.at[parts])]
@@ -88,37 +90,61 @@
         copy.start()
     dense_ref[...] = jnp.zeros_like(dense_ref)
     my_row, my_col = lax.axis_index("row"), lax.axis_index("col")
-    dead = dense_ref.shape[0] // size - 1
+    for at in range(row_at.shape[0]):
+        row_at[at] = row_of(jnp.int32(at), my_col) * size
+    for at in range(col_at.shape[0]):
+        col_at[at] = col_of(jnp.int32(at), my_row) * size
+    dead = dense_ref.shape[0] - size
     count = count_ref[0, 0]
-    for copy in copies:
+    copies[0].wait()
+    unroll = 4
+    for copy, start in zip(copies[1:], range(0, total, step)):
+        end = min(start + step, total)
         copy.wait()
-    unroll = 4
-
-    def some_tiles(first, carry):
-        for inner in range(unroll):
-            k = jnp.minimum(first * unroll + inner, total - 1)
-            row_at, col_at = place(slots[0, 0, k], my_row, my_col)
-            row_at = jnp.where(first * unroll + inner < count, row_at, dead)
-            rows = pl.ds(pl.multiple_of(row_at * size, size), size)
-            cols = pl.ds(pl.multiple_of(col_at * size, size), size)
-            dense_ref[rows, cols] = held[k]
-        return carry
-
-    lax.fori_loop(0, (count + unroll - 1) // unroll, some_tiles, 0)
-
-
-def forward(parts, groups, *refs):
-    dense_ref, pieces, outs = refs[0], refs[1 : 1 + parts], refs[1 + parts :]
-    for m, ref in zip(groups, outs):
-        group, total, at = ref.shape[0], None, 0
-        for piece in pieces:
-            depth = piece.shape[0]
-            term = jnp.dot(
-                dense_ref[m * group : (m + 1) * group, at : at + depth], piece[...], preferred_element_type=F32
-            )
-            total = term if total is None else total + term
-            at += depth
-        ref[...] = total.astype(ref.dtype)
+
+        def some_tiles(turn, carry, start=start, end=end):
+            for inner in range(unroll):
+                k = start + turn * unroll + inner
+                at = jnp.minimum(k, end - 1)
+                tile_row, tile_col = quotient(slots[0, 0, at], col_at.shape[0])
+                row = jnp.where((k < count) & (k < end), row_at[tile_row], dead)
+                rows = pl.ds(pl.multiple_of(row, size), size)
+                cols = pl.ds(pl.multiple_of(col_at[tile_col], size), size)
+                dense_ref[rows, cols] = held[at]
+            return carry
+
+        turns = (jnp.clip(count - start, 0, end - start) + unroll - 1) // unroll
+        lax.fori_loop(0, turns, some_tiles, 0)
+
+
+def rows_of(dense_ref, pieces, first, step, rows):
+    total = None
+    for at, piece in enumerate(pieces):
+        depth = piece.shape[0]
+        start = (first + at * step) * depth
+        term = jnp.dot(dense_ref[rows, start : start + depth], piece[...], preferred_element_type=F32)
+        total = term if total is None else total + term
+    return total
+
+
+def forward_early(sent, dense_ref, *refs):
+    pieces, total_ref = refs[:-1], refs[-1]
+    rows = total_ref.shape[0]
+    group = rows // sent
+    total_ref[...] = rows_of(dense_ref, pieces, 0, 2, slice(group, group + rows))
+
+
+def forward_sent(parts, dense_ref, total_ref, *refs):
+    pieces, outs = refs[:parts], refs[parts:]
+    for m, ref in enumerate(outs):
+        group = ref.shape[0]
+        total = rows_of(dense_ref, pieces, 1, 2, slice((m + 1) * group, (m + 2) * group))
+        ref[...] = (total + total_ref[m * group : (m + 1) * group, :]).astype(BF16)
+
+
+def forward_own(dense_ref, *refs):
+    pieces, out_ref = refs[:-1], refs[-1]
+    out_ref[...] = rows_of(dense_ref, pieces, 0, 1, slice(0, out_ref.shape[0]))
 
 
 def middle(near, share, left_ref, right_ref, weight_ref, *refs):
@@ -204,9 +230,9 @@
 
 
 class DenseBlock:
-    def __init__(self, place, rows, cols, tiles, tile_slots, tile_counts):
+    def __init__(self, row_of, col_of, rows, cols, tiles, tile_slots, tile_counts):
         (self.dense,) = kernel_call(
-            functools.partial(densify, place, 4),
+            functools.partial(densify, row_of, col_of, DENSIFY_PARTS),
             [((rows + tiles.shape[-1], cols), BF16, True)],
             0,
             "densify",
@@ -214,7 +240,9 @@
             [
                 pltpu.VMEM(tiles.shape[2:], BF16),
                 pltpu.SMEM(tile_slots.shape, jnp.int32),
-                pltpu.SemaphoreType.DMA((5,)),
+                pltpu.SMEM((rows // tiles.shape[-1],), jnp.int32),
+                pltpu.SMEM((cols // tiles.shape[-1],), jnp.int32),
+                pltpu.SemaphoreType.DMA((DENSIFY_PARTS + 1,)),
             ],
         )(in_hbm(tiles), in_hbm(tile_slots), tile_counts)
         self.rows, self.cols = rows, cols
@@ -225,20 +253,27 @@
 
     def forward(self, pieces, groups):
         width, group = pieces[0].shape[-1], self.rows // groups
-
-        def some(name, which, dtype):
-            return kernel_call(
-                functools.partial(forward, len(pieces), which),
-                [((group, width), dtype, True) for _ in which],
-                2 * len(which) * group * self.cols * width,
-                name,
-                [VM] * (1 + len(pieces)),
-            )(in_vmem(self.dense), *pieces)
-
-        sends = some("forward_sent", range(1, groups), BF16) if groups > 1 else []
-        if SPLIT:
-            (self.dense, sends) = lax.optimization_barrier((self.dense, sends))
-        return [*some("forward_own", [0], F32), *sends]
+        sent = groups - 1
+        dense = in_vmem(self.dense)
+        flops = 2 * group * self.cols * width
+
+        def some(kernel, outs, flops, name, *given):
+            return kernel_call(kernel, outs, flops, name, [VM] * (1 + len(given)))(dense, *given)
+
+        (total,) = some(
+            functools.partial(forward_early, sent), [((sent * group, width), F32, True)], flops * sent // 2, "forward_early", *pieces[::2]
+        )
+        late = pieces[1::2]
+        sends = some(
+            functools.partial(forward_sent, len(late)),
+            [((group, width), BF16, True)] * sent,
+            flops * sent // 2,
+            "forward_sent",
+            total,
+            *late,
+        )
+        (own,) = some(forward_own, [((group, width), F32, True)], flops, "forward_own", *pieces)
+        return [own, *sends]
 
     def backward(self, grads):
         rows, cols = self.rows, self.cols
@@ -257,11 +292,13 @@
 
 
 class TiledBlock:
-    def __init__(self, place, rows, cols, tiles, tile_slots, tile_counts):
+    def __init__(self, row_of, col_of, rows, cols, tiles, tile_slots, tile_counts):
         self.tiles, slots = tiles[0, 0], tile_slots[0, 0]
         self.size = self.tiles.shape[-1]
         self.row_count, self.col_count = rows // self.size, cols // self.size
-        self.row_at, self.col_at = place(slots, lax.axis_index("row"), lax.axis_index("col"))
+        tile_row, tile_col = quotient(slots, self.col_count)
+        self.row_at = row_of(tile_row, lax.axis_index("col"))
+        self.col_at = col_of(tile_col, lax.axis_index("row"))
         self.live = jnp.arange(slots.shape[0], dtype=jnp.int32) < tile_counts[0, 0]
 
     def after(self, x):
@@ -295,11 +332,10 @@
     near = min(2, col_bits)
     rows, cols = share * col_count, share * row_count
     group = rows >> near
-    place = functools.partial(
-        place_of, row_bits=row_bits, near=near, share_tiles=share // size, group_tiles=group // size
-    )
+    row_of = functools.partial(row_place, near=near, share_tiles=share // size, group_tiles=group // size)
+    col_of = functools.partial(col_place, row_bits=row_bits, share_tiles=share // size)
     block_type = DenseBlock if 2 * rows * cols <= DENSE_LIMIT else TiledBlock
-    block = block_type(place, rows, cols, tiles, tile_slots, tile_counts)
+    block = block_type(row_of, col_of, rows, cols, tiles, tile_slots, tile_counts)
 
     pieces = [features]
     for bit in reversed(range(row_bits)):

time: 44.4 us -> 44 us (level)
    pallas_call x3 -> x4, Pallas kernels: 3.07 us -> 2.94 us  [the longest x3 1.58 us: some(): kernel_call(kernel, outs, flops, name, [VM] * (1 + len(given)))]
  transfers between devices with their start and end apart: 13 -> 13, of which waited for: 10 -> 10; matrix products, arithmetic and copies ran while one was open for 0% -> 0% of each run, Pallas kernels for 8% -> 9%
where the time goes in v3:
time: 44 us; the launch traced here: 43.8 us
  starting transfers between devices  18.7 us (42%)
  waiting for transfers between devices  17.4 us (40%)
  Pallas kernels  6.25 us (14%)
  between operations  1.42 us (3%)
    ppermute x13, starting transfers between devices, swap(): return lax.ppermute(x, axis, [(i, i ^ mask) for i in range(n)])  18.7 us
    ppermute x13, waiting for transfers between devices, swap(): return lax.ppermute(x, axis, [(i, i ^ mask) for i in range(n)])  17.4 us
    pallas_call x3, Pallas kernels, some(): kernel_call(kernel, outs, flops, name, [VM] * (1 + len(given)))  1.58 us
    pallas_call x1, Pallas kernels, __init__(): kernel_call(functools.partial(densify, row_of, col_of, DENSIFY_PARTS), [(...  1.36 us
    pallas_call x3, Pallas kernels, some(): kernel_call(kernel, [(shape, dtype, True)], flops, name, [VM] * (1 + len(...  1.3 us
  transfers between devices with their start and end apart: 13, of which 10 were waited for; matrix products, arithmetic and copies ran while one was open for 0% of the time, Pallas kernels for 9%

profile of v3, /device:TPU:0, one launch (start us, length us, event | category | flops | bytes accessed | tf_op | source)
XLA Modules:
  0.0 43.8 jit_solution(11158921750299244969)
XLA Ops:
  0.6 0.0 copy-start
  0.6 3.0 %collective-permute-start = (bf16[256,128]{1,0:T(8,128)(2,1)}, bf16[256,128]{1,0:T(8,128)(2,1)S(1)}, u32[]{:S(2)}, u32[]{:S(2)}) collective-permute-start(bf16[256,128]{1,0:T(8,128)(2,1)} %refs_0_.3), channel_id=1, source_target_pairs={{0,16},{8,24},{16,0},{24,8},{1,17},{9,25},{17,1},{25,9},{2,18},{10... | collective-permute-start | bytes 196616 | tf_op jit(solution)/shard_map/ppermute | solution.py:229
  3.7 0.0 collective-permute-start.1
  4.3 1.4 %densify.1.dense_ref = bf16[2176,1024]{1,0:T(8,128)(2,1)S(1)} custom-call(bf16[1,1,44,128,128]{4,3,2,1,0:T(8,128)(2,1)} %tiles_ref.1, s32[1,1,44]{2,1,0:T(1,128)} %slots_ref.1, s32[1,1]{1,0:T(1,128)S(6)} %copy.9.count_ref), custom_call_target="tpu_custom_call" | custom-call | bytes 4456448 | tf_op jit(solution)/shard_map/densify/pallas_call | solution.py:234
  5.7 0.0 copy-start.2
  5.7 0.4 collective-permute-done.refs_1_.refs_0_
  6.1 0.2 collective-permute-start.2
  6.3 0.0 collective-permute-done.1.refs_2_.refs_1_
  6.3 0.0 copy-done
  6.3 0.6 %forward_early.1.total_ref = f32[1536,128]{1,0:T(8,128)S(1)} custom-call(bf16[2176,1024]{1,0:T(8,128)(2,1)S(1)} %densify.1.dense_ref, bf16[256,128]{1,0:T(8,128)(2,1)S(1)} %copy-done, bf16[256,128]{1,0:T(8,128)(2,1)S(1)} %collective-permute-done.1.refs_2_.refs_1_), custom_call_target="tpu_custom_call" | custom-call | flops 201326592 | bytes 786432 | tf_op jit(solution)/shard_map/forward_early/pallas_call | solution.py:261
  6.9 0.0 copy-start.1
  6.9 0.5 %collective-permute-done.2.refs_3_.refs_1_ = bf16[256,128]{1,0:T(8,128)(2,1)S(1)} collective-permute-done((bf16[256,128]{1,0:T(8,128)(2,1)S(1)}, bf16[256,128]{1,0:T(8,128)(2,1)S(1)}, u32[]{:S(2)}, u32[]{:S(2)}) %collective-permute-start.2) | collective-permute-done | bytes 65568 | tf_op jit(solution)/shard_map/ppermute | solution.py:229
  7.4 0.6 %forward_sent.1 = (bf16[512,128]{1,0:T(8,128)(2,1)S(1)}, bf16[512,128]{1,0:T(8,128)(2,1)S(1)}, bf16[512,128]{1,0:T(8,128)(2,1)S(1)}) custom-call(bf16[2176,1024]{1,0:T(8,128)(2,1)S(1)} %densify.1.dense_ref, f32[1536,128]{1,0:T(8,128)S(1)} %forward_early.1.total_ref, bf16[256,128]{1,0:T(8,128)(2,1)S(1)} %collective-permute-done.refs_1_.refs_0_, ...), custom_call_target="tpu_custom_call" | custom-call | flops 201326592 | bytes 393216 | tf_op jit(solution)/shard_map/forward_sent/pallas_call | solution.py:261
  8.0 2.1 %collective-permute-start.3 = (bf16[512,128]{1,0:T(8,128)(2,1)S(1)}, bf16[512,128]{1,0:T(8,128)(2,1)S(1)}, u32[]{:S(2)}, u32[]{:S(2)}) collective-permute-start(bf16[512,128]{1,0:T(8,128)(2,1)S(1)} %get-tuple-element.24), channel_id=1, source_target_pairs={{0,2},{1,3},{2,0},{3,1},{4,6},{5,7},{6,4},{7,5},{8,10},{9,11},{10,... | collective-permute-start | bytes 393224 | tf_op jit(solution)/shard_map/ppermute | solution.py:229
  10.1 1.5 %collective-permute-start.4 = (bf16[512,128]{1,0:T(8,128)(2,1)S(1)}, bf16[512,128]{1,0:T(8,128)(2,1)S(1)}, u32[]{:S(2)}, u32[]{:S(2)}) collective-permute-start(bf16[512,128]{1,0:T(8,128)(2,1)S(1)} %get-tuple-element.25), channel_id=1, source_target_pairs={{0,1},{1,0},{2,3},{3,2},{4,5},{5,4},{6,7},{7,6},{8,9},{9,8},{10,11... | collective-permute-start | bytes 393224 | tf_op jit(solution)/shard_map/ppermute | solution.py:229
  11.6 0.0 collective-permute-start.5
  11.6 0.0 copy-done.2
  11.7 4.0 %collective-permute-start.6 = (bf16[256,128]{1,0:T(8,128)(2,1)S(1)}, bf16[256,128]{1,0:T(8,128)(2,1)S(1)}, u32[]{:S(2)}, u32[]{:S(2)}) collective-permute-start(bf16[256,128]{1,0:T(8,128)(2,1)S(1)} %copy-done.2), channel_id=1, source_target_pairs={{0,6},{1,7},{2,4},{3,5},{4,2},{5,3},{6,0},{7,1},{8,14},{9,15},{10,... | collective-permute-start | bytes 196616 | tf_op jit(solution)/shard_map/ppermute | solution.py:229
  15.6 0.4 forward_own.1
  16.1 0.0 collective-permute-done.3
  16.1 2.1 %collective-permute-done.4 = bf16[512,128]{1,0:T(8,128)(2,1)S(1)} collective-permute-done((bf16[512,128]{1,0:T(8,128)(2,1)S(1)}, bf16[512,128]{1,0:T(8,128)(2,1)S(1)}, u32[]{:S(2)}, u32[]{:S(2)}) %collective-permute-start.4) | collective-permute-done | bytes 131104 | tf_op jit(solution)/shard_map/ppermute | solution.py:229
  18.2 0.0 collective-permute-done.5
  18.2 0.1 add_convert_fusion.left_ref
  18.3 2.1 %collective-permute-done.6.refs_1_ = bf16[256,128]{1,0:T(8,128)(2,1)S(1)} collective-permute-done((bf16[256,128]{1,0:T(8,128)(2,1)S(1)}, bf16[256,128]{1,0:T(8,128)(2,1)S(1)}, u32[]{:S(2)}, u32[]{:S(2)}) %collective-permute-start.6) | collective-permute-done | bytes 65568 | tf_op jit(solution)/shard_map/ppermute | solution.py:229
  20.4 2.6 %collective-permute-start.7 = (bf16[512,128]{1,0:T(8,128)(2,1)S(1)}, bf16[512,128]{1,0:T(8,128)(2,1)S(1)}, u32[]{:S(2)}, u32[]{:S(2)}) collective-permute-start(bf16[512,128]{1,0:T(8,128)(2,1)S(1)} %add_convert_fusion.left_ref), channel_id=1, source_target_pairs={{0,6},{1,7},{2,4},{3,5},{4,2},{5,3},{6,0},{7,1},{8,14},{9,15},{10,... | collective-permute-start | bytes 393224 | tf_op jit(solution)/shard_map/ppermute | solution.py:229
  23.0 4.3 %collective-permute-done.7.right_ref = bf16[512,128]{1,0:T(8,128)(2,1)S(1)} collective-permute-done((bf16[512,128]{1,0:T(8,128)(2,1)S(1)}, bf16[512,128]{1,0:T(8,128)(2,1)S(1)}, u32[]{:S(2)}, u32[]{:S(2)}) %collective-permute-start.7) | collective-permute-done | bytes 131104 | tf_op jit(solution)/shard_map/ppermute | solution.py:229
  27.2 0.0 copy-done.1
  27.2 0.6 %middle.1 = (bf16[640,128]{1,0:T(8,128)(2,1)S(1)}, bf16[256,128]{1,0:T(8,128)(2,1)S(1)}) custom-call(bf16[512,128]{1,0:T(8,128)(2,1)S(1)} %add_convert_fusion.left_ref, bf16[512,128]{1,0:T(8,128)(2,1)S(1)} %collective-permute-done.7.right_ref, bf16[128,128]{1,0:T(8,128)(2,1)S(1)} %copy-done.1, bf16[256,128]{1,0:T(8,128)(2,1)S(1)} %copy-done.2, ...), custom_call_target="tpu_custom_call" | custom-call | flops 67108864 | bytes 229376 | tf_op jit(solution)/shard_map/middle/pallas_call | solution.py:361
  27.8 0.3 collective-permute-start.10
  28.1 2.7 %collective-permute-start.8 = (bf16[640,128]{1,0:T(8,128)(2,1)S(1)}, bf16[640,128]{1,0:T(8,128)(2,1)S(1)}, u32[]{:S(2)}, u32[]{:S(2)}) collective-permute-start(bf16[640,128]{1,0:T(8,128)(2,1)S(1)} %get-tuple-element.32.grad_ref.refs_0_), channel_id=1, source_target_pairs={{0,2},{1,3},{2,0},{3,1},{4,6},{5,7},{6,4},{7,5},{8,10},{9,11},{10,... | collective-permute-start | bytes 491528 | tf_op jit(solution)/shard_map/ppermute | solution.py:229
  30.8 0.6 %collective-permute-start.9 = (bf16[640,128]{1,0:T(8,128)(2,1)S(1)}, bf16[640,128]{1,0:T(8,128)(2,1)S(1)}, u32[]{:S(2)}, u32[]{:S(2)}) collective-permute-start(bf16[640,128]{1,0:T(8,128)(2,1)S(1)} %get-tuple-element.32.grad_ref.refs_0_), channel_id=1, source_target_pairs={{0,1},{1,0},{2,3},{3,2},{4,5},{5,4},{6,7},{7,6},{8,9},{9,8},{10,11... | collective-permute-start | bytes 491528 | tf_op jit(solution)/shard_map/ppermute | solution.py:229
  31.4 0.3 backward_own.1.total_ref
  31.7 2.5 %collective-permute-done.10.refs_2_.refs_3_ = bf16[640,128]{1,0:T(8,128)(2,1)S(1)} collective-permute-done((bf16[640,128]{1,0:T(8,128)(2,1)S(1)}, bf16[640,128]{1,0:T(8,128)(2,1)S(1)}, u32[]{:S(2)}, u32[]{:S(2)}) %collective-permute-start.10) | collective-permute-done | bytes 163872 | tf_op jit(solution)/shard_map/ppermute | solution.py:229
  34.2 1.8 %collective-permute-done.8.refs_0_.refs_1_ = bf16[640,128]{1,0:T(8,128)(2,1)S(1)} collective-permute-done((bf16[640,128]{1,0:T(8,128)(2,1)S(1)}, bf16[640,128]{1,0:T(8,128)(2,1)S(1)}, u32[]{:S(2)}, u32[]{:S(2)}) %collective-permute-start.8) | collective-permute-done | bytes 163872 | tf_op jit(solution)/shard_map/ppermute | solution.py:229
  36.0 0.1 collective-permute-done.9.refs_1_.refs_2_
  36.1 0.5 %backward_sent.1 = bf16[640,128]{1,0:T(8,128)(2,1)S(1)} custom-call(bf16[2176,1024]{1,0:T(8,128)(2,1)S(1)} %densify.1.dense_ref, f32[128,1024]{1,0:T(8,128)S(1)} %backward_own.1.total_ref, bf16[640,128]{1,0:T(8,128)(2,1)S(1)} %get-tuple-element.32.grad_ref.refs_0_, bf16[640,128]{1,0:T(8,128)(2,1)S(1)} %collective-permute-done.8.refs_0_.refs_1_, ...), custom_call_target="tpu_custom_call" | custom-call | flops 268435456 | bytes 163840 | tf_op jit(solution)/shard_map/backward_sent/pallas_call | solution.py:284
  36.6 0.1 collective-permute-start.11
  36.7 0.5 %backward_kept.1 = f32[512,128]{1,0:T(8,128)S(1)} custom-call(bf16[2176,1024]{1,0:T(8,128)(2,1)S(1)} %densify.1.dense_ref, f32[128,1024]{1,0:T(8,128)S(1)} %backward_own.1.total_ref, bf16[640,128]{1,0:T(8,128)(2,1)S(1)} %collective-permute-done.8.refs_0_.refs_1_, bf16[640,128]{1,0:T(8,128)(2,1)S(1)} %collective-permute-done.9.refs_1_.refs_2_, ...), custom_call_target="tpu_custom_call" | custom-call | flops 268435456 | bytes 262144 | tf_op jit(solution)/shard_map/backward_kept/pallas_call | solution.py:284
  37.2 0.9 %collective-permute-done.11 = bf16[640,128]{1,0:T(8,128)(2,1)S(1)} collective-permute-done((bf16[640,128]{1,0:T(8,128)(2,1)S(1)}, bf16[640,128]{1,0:T(8,128)(2,1)S(1)}, u32[]{:S(2)}, u32[]{:S(2)}) %collective-permute-start.11) | collective-permute-done | bytes 163872 | tf_op jit(solution)/shard_map/ppermute | solution.py:229
  38.1 1.6 %collective-permute-start.12 = (bf16[384,128]{1,0:T(8,128)(2,1)S(1)}, bf16[384,128]{1,0:T(8,128)(2,1)S(1)}, u32[]{:S(2)}, u32[]{:S(2)}) collective-permute-start(bf16[384,128]{1,0:T(8,128)(2,1)S(1)} %pad_maximum_fusion.own_ref), channel_id=1, source_target_pairs={{0,16},{8,24},{16,0},{24,8},{1,17},{9,25},{17,1},{25,9},{2,18},{10... | collective-permute-start | bytes 294920 | tf_op jit(solution)/shard_map/ppermute | solution.py:229
  39.7 0.6 %emit.1 = bf16[256,128]{1,0:T(8,128)(2,1)} custom-call(bf16[256,128]{1,0:T(8,128)(2,1)S(1)} %get-tuple-element.31.given_ref), custom_call_target="tpu_custom_call" | custom-call | bytes 65536 | tf_op jit(solution)/shard_map/emit/pallas_call | solution.py:369
  40.4 2.7 %collective-permute-done.12.other_ref = bf16[384,128]{1,0:T(8,128)(2,1)S(1)} collective-permute-done((bf16[384,128]{1,0:T(8,128)(2,1)S(1)}, bf16[384,128]{1,0:T(8,128)(2,1)S(1)}, u32[]{:S(2)}, u32[]{:S(2)}) %collective-permute-start.12) | collective-permute-done | bytes 98336 | tf_op jit(solution)/shard_map/ppermute | solution.py:229
  43.0 0.8 %finish.1 = (bf16[256,128]{1,0:T(8,128)(2,1)}, f32[128,128]{1,0:T(8,128)}) custom-call(f32[256,128]{1,0:T(8,128)S(1)} %slice.22.keep_ref, bf16[384,128]{1,0:T(8,128)(2,1)S(1)} %pad_maximum_fusion.own_ref, bf16[384,128]{1,0:T(8,128)(2,1)S(1)} %collective-permute-done.12.other_ref, bf16[128,128]{1,0:T(8,128)(2,1)S(1)} %copy-done.1), custom_call_target="tpu_custom_call" | custom-call | flops 8388608 | bytes 131072 | tf_op jit(solution)/shard_map/finish/pallas_call | solution.py:383
  (5 shorter events, 0.1 us)
Async XLA Ops:
  0.6 5.7 %copy-start = (bf16[256,128]{1,0:T(8,128)(2,1)S(1)}, bf16[256,128]{1,0:T(8,128)(2,1)}, u32[]{:S(2)}) copy-start(bf16[256,128]{1,0:T(8,128)(2,1)} %refs_0_.3) | copy-start | bytes 196612
  0.6 5.5 %collective-permute-start = (bf16[256,128]{1,0:T(8,128)(2,1)}, bf16[256,128]{1,0:T(8,128)(2,1)S(1)}, u32[]{:S(2)}, u32[]{:S(2)}) collective-permute-start(bf16[256,128]{1,0:T(8,128)(2,1)} %refs_0_.3), channel_id=1, source_target_pairs={{0,16},{8,24},{16,0},{24,8},{1,17},{9,25},{17,1},{25,9},{2,18},{10... | collective-permute-start | bytes 196616 | tf_op jit(solution)/shard_map/ppermute | solution.py:229
  3.7 2.6 %collective-permute-start.1 = (bf16[256,128]{1,0:T(8,128)(2,1)}, bf16[256,128]{1,0:T(8,128)(2,1)S(1)}, u32[]{:S(2)}, u32[]{:S(2)}) collective-permute-start(bf16[256,128]{1,0:T(8,128)(2,1)} %refs_0_.3), channel_id=1, source_target_pairs={{0,8},{8,0},{16,24},{24,16},{1,9},{9,1},{17,25},{25,17},{2,10},{10... | collective-permute-start | bytes 196616 | tf_op jit(solution)/shard_map/ppermute | solution.py:229
  5.7 6.0 %copy-start.2 = (bf16[256,128]{1,0:T(8,128)(2,1)S(1)}, bf16[256,128]{1,0:T(8,128)(2,1)}, u32[]{:S(2)}) copy-start(bf16[256,128]{1,0:T(8,128)(2,1)} %refs_0_.4) | copy-start | bytes 196612
  6.1 1.3 %collective-permute-start.2 = (bf16[256,128]{1,0:T(8,128)(2,1)S(1)}, bf16[256,128]{1,0:T(8,128)(2,1)S(1)}, u32[]{:S(2)}, u32[]{:S(2)}) collective-permute-start(bf16[256,128]{1,0:T(8,128)(2,1)S(1)} %collective-permute-done.refs_1_.refs_0_), channel_id=1, source_target_pairs={{0,8},{8,0},{16,24},{24,16},{1,9},{9,1},{17,25},{25,17},{2,10},{10... | collective-permute-start | bytes 196616 | tf_op jit(solution)/shard_map/ppermute | solution.py:229
  6.9 20.4 %copy-start.1 = (bf16[128,128]{1,0:T(8,128)(2,1)S(1)}, bf16[128,128]{1,0:T(8,128)(2,1)}, u32[]{:S(2)}) copy-start(bf16[128,128]{1,0:T(8,128)(2,1)} %weight_ref.3) | copy-start | bytes 98308
  8.0 8.1 %collective-permute-start.3 = (bf16[512,128]{1,0:T(8,128)(2,1)S(1)}, bf16[512,128]{1,0:T(8,128)(2,1)S(1)}, u32[]{:S(2)}, u32[]{:S(2)}) collective-permute-start(bf16[512,128]{1,0:T(8,128)(2,1)S(1)} %get-tuple-element.24), channel_id=1, source_target_pairs={{0,2},{1,3},{2,0},{3,1},{4,6},{5,7},{6,4},{7,5},{8,10},{9,11},{10,... | collective-permute-start | bytes 393224 | tf_op jit(solution)/shard_map/ppermute | solution.py:229
  10.1 8.1 %collective-permute-start.4 = (bf16[512,128]{1,0:T(8,128)(2,1)S(1)}, bf16[512,128]{1,0:T(8,128)(2,1)S(1)}, u32[]{:S(2)}, u32[]{:S(2)}) collective-permute-start(bf16[512,128]{1,0:T(8,128)(2,1)S(1)} %get-tuple-element.25), channel_id=1, source_target_pairs={{0,1},{1,0},{2,3},{3,2},{4,5},{5,4},{6,7},{7,6},{8,9},{9,8},{10,11... | collective-permute-start | bytes 393224 | tf_op jit(solution)/shard_map/ppermute | solution.py:229
  11.6 6.6 %collective-permute-start.5 = (bf16[512,128]{1,0:T(8,128)(2,1)S(1)}, bf16[512,128]{1,0:T(8,128)(2,1)S(1)}, u32[]{:S(2)}, u32[]{:S(2)}) collective-permute-start(bf16[512,128]{1,0:T(8,128)(2,1)S(1)} %get-tuple-element.26), channel_id=1, source_target_pairs={{0,3},{1,2},{2,1},{3,0},{4,7},{5,6},{6,5},{7,4},{8,11},{9,10},{10,... | collective-permute-start | bytes 393224 | tf_op jit(solution)/shard_map/ppermute | solution.py:229
  11.7 8.7 %collective-permute-start.6 = (bf16[256,128]{1,0:T(8,128)(2,1)S(1)}, bf16[256,128]{1,0:T(8,128)(2,1)S(1)}, u32[]{:S(2)}, u32[]{:S(2)}) collective-permute-start(bf16[256,128]{1,0:T(8,128)(2,1)S(1)} %copy-done.2), channel_id=1, source_target_pairs={{0,6},{1,7},{2,4},{3,5},{4,2},{5,3},{6,0},{7,1},{8,14},{9,15},{10,... | collective-permute-start | bytes 196616 | tf_op jit(solution)/shard_map/ppermute | solution.py:229
  20.4 6.9 %collective-permute-start.7 = (bf16[512,128]{1,0:T(8,128)(2,1)S(1)}, bf16[512,128]{1,0:T(8,128)(2,1)S(1)}, u32[]{:S(2)}, u32[]{:S(2)}) collective-permute-start(bf16[512,128]{1,0:T(8,128)(2,1)S(1)} %add_convert_fusion.left_ref), channel_id=1, source_target_pairs={{0,6},{1,7},{2,4},{3,5},{4,2},{5,3},{6,0},{7,1},{8,14},{9,15},{10,... | collective-permute-start | bytes 393224 | tf_op jit(solution)/shard_map/ppermute | solution.py:229
  27.8 6.4 %collective-permute-start.10 = (bf16[640,128]{1,0:T(8,128)(2,1)S(1)}, bf16[640,128]{1,0:T(8,128)(2,1)S(1)}, u32[]{:S(2)}, u32[]{:S(2)}) collective-permute-start(bf16[640,128]{1,0:T(8,128)(2,1)S(1)} %get-tuple-element.32.grad_ref.refs_0_), channel_id=1, source_target_pairs={{0,3},{1,2},{2,1},{3,0},{4,7},{5,6},{6,5},{7,4},{8,11},{9,10},{10,... | collective-permute-start | bytes 491528 | tf_op jit(solution)/shard_map/ppermute | solution.py:229
  28.1 7.9 %collective-permute-start.8 = (bf16[640,128]{1,0:T(8,128)(2,1)S(1)}, bf16[640,128]{1,0:T(8,128)(2,1)S(1)}, u32[]{:S(2)}, u32[]{:S(2)}) collective-permute-start(bf16[640,128]{1,0:T(8,128)(2,1)S(1)} %get-tuple-element.32.grad_ref.refs_0_), channel_id=1, source_target_pairs={{0,2},{1,3},{2,0},{3,1},{4,6},{5,7},{6,4},{7,5},{8,10},{9,11},{10,... | collective-permute-start | bytes 491528 | tf_op jit(solution)/shard_map/ppermute | solution.py:229
  30.8 5.3 %collective-permute-start.9 = (bf16[640,128]{1,0:T(8,128)(2,1)S(1)}, bf16[640,128]{1,0:T(8,128)(2,1)S(1)}, u32[]{:S(2)}, u32[]{:S(2)}) collective-permute-start(bf16[640,128]{1,0:T(8,128)(2,1)S(1)} %get-tuple-element.32.grad_ref.refs_0_), channel_id=1, source_target_pairs={{0,1},{1,0},{2,3},{3,2},{4,5},{5,4},{6,7},{7,6},{8,9},{9,8},{10,11... | collective-permute-start | bytes 491528 | tf_op jit(solution)/shard_map/ppermute | solution.py:229
  36.6 1.5 %collective-permute-start.11 = (bf16[640,128]{1,0:T(8,128)(2,1)S(1)}, bf16[640,128]{1,0:T(8,128)(2,1)S(1)}, u32[]{:S(2)}, u32[]{:S(2)}) collective-permute-start(bf16[640,128]{1,0:T(8,128)(2,1)S(1)} %backward_sent.1), channel_id=1, source_target_pairs={{0,8},{8,0},{16,24},{24,16},{1,9},{9,1},{17,25},{25,17},{2,10},{10... | collective-permute-start | bytes 491528 | tf_op jit(solution)/shard_map/ppermute | solution.py:229
  38.1 4.9 %collective-permute-start.12 = (bf16[384,128]{1,0:T(8,128)(2,1)S(1)}, bf16[384,128]{1,0:T(8,128)(2,1)S(1)}, u32[]{:S(2)}, u32[]{:S(2)}) collective-permute-start(bf16[384,128]{1,0:T(8,128)(2,1)S(1)} %pad_maximum_fusion.own_ref), channel_id=1, source_target_pairs={{0,16},{8,24},{16,0},{24,8},{1,17},{9,25},{17,1},{25,9},{2,18},{10... | collective-permute-start | bytes 294920 | tf_op jit(solution)/shard_map/ppermute | solution.py:229

commit v4 on v3

--- a/solution.py
+++ b/solution.py
@@ -117,12 +117,11 @@
         lax.fori_loop(0, turns, some_tiles, 0)
 
 
-def rows_of(dense_ref, pieces, first, step, rows):
+def rows_of(dense_ref, pieces, first, rows):
     total = None
-    for at, piece in enumerate(pieces):
+    for at, piece in enumerate(pieces, first):
         depth = piece.shape[0]
-        start = (first + at * step) * depth
-        term = jnp.dot(dense_ref[rows, start : start + depth], piece[...], preferred_element_type=F32)
+        term = jnp.dot(dense_ref[rows, at * depth : (at + 1) * depth], piece[...], preferred_element_type=F32)
         total = term if total is None else total + term
     return total
 
@@ -131,45 +130,43 @@
     pieces, total_ref = refs[:-1], refs[-1]
     rows = total_ref.shape[0]
     group = rows // sent
-    total_ref[...] = rows_of(dense_ref, pieces, 0, 2, slice(group, group + rows))
-
-
-def forward_sent(parts, dense_ref, total_ref, *refs):
-    pieces, outs = refs[:parts], refs[parts:]
+    total_ref[...] = rows_of(dense_ref, pieces, 0, slice(group, group + rows))
+
+
+def forward_sent(last, dense_ref, total_ref, piece_ref, *outs):
     for m, ref in enumerate(outs):
         group = ref.shape[0]
-        total = rows_of(dense_ref, pieces, 1, 2, slice((m + 1) * group, (m + 2) * group))
+        total = rows_of(dense_ref, [piece_ref], last, slice((m + 1) * group, (m + 2) * group))
         ref[...] = (total + total_ref[m * group : (m + 1) * group, :]).astype(BF16)
 
 
 def forward_own(dense_ref, *refs):
     pieces, out_ref = refs[:-1], refs[-1]
-    out_ref[...] = rows_of(dense_ref, pieces, 0, 1, slice(0, out_ref.shape[0]))
-
-
-def middle(near, share, left_ref, right_ref, weight_ref, *refs):
-    cot_refs, (send_ref, hidden_ref, agg_ref) = refs[:-3], refs[-3:]
-    group, width = agg_ref.shape[0], left_ref.shape[1]
+    out_ref[...] = rows_of(dense_ref, pieces, 0, slice(0, out_ref.shape[0]))
+
+
+def project(left_ref, weight_ref, out_ref):
+    out_ref[...] = jnp.dot(left_ref[...], weight_ref[...], preferred_element_type=F32)
+
+
+def middle(near, share, first_ref, left_ref, right_ref, weight_ref, *refs):
+    cot_refs, (send_ref, hidden_ref) = refs[:-2], refs[-2:]
+    group, width = left_ref.shape
     place = lax.axis_index("col") >> near
-    weight = jnp.concatenate([weight_ref[...]] * 2)
+    weight = weight_ref[...]
     at = 0
     for cot_ref in cot_refs:
         for start in range(0, cot_ref.shape[0], share):
             rows = pl.ds(pl.multiple_of((place ^ at) * share, share), share)
-            agg = left_ref[rows, :].astype(F32) + right_ref[rows, :].astype(F32)
-            high = agg.astype(BF16)
-            both = jnp.concatenate([high, (agg - high.astype(F32)).astype(BF16)], axis=1)
-            agg_ref[rows, :] = both
-            summed = jnp.dot(both, weight, preferred_element_type=F32)
+            summed = first_ref[rows, :] + jnp.dot(right_ref[rows, :], weight, preferred_element_type=F32)
             gate = 1.0 / (1.0 + jnp.exp(-summed))
             if at == 0:
                 hidden_ref[...] = (summed * gate).astype(BF16)
             slope = gate * (1.0 + summed * (1.0 - gate))
             send_ref[rows, :] = (cot_ref[start : start + share, :].astype(F32) * slope).astype(BF16)
             at += 1
-    term = lax.dot_general(
-        send_ref[:group, :], agg_ref[...], (((0,), (0,)), ((), ())), preferred_element_type=F32
-    )
+    both = jnp.concatenate([left_ref[...], right_ref[...]], axis=1)
+    term = lax.dot_general(send_ref[:group, :], both, (((0,), (0,)), ((), ())), preferred_element_type=F32)
     send_ref[group:, :] = (term[:, :width] + term[:, width:]).T.astype(BF16)
 
 
@@ -203,10 +200,13 @@
 
 def backward_sent(dense_ref, total_ref, *refs):
     grads, send_ref = refs[:-1], refs[-1]
-    kept = total_ref.shape[1] // 2
+    width, kept = total_ref.shape[0], total_ref.shape[1] // 2
     columns = slice(kept, 2 * kept)
     send_ref[:kept, :] = (columns_of(dense_ref, grads[1:], 1, columns) + total_ref[:, columns]).T.astype(BF16)
-    send_ref[kept:, :] = pair_sums([grad[-grad.shape[1] :, :].astype(F32) for grad in grads]).astype(BF16)
+    term = pair_sums([grad[-width:, :].astype(F32) for grad in grads])
+    high = term.astype(BF16)
+    send_ref[kept : kept + width, :] = high
+    send_ref[kept + width :, :] = (term - high.astype(F32)).astype(BF16)
 
 
 def backward_kept(dense_ref, total_ref, *refs):
@@ -260,17 +260,21 @@
         def some(kernel, outs, flops, name, *given):
             return kernel_call(kernel, outs, flops, name, [VM] * (1 + len(given)))(dense, *given)
 
+        last = len(pieces) - 1
         (total,) = some(
-            functools.partial(forward_early, sent), [((sent * group, width), F32, True)], flops * sent // 2, "forward_early", *pieces[::2]
+            functools.partial(forward_early, sent),
+            [((sent * group, width), F32, True)],
+            flops * sent * last // len(pieces),
+            "forward_early",
+            *pieces[:last],
         )
-        late = pieces[1::2]
         sends = some(
-            functools.partial(forward_sent, len(late)),
+            functools.partial(forward_sent, last),
             [((group, width), BF16, True)] * sent,
-            flops * sent // 2,
+            flops * sent // len(pieces),
             "forward_sent",
             total,
-            *late,
+            pieces[last],
         )
         (own,) = some(forward_own, [((group, width), F32, True)], flops, "forward_own", *pieces)
         return [own, *sends]
@@ -287,7 +291,7 @@
         flops = 2 * rows * cols * width // len(grads)
         total = some(backward_own, (width, cols), F32, flops, "backward_own", grads[0])
         flops = 2 * rows * cols * width // 2
-        send = some(backward_sent, (cols // 2 + width, width), BF16, flops, "backward_sent", total, *grads)
+        send = some(backward_sent, (cols // 2 + 2 * width, width), BF16, flops, "backward_sent", total, *grads)
         return send, some(backward_kept, (cols // 2, width), F32, flops, "backward_kept", total, *grads[1:])
 
 
@@ -321,7 +325,8 @@
         sums = jax.ops.segment_sum(terms, at, self.col_count + 1)[: self.col_count]
         keep, send = jnp.split(sums.reshape(-1, given.shape[-1]), 2)
         wsum = pair_sums([grad[group:].astype(F32) for grad in grads])
-        return lax.optimization_barrier(jnp.concatenate([send, wsum]).astype(BF16)), keep
+        high = lax.reduce_precision(wsum, 8, 7)
+        return lax.optimization_barrier(jnp.concatenate([send, high, wsum - high]).astype(BF16)), keep
 
 
 def body(features, weight, tiles, tile_slots, tile_counts, cotangent):
@@ -358,14 +363,16 @@
             left = lax.optimization_barrier((left.astype(F32) + right.astype(F32)).astype(BF16))
         right = swap(left, "col", sum_mask(bit, near))
 
+    (first,) = kernel_call(
+        project, [((group, width), F32, True)], 2 * group * width * width, "project", [VM] * 2
+    )(left, weight)
     grads, hidden = kernel_call(
         functools.partial(middle, near, share),
         [((group + width, width), BF16, True), ((share, width), BF16, True)],
-        8 * group * width * width,
+        6 * group * width * width,
         "middle",
-        [VM] * (3 + len(cots)),
-        [pltpu.VMEM((group, 2 * width), BF16)],
-    )(left, right, weight, *cots)
+        [VM] * (4 + len(cots)),
+    )(first, left, right, weight, *cots)
     (hidden,) = kernel_call(emit, [((share, width), BF16, False)], 0, "emit", [VM])(hidden)
     send, keep = block.backward([grads, *[swap(grads, "col", mask) for mask in PARTNERS[near]]])
 
@@ -375,7 +382,8 @@
         if bit == row_bits - 1:
             break
         keep = keep + other[:kept].astype(F32)
-        wsum = send[kept:].astype(F32) + other[kept:].astype(F32)
+        terms = [jnp.sum(part[kept:].astype(F32).reshape(-1, width, width), axis=0) for part in (send, other)]
+        wsum = pair_sums(terms)
         kept //= 2
         send = lax.optimization_barrier(jnp.concatenate([keep[kept:].astype(BF16), wsum.astype(BF16)]))
         keep = keep[:kept]

time: 44 us -> 43.9 us (level)
  waiting for transfers between devices: 17.4 us -> 16.9 us
    ppermute x13, waiting for transfers between devices: 17.4 us -> 16.9 us  [swap(): return lax.ppermute(x, axis, [(i, i ^ mask) for i in range(n)])]
  transfers between devices with their start and end apart: 13 -> 13, of which waited for: 10 -> 10; matrix products, arithmetic and copies ran while one was open for 0% -> 0% of each run, Pallas kernels for 9% -> 10%
where the time goes in v4:
time: 43.9 us; the launch traced here: 43.7 us
  starting transfers between devices  18.7 us (43%)
  waiting for transfers between devices  16.9 us (38%)
  Pallas kernels  6.4 us (15%)
  between operations  1.45 us (3%)
    ppermute x13, starting transfers between devices, swap(): return lax.ppermute(x, axis, [(i, i ^ mask) for i in range(n)])  18.7 us
    ppermute x13, waiting for transfers between devices, swap(): return lax.ppermute(x, axis, [(i, i ^ mask) for i in range(n)])  16.9 us
    pallas_call x3, Pallas kernels, some(): kernel_call(kernel, outs, flops, name, [VM] * (1 + len(given)))  1.58 us
    pallas_call x1, Pallas kernels, __init__(): kernel_call(functools.partial(densify, row_of, col_of, DENSIFY_PARTS), [(...  1.36 us
    pallas_call x3, Pallas kernels, some(): kernel_call(kernel, [(shape, dtype, True)], flops, name, [VM] * (1 + len(...  1.3 us
  transfers between devices with their start and end apart: 13, of which 10 were waited for; matrix products, arithmetic and copies ran while one was open for 0% of the time, Pallas kernels for 10%

profile of v4, /device:TPU:0, one launch (start us, length us, event | category | flops | bytes accessed | tf_op | source)
XLA Modules:
  0.0 43.7 jit_solution(7277757268490256222)
XLA Ops:
  0.6 0.0 copy-start.1
  0.6 3.0 %collective-permute-start = (bf16[256,128]{1,0:T(8,128)(2,1)}, bf16[256,128]{1,0:T(8,128)(2,1)S(1)}, u32[]{:S(2)}, u32[]{:S(2)}) collective-permute-start(bf16[256,128]{1,0:T(8,128)(2,1)} %refs_0_.3), channel_id=1, source_target_pairs={{0,16},{8,24},{16,0},{24,8},{1,17},{9,25},{17,1},{25,9},{2,18},{10... | collective-permute-start | bytes 196616 | tf_op jit(solution)/shard_map/ppermute | solution.py:229
  3.7 0.0 collective-permute-start.1
  4.3 1.4 %densify.1.dense_ref = bf16[2176,1024]{1,0:T(8,128)(2,1)S(1)} custom-call(bf16[1,1,44,128,128]{4,3,2,1,0:T(8,128)(2,1)} %tiles_ref.1, s32[1,1,44]{2,1,0:T(1,128)} %slots_ref.1, s32[1,1]{1,0:T(1,128)S(6)} %copy.9.count_ref), custom_call_target="tpu_custom_call" | custom-call | bytes 4456448 | tf_op jit(solution)/shard_map/densify/pallas_call | solution.py:234
  5.7 0.0 copy-start.2
  5.7 0.4 collective-permute-done.refs_1_
  6.1 0.2 collective-permute-start.2
  6.4 0.0 collective-permute-done.1.refs_2_
  6.4 0.0 copy-done.1
  6.4 0.8 %forward_early.1.total_ref = f32[1536,128]{1,0:T(8,128)S(1)} custom-call(bf16[2176,1024]{1,0:T(8,128)(2,1)S(1)} %densify.1.dense_ref, bf16[256,128]{1,0:T(8,128)(2,1)S(1)} %copy-done.1, bf16[256,128]{1,0:T(8,128)(2,1)S(1)} %collective-permute-done.refs_1_, bf16[256,128]{1,0:T(8,128)(2,1)S(1)} %collective-permute-done.1.refs_2_), custom_call_target="tpu_custom_call" | custom-call | flops 301989888 | bytes 786432 | tf_op jit(solution)/shard_map/forward_early/pallas_call | solution.py:261
  7.2 0.0 copy-start
  7.2 0.2 collective-permute-done.2.refs_3_.piece_ref
  7.4 0.4 forward_sent.1
  7.8 2.1 %collective-permute-start.3 = (bf16[512,128]{1,0:T(8,128)(2,1)S(1)}, bf16[512,128]{1,0:T(8,128)(2,1)S(1)}, u32[]{:S(2)}, u32[]{:S(2)}) collective-permute-start(bf16[512,128]{1,0:T(8,128)(2,1)S(1)} %get-tuple-element.24), channel_id=1, source_target_pairs={{0,2},{1,3},{2,0},{3,1},{4,6},{5,7},{6,4},{7,5},{8,10},{9,11},{10,... | collective-permute-start | bytes 393224 | tf_op jit(solution)/shard_map/ppermute | solution.py:229
  9.9 1.5 %collective-permute-start.4 = (bf16[512,128]{1,0:T(8,128)(2,1)S(1)}, bf16[512,128]{1,0:T(8,128)(2,1)S(1)}, u32[]{:S(2)}, u32[]{:S(2)}) collective-permute-start(bf16[512,128]{1,0:T(8,128)(2,1)S(1)} %get-tuple-element.25), channel_id=1, source_target_pairs={{0,1},{1,0},{2,3},{3,2},{4,5},{5,4},{6,7},{7,6},{8,9},{9,8},{10,11... | collective-permute-start | bytes 393224 | tf_op jit(solution)/shard_map/ppermute | solution.py:229
  11.4 0.0 collective-permute-start.5
  11.4 0.0 copy-done.2
  11.4 4.0 %collective-permute-start.6 = (bf16[256,128]{1,0:T(8,128)(2,1)S(1)}, bf16[256,128]{1,0:T(8,128)(2,1)S(1)}, u32[]{:S(2)}, u32[]{:S(2)}) collective-permute-start(bf16[256,128]{1,0:T(8,128)(2,1)S(1)} %copy-done.2), channel_id=1, source_target_pairs={{0,6},{1,7},{2,4},{3,5},{4,2},{5,3},{6,0},{7,1},{8,14},{9,15},{10,... | collective-permute-start | bytes 196616 | tf_op jit(solution)/shard_map/ppermute | solution.py:229
  15.4 0.4 forward_own.1
  15.9 0.0 collective-permute-done.3
  15.9 2.1 %collective-permute-done.4 = bf16[512,128]{1,0:T(8,128)(2,1)S(1)} collective-permute-done((bf16[512,128]{1,0:T(8,128)(2,1)S(1)}, bf16[512,128]{1,0:T(8,128)(2,1)S(1)}, u32[]{:S(2)}, u32[]{:S(2)}) %collective-permute-start.4) | collective-permute-done | bytes 131104 | tf_op jit(solution)/shard_map/ppermute | solution.py:229
  18.0 0.0 collective-permute-done.5
  18.0 0.1 add_convert_fusion.left_ref
  18.1 2.1 %collective-permute-done.6.refs_1_ = bf16[256,128]{1,0:T(8,128)(2,1)S(1)} collective-permute-done((bf16[256,128]{1,0:T(8,128)(2,1)S(1)}, bf16[256,128]{1,0:T(8,128)(2,1)S(1)}, u32[]{:S(2)}, u32[]{:S(2)}) %collective-permute-start.6) | collective-permute-done | bytes 65568 | tf_op jit(solution)/shard_map/ppermute | solution.py:229
  20.2 2.6 %collective-permute-start.7 = (bf16[512,128]{1,0:T(8,128)(2,1)S(1)}, bf16[512,128]{1,0:T(8,128)(2,1)S(1)}, u32[]{:S(2)}, u32[]{:S(2)}) collective-permute-start(bf16[512,128]{1,0:T(8,128)(2,1)S(1)} %add_convert_fusion.left_ref), channel_id=1, source_target_pairs={{0,6},{1,7},{2,4},{3,5},{4,2},{5,3},{6,0},{7,1},{8,14},{9,15},{10,... | collective-permute-start | bytes 393224 | tf_op jit(solution)/shard_map/ppermute | solution.py:229
  22.8 0.0 copy-done
  22.8 0.2 project.1.first_ref
  22.9 4.1 %collective-permute-done.7.right_ref = bf16[512,128]{1,0:T(8,128)(2,1)S(1)} collective-permute-done((bf16[512,128]{1,0:T(8,128)(2,1)S(1)}, bf16[512,128]{1,0:T(8,128)(2,1)S(1)}, u32[]{:S(2)}, u32[]{:S(2)}) %collective-permute-start.7) | collective-permute-done | bytes 131104 | tf_op jit(solution)/shard_map/ppermute | solution.py:229
  27.0 0.6 %middle.1 = (bf16[640,128]{1,0:T(8,128)(2,1)S(1)}, bf16[256,128]{1,0:T(8,128)(2,1)S(1)}) custom-call(f32[512,128]{1,0:T(8,128)S(1)} %project.1.first_ref, bf16[512,128]{1,0:T(8,128)(2,1)S(1)} %add_convert_fusion.left_ref, bf16[512,128]{1,0:T(8,128)(2,1)S(1)} %collective-permute-done.7.right_ref, bf16[128,128]{1,0:T(8,128)(2,1)S(1)} %copy-done, ...), custom_call_target="tpu_custom_call" | custom-call | flops 50331648 | bytes 229376 | tf_op jit(solution)/shard_map/middle/pallas_call | solution.py:369
  27.6 0.3 collective-permute-start.10
  27.9 2.0 %collective-permute-start.9 = (bf16[640,128]{1,0:T(8,128)(2,1)S(1)}, bf16[640,128]{1,0:T(8,128)(2,1)S(1)}, u32[]{:S(2)}, u32[]{:S(2)}) collective-permute-start(bf16[640,128]{1,0:T(8,128)(2,1)S(1)} %get-tuple-element.32.grad_ref.refs_0_), channel_id=1, source_target_pairs={{0,1},{1,0},{2,3},{3,2},{4,5},{5,4},{6,7},{7,6},{8,9},{9,8},{10,11... | collective-permute-start | bytes 491528 | tf_op jit(solution)/shard_map/ppermute | solution.py:229
  29.9 1.2 %collective-permute-start.8 = (bf16[640,128]{1,0:T(8,128)(2,1)S(1)}, bf16[640,128]{1,0:T(8,128)(2,1)S(1)}, u32[]{:S(2)}, u32[]{:S(2)}) collective-permute-start(bf16[640,128]{1,0:T(8,128)(2,1)S(1)} %get-tuple-element.32.grad_ref.refs_0_), channel_id=1, source_target_pairs={{0,2},{1,3},{2,0},{3,1},{4,6},{5,7},{6,4},{7,5},{8,10},{9,11},{10,... | collective-permute-start | bytes 491528 | tf_op jit(solution)/shard_map/ppermute | solution.py:229
  31.2 0.3 backward_own.1.total_ref
  31.5 2.7 %collective-permute-done.10.refs_2_.refs_3_ = bf16[640,128]{1,0:T(8,128)(2,1)S(1)} collective-permute-done((bf16[640,128]{1,0:T(8,128)(2,1)S(1)}, bf16[640,128]{1,0:T(8,128)(2,1)S(1)}, u32[]{:S(2)}, u32[]{:S(2)}) %collective-permute-start.10) | collective-permute-done | bytes 163872 | tf_op jit(solution)/shard_map/ppermute | solution.py:229
  34.2 0.8 %collective-permute-done.9.refs_1_.refs_2_ = bf16[640,128]{1,0:T(8,128)(2,1)S(1)} collective-permute-done((bf16[640,128]{1,0:T(8,128)(2,1)S(1)}, bf16[640,128]{1,0:T(8,128)(2,1)S(1)}, u32[]{:S(2)}, u32[]{:S(2)}) %collective-permute-start.9) | collective-permute-done | bytes 163872 | tf_op jit(solution)/shard_map/ppermute | solution.py:229
  35.0 0.9 %collective-permute-done.8.refs_0_.refs_1_ = bf16[640,128]{1,0:T(8,128)(2,1)S(1)} collective-permute-done((bf16[640,128]{1,0:T(8,128)(2,1)S(1)}, bf16[640,128]{1,0:T(8,128)(2,1)S(1)}, u32[]{:S(2)}, u32[]{:S(2)}) %collective-permute-start.8) | collective-permute-done | bytes 163872 | tf_op jit(solution)/shard_map/ppermute | solution.py:229
  35.9 0.5 %backward_sent.1 = bf16[768,128]{1,0:T(8,128)(2,1)S(1)} custom-call(bf16[2176,1024]{1,0:T(8,128)(2,1)S(1)} %densify.1.dense_ref, f32[128,1024]{1,0:T(8,128)S(1)} %backward_own.1.total_ref, bf16[640,128]{1,0:T(8,128)(2,1)S(1)} %get-tuple-element.32.grad_ref.refs_0_, bf16[640,128]{1,0:T(8,128)(2,1)S(1)} %collective-permute-done.8.refs_0_.refs_1_, ...), custom_call_target="tpu_custom_call" | custom-call | flops 268435456 | bytes 196608 | tf_op jit(solution)/shard_map/backward_sent/pallas_call | solution.py:288
  36.4 0.1 collective-permute-start.11
  36.5 0.5 %backward_kept.1 = f32[512,128]{1,0:T(8,128)S(1)} custom-call(bf16[2176,1024]{1,0:T(8,128)(2,1)S(1)} %densify.1.dense_ref, f32[128,1024]{1,0:T(8,128)S(1)} %backward_own.1.total_ref, bf16[640,128]{1,0:T(8,128)(2,1)S(1)} %collective-permute-done.8.refs_0_.refs_1_, bf16[640,128]{1,0:T(8,128)(2,1)S(1)} %collective-permute-done.9.refs_1_.refs_2_, ...), custom_call_target="tpu_custom_call" | custom-call | flops 268435456 | bytes 262144 | tf_op jit(solution)/shard_map/backward_kept/pallas_call | solution.py:288
  37.0 0.9 %collective-permute-done.11 = bf16[768,128]{1,0:T(8,128)(2,1)S(1)} collective-permute-done((bf16[768,128]{1,0:T(8,128)(2,1)S(1)}, bf16[768,128]{1,0:T(8,128)(2,1)S(1)}, u32[]{:S(2)}, u32[]{:S(2)}) %collective-permute-start.11) | collective-permute-done | bytes 196640 | tf_op jit(solution)/shard_map/ppermute | solution.py:229
  38.0 1.6 %collective-permute-start.12 = (bf16[384,128]{1,0:T(8,128)(2,1)S(1)}, bf16[384,128]{1,0:T(8,128)(2,1)S(1)}, u32[]{:S(2)}, u32[]{:S(2)}) collective-permute-start(bf16[384,128]{1,0:T(8,128)(2,1)S(1)} %pad_maximum_fusion.own_ref), channel_id=1, source_target_pairs={{0,16},{8,24},{16,0},{24,8},{1,17},{9,25},{17,1},{25,9},{2,18},{10... | collective-permute-start | bytes 294920 | tf_op jit(solution)/shard_map/ppermute | solution.py:229
  39.6 0.6 %emit.1 = bf16[256,128]{1,0:T(8,128)(2,1)} custom-call(bf16[256,128]{1,0:T(8,128)(2,1)S(1)} %get-tuple-element.31.given_ref), custom_call_target="tpu_custom_call" | custom-call | bytes 65536 | tf_op jit(solution)/shard_map/emit/pallas_call | solution.py:376
  40.2 2.7 %collective-permute-done.12.other_ref = bf16[384,128]{1,0:T(8,128)(2,1)S(1)} collective-permute-done((bf16[384,128]{1,0:T(8,128)(2,1)S(1)}, bf16[384,128]{1,0:T(8,128)(2,1)S(1)}, u32[]{:S(2)}, u32[]{:S(2)}) %collective-permute-start.12) | collective-permute-done | bytes 98336 | tf_op jit(solution)/shard_map/ppermute | solution.py:229
  42.9 0.8 %finish.1 = (bf16[256,128]{1,0:T(8,128)(2,1)}, f32[128,128]{1,0:T(8,128)}) custom-call(f32[256,128]{1,0:T(8,128)S(1)} %slice.22.keep_ref, bf16[384,128]{1,0:T(8,128)(2,1)S(1)} %pad_maximum_fusion.own_ref, bf16[384,128]{1,0:T(8,128)(2,1)S(1)} %collective-permute-done.12.other_ref, bf16[128,128]{1,0:T(8,128)(2,1)S(1)} %copy-done), custom_call_target="tpu_custom_call" | custom-call | flops 8388608 | bytes 131072 | tf_op jit(solution)/shard_map/finish/pallas_call | solution.py:391
  (9 shorter events, 0.1 us)
Async XLA Ops:
  0.6 5.7 %copy-start.1 = (bf16[256,128]{1,0:T(8,128)(2,1)S(1)}, bf16[256,128]{1,0:T(8,128)(2,1)}, u32[]{:S(2)}) copy-start(bf16[256,128]{1,0:T(8,128)(2,1)} %refs_0_.3) | copy-start | bytes 196612
  0.6 5.5 %collective-permute-start = (bf16[256,128]{1,0:T(8,128)(2,1)}, bf16[256,128]{1,0:T(8,128)(2,1)S(1)}, u32[]{:S(2)}, u32[]{:S(2)}) collective-permute-start(bf16[256,128]{1,0:T(8,128)(2,1)} %refs_0_.3), channel_id=1, source_target_pairs={{0,16},{8,24},{16,0},{24,8},{1,17},{9,25},{17,1},{25,9},{2,18},{10... | collective-permute-start | bytes 196616 | tf_op jit(solution)/shard_map/ppermute | solution.py:229
  3.7 2.7 %collective-permute-start.1 = (bf16[256,128]{1,0:T(8,128)(2,1)}, bf16[256,128]{1,0:T(8,128)(2,1)S(1)}, u32[]{:S(2)}, u32[]{:S(2)}) collective-permute-start(bf16[256,128]{1,0:T(8,128)(2,1)} %refs_0_.3), channel_id=1, source_target_pairs={{0,8},{8,0},{16,24},{24,16},{1,9},{9,1},{17,25},{25,17},{2,10},{10... | collective-permute-start | bytes 196616 | tf_op jit(solution)/shard_map/ppermute | solution.py:229
  5.7 5.7 %copy-start.2 = (bf16[256,128]{1,0:T(8,128)(2,1)S(1)}, bf16[256,128]{1,0:T(8,128)(2,1)}, u32[]{:S(2)}) copy-start(bf16[256,128]{1,0:T(8,128)(2,1)} %refs_0_.4) | copy-start | bytes 196612
  6.1 1.3 %collective-permute-start.2 = (bf16[256,128]{1,0:T(8,128)(2,1)S(1)}, bf16[256,128]{1,0:T(8,128)(2,1)S(1)}, u32[]{:S(2)}, u32[]{:S(2)}) collective-permute-start(bf16[256,128]{1,0:T(8,128)(2,1)S(1)} %collective-permute-done.refs_1_), channel_id=1, source_target_pairs={{0,8},{8,0},{16,24},{24,16},{1,9},{9,1},{17,25},{25,17},{2,10},{10... | collective-permute-start | bytes 196616 | tf_op jit(solution)/shard_map/ppermute | solution.py:229
  7.2 15.6 %copy-start = (bf16[128,128]{1,0:T(8,128)(2,1)S(1)}, bf16[128,128]{1,0:T(8,128)(2,1)}, u32[]{:S(2)}) copy-start(bf16[128,128]{1,0:T(8,128)(2,1)} %weight_ref.5) | copy-start | bytes 98308
  7.8 8.1 %collective-permute-start.3 = (bf16[512,128]{1,0:T(8,128)(2,1)S(1)}, bf16[512,128]{1,0:T(8,128)(2,1)S(1)}, u32[]{:S(2)}, u32[]{:S(2)}) collective-permute-start(bf16[512,128]{1,0:T(8,128)(2,1)S(1)} %get-tuple-element.24), channel_id=1, source_target_pairs={{0,2},{1,3},{2,0},{3,1},{4,6},{5,7},{6,4},{7,5},{8,10},{9,11},{10,... | collective-permute-start | bytes 393224 | tf_op jit(solution)/shard_map/ppermute | solution.py:229
  9.9 8.1 %collective-permute-start.4 = (bf16[512,128]{1,0:T(8,128)(2,1)S(1)}, bf16[512,128]{1,0:T(8,128)(2,1)S(1)}, u32[]{:S(2)}, u32[]{:S(2)}) collective-permute-start(bf16[512,128]{1,0:T(8,128)(2,1)S(1)} %get-tuple-element.25), channel_id=1, source_target_pairs={{0,1},{1,0},{2,3},{3,2},{4,5},{5,4},{6,7},{7,6},{8,9},{9,8},{10,11... | collective-permute-start | bytes 393224 | tf_op jit(solution)/shard_map/ppermute | solution.py:229
  11.4 6.6 %collective-permute-start.5 = (bf16[512,128]{1,0:T(8,128)(2,1)S(1)}, bf16[512,128]{1,0:T(8,128)(2,1)S(1)}, u32[]{:S(2)}, u32[]{:S(2)}) collective-permute-start(bf16[512,128]{1,0:T(8,128)(2,1)S(1)} %get-tuple-element.26), channel_id=1, source_target_pairs={{0,3},{1,2},{2,1},{3,0},{4,7},{5,6},{6,5},{7,4},{8,11},{9,10},{10,... | collective-permute-start | bytes 393224 | tf_op jit(solution)/shard_map/ppermute | solution.py:229
  11.4 8.7 %collective-permute-start.6 = (bf16[256,128]{1,0:T(8,128)(2,1)S(1)}, bf16[256,128]{1,0:T(8,128)(2,1)S(1)}, u32[]{:S(2)}, u32[]{:S(2)}) collective-permute-start(bf16[256,128]{1,0:T(8,128)(2,1)S(1)} %copy-done.2), channel_id=1, source_target_pairs={{0,6},{1,7},{2,4},{3,5},{4,2},{5,3},{6,0},{7,1},{8,14},{9,15},{10,... | collective-permute-start | bytes 196616 | tf_op jit(solution)/shard_map/ppermute | solution.py:229
  20.2 6.9 %collective-permute-start.7 = (bf16[512,128]{1,0:T(8,128)(2,1)S(1)}, bf16[512,128]{1,0:T(8,128)(2,1)S(1)}, u32[]{:S(2)}, u32[]{:S(2)}) collective-permute-start(bf16[512,128]{1,0:T(8,128)(2,1)S(1)} %add_convert_fusion.left_ref), channel_id=1, source_target_pairs={{0,6},{1,7},{2,4},{3,5},{4,2},{5,3},{6,0},{7,1},{8,14},{9,15},{10,... | collective-permute-start | bytes 393224 | tf_op jit(solution)/shard_map/ppermute | solution.py:229
  27.6 6.6 %collective-permute-start.10 = (bf16[640,128]{1,0:T(8,128)(2,1)S(1)}, bf16[640,128]{1,0:T(8,128)(2,1)S(1)}, u32[]{:S(2)}, u32[]{:S(2)}) collective-permute-start(bf16[640,128]{1,0:T(8,128)(2,1)S(1)} %get-tuple-element.32.grad_ref.refs_0_), channel_id=1, source_target_pairs={{0,3},{1,2},{2,1},{3,0},{4,7},{5,6},{6,5},{7,4},{8,11},{9,10},{10,... | collective-permute-start | bytes 491528 | tf_op jit(solution)/shard_map/ppermute | solution.py:229
  27.9 7.1 %collective-permute-start.9 = (bf16[640,128]{1,0:T(8,128)(2,1)S(1)}, bf16[640,128]{1,0:T(8,128)(2,1)S(1)}, u32[]{:S(2)}, u32[]{:S(2)}) collective-permute-start(bf16[640,128]{1,0:T(8,128)(2,1)S(1)} %get-tuple-element.32.grad_ref.refs_0_), channel_id=1, source_target_pairs={{0,1},{1,0},{2,3},{3,2},{4,5},{5,4},{6,7},{7,6},{8,9},{9,8},{10,11... | collective-permute-start | bytes 491528 | tf_op jit(solution)/shard_map/ppermute | solution.py:229
  29.9 6.0 %collective-permute-start.8 = (bf16[640,128]{1,0:T(8,128)(2,1)S(1)}, bf16[640,128]{1,0:T(8,128)(2,1)S(1)}, u32[]{:S(2)}, u32[]{:S(2)}) collective-permute-start(bf16[640,128]{1,0:T(8,128)(2,1)S(1)} %get-tuple-element.32.grad_ref.refs_0_), channel_id=1, source_target_pairs={{0,2},{1,3},{2,0},{3,1},{4,6},{5,7},{6,4},{7,5},{8,10},{9,11},{10,... | collective-permute-start | bytes 491528 | tf_op jit(solution)/shard_map/ppermute | solution.py:229
  36.4 1.5 %collective-permute-start.11 = (bf16[768,128]{1,0:T(8,128)(2,1)S(1)}, bf16[768,128]{1,0:T(8,128)(2,1)S(1)}, u32[]{:S(2)}, u32[]{:S(2)}) collective-permute-start(bf16[768,128]{1,0:T(8,128)(2,1)S(1)} %backward_sent.1), channel_id=1, source_target_pairs={{0,8},{8,0},{16,24},{24,16},{1,9},{9,1},{17,25},{25,17},{2,10},{10... | collective-permute-start | bytes 589832 | tf_op jit(solution)/shard_map/ppermute | solution.py:229
  38.0 4.9 %collective-permute-start.12 = (bf16[384,128]{1,0:T(8,128)(2,1)S(1)}, bf16[384,128]{1,0:T(8,128)(2,1)S(1)}, u32[]{:S(2)}, u32[]{:S(2)}) collective-permute-start(bf16[384,128]{1,0:T(8,128)(2,1)S(1)} %pad_maximum_fusion.own_ref), channel_id=1, source_target_pairs={{0,16},{8,24},{16,0},{24,8},{1,17},{9,25},{17,1},{25,9},{2,18},{10... | collective-permute-start | bytes 294920 | tf_op jit(solution)/shard_map/ppermute | solution.py:229

commit v5 on v4

--- a/solution.py
+++ b/solution.py
@@ -215,6 +215,20 @@
     keep_ref[...] = (columns_of(dense_ref, grads, 1, columns) + total_ref[:, columns]).T
 
 
+def fold(width, keep_ref, own_ref, other_ref, send_ref, kept_ref):
+    whole = keep_ref.shape[0]
+    kept = whole // 2
+    send_ref[:kept, :] = (keep_ref[kept:, :] + other_ref[kept:whole, :].astype(F32)).astype(BF16)
+    terms = []
+    for ref in (own_ref, other_ref):
+        total = ref[whole : whole + width, :].astype(F32)
+        for start in range(whole + width, ref.shape[0], width):
+            total += ref[start : start + width, :].astype(F32)
+        terms.append(total)
+    send_ref[kept:, :] = (terms[0] + terms[1]).astype(BF16)
+    kept_ref[...] = keep_ref[:kept, :] + other_ref[:kept, :].astype(F32)
+
+
 def finish(scale, keep_ref, own_ref, other_ref, weight_ref, grad_ref, wgrad_ref):
     share = keep_ref.shape[0]
     grad_proj = (keep_ref[...] + other_ref[:share, :].astype(F32)).astype(BF16)
@@ -381,12 +395,14 @@
         other = swap(send, "row", 1 << bit)
         if bit == row_bits - 1:
             break
-        keep = keep + other[:kept].astype(F32)
-        terms = [jnp.sum(part[kept:].astype(F32).reshape(-1, width, width), axis=0) for part in (send, other)]
-        wsum = pair_sums(terms)
         kept //= 2
-        send = lax.optimization_barrier(jnp.concatenate([keep[kept:].astype(BF16), wsum.astype(BF16)]))
-        keep = keep[:kept]
+        send, keep = kernel_call(
+            functools.partial(fold, width),
+            [((kept + width, width), BF16, True), ((kept, width), F32, True)],
+            0,
+            "fold",
+            [VM] * 3,
+        )(keep, send, other)
 
     feature_grad, weight_grad = kernel_call(
         functools.partial(finish, 1.0 / math.sqrt(share * row_count * col_count)),

time: 43.9 us -> 43.8 us (level)
  no operation moved by 1% of the time
where the time goes in v5:
time: 43.8 us; the launch traced here: 43.6 us
  starting transfers between devices  18.7 us (43%)
  waiting for transfers between devices  17 us (39%)
  Pallas kernels  6.44 us (15%)
  between operations  1.4 us (3%)
    ppermute x13, starting transfers between devices, swap(): return lax.ppermute(x, axis, [(i, i ^ mask) for i in range(n)])  18.7 us
    ppermute x13, waiting for transfers between devices, swap(): return lax.ppermute(x, axis, [(i, i ^ mask) for i in range(n)])  17 us
    pallas_call x3, Pallas kernels, some(): kernel_call(kernel, outs, flops, name, [VM] * (1 + len(given)))  1.58 us
    pallas_call x1, Pallas kernels, __init__(): kernel_call(functools.partial(densify, row_of, col_of, DENSIFY_PARTS), [(...  1.36 us
    pallas_call x3, Pallas kernels, some(): kernel_call(kernel, [(shape, dtype, True)], flops, name, [VM] * (1 + len(...  1.3 us
  transfers between devices with their start and end apart: 13, of which 10 were waited for; matrix products, arithmetic and copies ran while one was open for 0% of the time, Pallas kernels for 10%

profile of v5, /device:TPU:0, one launch (start us, length us, event | category | flops | bytes accessed | tf_op | source)
XLA Modules:
  0.0 43.6 jit_solution(3931131040395361307)
XLA Ops:
  0.6 0.0 copy-start.1
  0.6 3.0 %collective-permute-start = (bf16[256,128]{1,0:T(8,128)(2,1)}, bf16[256,128]{1,0:T(8,128)(2,1)S(1)}, u32[]{:S(2)}, u32[]{:S(2)}) collective-permute-start(bf16[256,128]{1,0:T(8,128)(2,1)} %refs_0_.3), channel_id=1, source_target_pairs={{0,16},{8,24},{16,0},{24,8},{1,17},{9,25},{17,1},{25,9},{2,18},{10... | collective-permute-start | bytes 196616 | tf_op jit(solution)/shard_map/ppermute | solution.py:243
  3.7 0.0 collective-permute-start.1
  4.3 1.4 %densify.1.dense_ref = bf16[2176,1024]{1,0:T(8,128)(2,1)S(1)} custom-call(bf16[1,1,44,128,128]{4,3,2,1,0:T(8,128)(2,1)} %tiles_ref.1, s32[1,1,44]{2,1,0:T(1,128)} %slots_ref.1, s32[1,1]{1,0:T(1,128)S(6)} %copy.9.count_ref), custom_call_target="tpu_custom_call" | custom-call | bytes 4456448 | tf_op jit(solution)/shard_map/densify/pallas_call | solution.py:248
  5.7 0.0 copy-start.2
  5.7 0.4 collective-permute-done.refs_1_
  6.1 0.2 collective-permute-start.2
  6.3 0.0 collective-permute-done.1.refs_2_
  6.3 0.0 copy-done.1
  6.3 0.8 %forward_early.1.total_ref = f32[1536,128]{1,0:T(8,128)S(1)} custom-call(bf16[2176,1024]{1,0:T(8,128)(2,1)S(1)} %densify.1.dense_ref, bf16[256,128]{1,0:T(8,128)(2,1)S(1)} %copy-done.1, bf16[256,128]{1,0:T(8,128)(2,1)S(1)} %collective-permute-done.refs_1_, bf16[256,128]{1,0:T(8,128)(2,1)S(1)} %collective-permute-done.1.refs_2_), custom_call_target="tpu_custom_call" | custom-call | flops 301989888 | bytes 786432 | tf_op jit(solution)/shard_map/forward_early/pallas_call | solution.py:275
  7.1 0.0 copy-start
  7.1 0.3 collective-permute-done.2.refs_3_.piece_ref
  7.4 0.4 forward_sent.1
  7.8 2.1 %collective-permute-start.3 = (bf16[512,128]{1,0:T(8,128)(2,1)S(1)}, bf16[512,128]{1,0:T(8,128)(2,1)S(1)}, u32[]{:S(2)}, u32[]{:S(2)}) collective-permute-start(bf16[512,128]{1,0:T(8,128)(2,1)S(1)} %get-tuple-element.26), channel_id=1, source_target_pairs={{0,2},{1,3},{2,0},{3,1},{4,6},{5,7},{6,4},{7,5},{8,10},{9,11},{10,... | collective-permute-start | bytes 393224 | tf_op jit(solution)/shard_map/ppermute | solution.py:243
  9.9 1.5 %collective-permute-start.4 = (bf16[512,128]{1,0:T(8,128)(2,1)S(1)}, bf16[512,128]{1,0:T(8,128)(2,1)S(1)}, u32[]{:S(2)}, u32[]{:S(2)}) collective-permute-start(bf16[512,128]{1,0:T(8,128)(2,1)S(1)} %get-tuple-element.27), channel_id=1, source_target_pairs={{0,1},{1,0},{2,3},{3,2},{4,5},{5,4},{6,7},{7,6},{8,9},{9,8},{10,11... | collective-permute-start | bytes 393224 | tf_op jit(solution)/shard_map/ppermute | solution.py:243
  11.4 0.0 collective-permute-start.5
  11.4 0.0 copy-done.2
  11.4 4.0 %collective-permute-start.6 = (bf16[256,128]{1,0:T(8,128)(2,1)S(1)}, bf16[256,128]{1,0:T(8,128)(2,1)S(1)}, u32[]{:S(2)}, u32[]{:S(2)}) collective-permute-start(bf16[256,128]{1,0:T(8,128)(2,1)S(1)} %copy-done.2), channel_id=1, source_target_pairs={{0,6},{1,7},{2,4},{3,5},{4,2},{5,3},{6,0},{7,1},{8,14},{9,15},{10,... | collective-permute-start | bytes 196616 | tf_op jit(solution)/shard_map/ppermute | solution.py:243
  15.4 0.4 forward_own.1
  15.9 0.0 collective-permute-done.3
  15.9 2.1 %collective-permute-done.4 = bf16[512,128]{1,0:T(8,128)(2,1)S(1)} collective-permute-done((bf16[512,128]{1,0:T(8,128)(2,1)S(1)}, bf16[512,128]{1,0:T(8,128)(2,1)S(1)}, u32[]{:S(2)}, u32[]{:S(2)}) %collective-permute-start.4) | collective-permute-done | bytes 131104 | tf_op jit(solution)/shard_map/ppermute | solution.py:243
  18.0 0.0 collective-permute-done.5
  18.0 0.1 add_convert_fusion.left_ref
  18.1 2.1 %collective-permute-done.6.refs_1_ = bf16[256,128]{1,0:T(8,128)(2,1)S(1)} collective-permute-done((bf16[256,128]{1,0:T(8,128)(2,1)S(1)}, bf16[256,128]{1,0:T(8,128)(2,1)S(1)}, u32[]{:S(2)}, u32[]{:S(2)}) %collective-permute-start.6) | collective-permute-done | bytes 65568 | tf_op jit(solution)/shard_map/ppermute | solution.py:243
  20.2 2.6 %collective-permute-start.7 = (bf16[512,128]{1,0:T(8,128)(2,1)S(1)}, bf16[512,128]{1,0:T(8,128)(2,1)S(1)}, u32[]{:S(2)}, u32[]{:S(2)}) collective-permute-start(bf16[512,128]{1,0:T(8,128)(2,1)S(1)} %add_convert_fusion.left_ref), channel_id=1, source_target_pairs={{0,6},{1,7},{2,4},{3,5},{4,2},{5,3},{6,0},{7,1},{8,14},{9,15},{10,... | collective-permute-start | bytes 393224 | tf_op jit(solution)/shard_map/ppermute | solution.py:243
  22.8 0.0 copy-done
  22.8 0.2 project.1.first_ref
  22.9 4.1 %collective-permute-done.7.right_ref = bf16[512,128]{1,0:T(8,128)(2,1)S(1)} collective-permute-done((bf16[512,128]{1,0:T(8,128)(2,1)S(1)}, bf16[512,128]{1,0:T(8,128)(2,1)S(1)}, u32[]{:S(2)}, u32[]{:S(2)}) %collective-permute-start.7) | collective-permute-done | bytes 131104 | tf_op jit(solution)/shard_map/ppermute | solution.py:243
  27.0 0.6 %middle.1 = (bf16[640,128]{1,0:T(8,128)(2,1)S(1)}, bf16[256,128]{1,0:T(8,128)(2,1)S(1)}) custom-call(f32[512,128]{1,0:T(8,128)S(1)} %project.1.first_ref, bf16[512,128]{1,0:T(8,128)(2,1)S(1)} %add_convert_fusion.left_ref, bf16[512,128]{1,0:T(8,128)(2,1)S(1)} %collective-permute-done.7.right_ref, bf16[128,128]{1,0:T(8,128)(2,1)S(1)} %copy-done, ...), custom_call_target="tpu_custom_call" | custom-call | flops 50331648 | bytes 229376 | tf_op jit(solution)/shard_map/middle/pallas_call | solution.py:383
  27.6 0.3 collective-permute-start.10
  27.9 2.0 %collective-permute-start.9 = (bf16[640,128]{1,0:T(8,128)(2,1)S(1)}, bf16[640,128]{1,0:T(8,128)(2,1)S(1)}, u32[]{:S(2)}, u32[]{:S(2)}) collective-permute-start(bf16[640,128]{1,0:T(8,128)(2,1)S(1)} %get-tuple-element.34.grad_ref.refs_0_), channel_id=1, source_target_pairs={{0,1},{1,0},{2,3},{3,2},{4,5},{5,4},{6,7},{7,6},{8,9},{9,8},{10,11... | collective-permute-start | bytes 491528 | tf_op jit(solution)/shard_map/ppermute | solution.py:243
  29.9 1.2 %collective-permute-start.8 = (bf16[640,128]{1,0:T(8,128)(2,1)S(1)}, bf16[640,128]{1,0:T(8,128)(2,1)S(1)}, u32[]{:S(2)}, u32[]{:S(2)}) collective-permute-start(bf16[640,128]{1,0:T(8,128)(2,1)S(1)} %get-tuple-element.34.grad_ref.refs_0_), channel_id=1, source_target_pairs={{0,2},{1,3},{2,0},{3,1},{4,6},{5,7},{6,4},{7,5},{8,10},{9,11},{10,... | collective-permute-start | bytes 491528 | tf_op jit(solution)/shard_map/ppermute | solution.py:243
  31.2 0.3 backward_own.1.total_ref
  31.5 2.7 %collective-permute-done.10.refs_2_.refs_3_ = bf16[640,128]{1,0:T(8,128)(2,1)S(1)} collective-permute-done((bf16[640,128]{1,0:T(8,128)(2,1)S(1)}, bf16[640,128]{1,0:T(8,128)(2,1)S(1)}, u32[]{:S(2)}, u32[]{:S(2)}) %collective-permute-start.10) | collective-permute-done | bytes 163872 | tf_op jit(solution)/shard_map/ppermute | solution.py:243
  34.2 0.8 %collective-permute-done.9.refs_1_.refs_2_ = bf16[640,128]{1,0:T(8,128)(2,1)S(1)} collective-permute-done((bf16[640,128]{1,0:T(8,128)(2,1)S(1)}, bf16[640,128]{1,0:T(8,128)(2,1)S(1)}, u32[]{:S(2)}, u32[]{:S(2)}) %collective-permute-start.9) | collective-permute-done | bytes 163872 | tf_op jit(solution)/shard_map/ppermute | solution.py:243
  35.0 0.9 %collective-permute-done.8.refs_0_.refs_1_ = bf16[640,128]{1,0:T(8,128)(2,1)S(1)} collective-permute-done((bf16[640,128]{1,0:T(8,128)(2,1)S(1)}, bf16[640,128]{1,0:T(8,128)(2,1)S(1)}, u32[]{:S(2)}, u32[]{:S(2)}) %collective-permute-start.8) | collective-permute-done | bytes 163872 | tf_op jit(solution)/shard_map/ppermute | solution.py:243
  35.9 0.5 %backward_sent.1.own_ref = bf16[768,128]{1,0:T(8,128)(2,1)S(1)} custom-call(bf16[2176,1024]{1,0:T(8,128)(2,1)S(1)} %densify.1.dense_ref, f32[128,1024]{1,0:T(8,128)S(1)} %backward_own.1.total_ref, bf16[640,128]{1,0:T(8,128)(2,1)S(1)} %get-tuple-element.34.grad_ref.refs_0_, bf16[640,128]{1,0:T(8,128)(2,1)S(1)} %collective-permute-done.8.refs_0_.refs_1_, ...), custom_call_target="tpu_custom_call" | custom-call | flops 268435456 | bytes 196608 | tf_op jit(solution)/shard_map/backward_sent/pallas_call | solution.py:302
  36.4 0.1 collective-permute-start.11
  36.4 0.5 %backward_kept.1.keep_ref = f32[512,128]{1,0:T(8,128)S(1)} custom-call(bf16[2176,1024]{1,0:T(8,128)(2,1)S(1)} %densify.1.dense_ref, f32[128,1024]{1,0:T(8,128)S(1)} %backward_own.1.total_ref, bf16[640,128]{1,0:T(8,128)(2,1)S(1)} %collective-permute-done.8.refs_0_.refs_1_, bf16[640,128]{1,0:T(8,128)(2,1)S(1)} %collective-permute-done.9.refs_1_.refs_2_, ...), custom_call_target="tpu_custom_call" | custom-call | flops 268435456 | bytes 262144 | tf_op jit(solution)/shard_map/backward_kept/pallas_call | solution.py:302
  36.9 0.9 %collective-permute-done.11.other_ref = bf16[768,128]{1,0:T(8,128)(2,1)S(1)} collective-permute-done((bf16[768,128]{1,0:T(8,128)(2,1)S(1)}, bf16[768,128]{1,0:T(8,128)(2,1)S(1)}, u32[]{:S(2)}, u32[]{:S(2)}) %collective-permute-start.11) | collective-permute-done | bytes 196640 | tf_op jit(solution)/shard_map/ppermute | solution.py:243
  37.9 1.6 %collective-permute-start.12 = (bf16[384,128]{1,0:T(8,128)(2,1)S(1)}, bf16[384,128]{1,0:T(8,128)(2,1)S(1)}, u32[]{:S(2)}, u32[]{:S(2)}) collective-permute-start(bf16[384,128]{1,0:T(8,128)(2,1)S(1)} %get-tuple-element.36.own_ref), channel_id=1, source_target_pairs={{0,16},{8,24},{16,0},{24,8},{1,17},{9,25},{17,1},{25,9},{2,18},{10... | collective-permute-start | bytes 294920 | tf_op jit(solution)/shard_map/ppermute | solution.py:243
  39.5 0.6 %emit.1 = bf16[256,128]{1,0:T(8,128)(2,1)} custom-call(bf16[256,128]{1,0:T(8,128)(2,1)S(1)} %get-tuple-element.33.given_ref), custom_call_target="tpu_custom_call" | custom-call | bytes 65536 | tf_op jit(solution)/shard_map/emit/pallas_call | solution.py:390
  40.1 2.7 %collective-permute-done.12.other_ref = bf16[384,128]{1,0:T(8,128)(2,1)S(1)} collective-permute-done((bf16[384,128]{1,0:T(8,128)(2,1)S(1)}, bf16[384,128]{1,0:T(8,128)(2,1)S(1)}, u32[]{:S(2)}, u32[]{:S(2)}) %collective-permute-start.12) | collective-permute-done | bytes 98336 | tf_op jit(solution)/shard_map/ppermute | solution.py:243
  42.8 0.8 %finish.1 = (bf16[256,128]{1,0:T(8,128)(2,1)}, f32[128,128]{1,0:T(8,128)}) custom-call(f32[256,128]{1,0:T(8,128)S(1)} %get-tuple-element.35.keep_ref, bf16[384,128]{1,0:T(8,128)(2,1)S(1)} %get-tuple-element.36.own_ref, bf16[384,128]{1,0:T(8,128)(2,1)S(1)} %collective-permute-done.12.other_ref, bf16[128,128]{1,0:T(8,128)(2,1)S(1)} %copy-done), custom_call_target="tpu_custom_call" | custom-call | flops 8388608 | bytes 131072 | tf_op jit(solution)/shard_map/finish/pallas_call | solution.py:407
  (1 shorter events, 0.0 us)
Async XLA Ops:
  0.6 5.7 %copy-start.1 = (bf16[256,128]{1,0:T(8,128)(2,1)S(1)}, bf16[256,128]{1,0:T(8,128)(2,1)}, u32[]{:S(2)}) copy-start(bf16[256,128]{1,0:T(8,128)(2,1)} %refs_0_.3) | copy-start | bytes 196612
  0.6 5.5 %collective-permute-start = (bf16[256,128]{1,0:T(8,128)(2,1)}, bf16[256,128]{1,0:T(8,128)(2,1)S(1)}, u32[]{:S(2)}, u32[]{:S(2)}) collective-permute-start(bf16[256,128]{1,0:T(8,128)(2,1)} %refs_0_.3), channel_id=1, source_target_pairs={{0,16},{8,24},{16,0},{24,8},{1,17},{9,25},{17,1},{25,9},{2,18},{10... | collective-permute-start | bytes 196616 | tf_op jit(solution)/shard_map/ppermute | solution.py:243
  3.7 2.6 %collective-permute-start.1 = (bf16[256,128]{1,0:T(8,128)(2,1)}, bf16[256,128]{1,0:T(8,128)(2,1)S(1)}, u32[]{:S(2)}, u32[]{:S(2)}) collective-permute-start(bf16[256,128]{1,0:T(8,128)(2,1)} %refs_0_.3), channel_id=1, source_target_pairs={{0,8},{8,0},{16,24},{24,16},{1,9},{9,1},{17,25},{25,17},{2,10},{10... | collective-permute-start | bytes 196616 | tf_op jit(solution)/shard_map/ppermute | solution.py:243
  5.7 5.7 %copy-start.2 = (bf16[256,128]{1,0:T(8,128)(2,1)S(1)}, bf16[256,128]{1,0:T(8,128)(2,1)}, u32[]{:S(2)}) copy-start(bf16[256,128]{1,0:T(8,128)(2,1)} %refs_0_.4) | copy-start | bytes 196612
  6.1 1.3 %collective-permute-start.2 = (bf16[256,128]{1,0:T(8,128)(2,1)S(1)}, bf16[256,128]{1,0:T(8,128)(2,1)S(1)}, u32[]{:S(2)}, u32[]{:S(2)}) collective-permute-start(bf16[256,128]{1,0:T(8,128)(2,1)S(1)} %collective-permute-done.refs_1_), channel_id=1, source_target_pairs={{0,8},{8,0},{16,24},{24,16},{1,9},{9,1},{17,25},{25,17},{2,10},{10... | collective-permute-start | bytes 196616 | tf_op jit(solution)/shard_map/ppermute | solution.py:243
  7.1 15.7 %copy-start = (bf16[128,128]{1,0:T(8,128)(2,1)S(1)}, bf16[128,128]{1,0:T(8,128)(2,1)}, u32[]{:S(2)}) copy-start(bf16[128,128]{1,0:T(8,128)(2,1)} %weight_ref.5) | copy-start | bytes 98308
  7.8 8.1 %collective-permute-start.3 = (bf16[512,128]{1,0:T(8,128)(2,1)S(1)}, bf16[512,128]{1,0:T(8,128)(2,1)S(1)}, u32[]{:S(2)}, u32[]{:S(2)}) collective-permute-start(bf16[512,128]{1,0:T(8,128)(2,1)S(1)} %get-tuple-element.26), channel_id=1, source_target_pairs={{0,2},{1,3},{2,0},{3,1},{4,6},{5,7},{6,4},{7,5},{8,10},{9,11},{10,... | collective-permute-start | bytes 393224 | tf_op jit(solution)/shard_map/ppermute | solution.py:243
  9.9 8.1 %collective-permute-start.4 = (bf16[512,128]{1,0:T(8,128)(2,1)S(1)}, bf16[512,128]{1,0:T(8,128)(2,1)S(1)}, u32[]{:S(2)}, u32[]{:S(2)}) collective-permute-start(bf16[512,128]{1,0:T(8,128)(2,1)S(1)} %get-tuple-element.27), channel_id=1, source_target_pairs={{0,1},{1,0},{2,3},{3,2},{4,5},{5,4},{6,7},{7,6},{8,9},{9,8},{10,11... | collective-permute-start | bytes 393224 | tf_op jit(solution)/shard_map/ppermute | solution.py:243
  11.4 6.6 %collective-permute-start.5 = (bf16[512,128]{1,0:T(8,128)(2,1)S(1)}, bf16[512,128]{1,0:T(8,128)(2,1)S(1)}, u32[]{:S(2)}, u32[]{:S(2)}) collective-permute-start(bf16[512,128]{1,0:T(8,128)(2,1)S(1)} %get-tuple-element.28), channel_id=1, source_target_pairs={{0,3},{1,2},{2,1},{3,0},{4,7},{5,6},{6,5},{7,4},{8,11},{9,10},{10,... | collective-permute-start | bytes 393224 | tf_op jit(solution)/shard_map/ppermute | solution.py:243
  11.4 8.7 %collective-permute-start.6 = (bf16[256,128]{1,0:T(8,128)(2,1)S(1)}, bf16[256,128]{1,0:T(8,128)(2,1)S(1)}, u32[]{:S(2)}, u32[]{:S(2)}) collective-permute-start(bf16[256,128]{1,0:T(8,128)(2,1)S(1)} %copy-done.2), channel_id=1, source_target_pairs={{0,6},{1,7},{2,4},{3,5},{4,2},{5,3},{6,0},{7,1},{8,14},{9,15},{10,... | collective-permute-start | bytes 196616 | tf_op jit(solution)/shard_map/ppermute | solution.py:243
  20.2 6.9 %collective-permute-start.7 = (bf16[512,128]{1,0:T(8,128)(2,1)S(1)}, bf16[512,128]{1,0:T(8,128)(2,1)S(1)}, u32[]{:S(2)}, u32[]{:S(2)}) collective-permute-start(bf16[512,128]{1,0:T(8,128)(2,1)S(1)} %add_convert_fusion.left_ref), channel_id=1, source_target_pairs={{0,6},{1,7},{2,4},{3,5},{4,2},{5,3},{6,0},{7,1},{8,14},{9,15},{10,... | collective-permute-start | bytes 393224 | tf_op jit(solution)/shard_map/ppermute | solution.py:243
  27.6 6.6 %collective-permute-start.10 = (bf16[640,128]{1,0:T(8,128)(2,1)S(1)}, bf16[640,128]{1,0:T(8,128)(2,1)S(1)}, u32[]{:S(2)}, u32[]{:S(2)}) collective-permute-start(bf16[640,128]{1,0:T(8,128)(2,1)S(1)} %get-tuple-element.34.grad_ref.refs_0_), channel_id=1, source_target_pairs={{0,3},{1,2},{2,1},{3,0},{4,7},{5,6},{6,5},{7,4},{8,11},{9,10},{10,... | collective-permute-start | bytes 491528 | tf_op jit(solution)/shard_map/ppermute | solution.py:243
  27.9 7.1 %collective-permute-start.9 = (bf16[640,128]{1,0:T(8,128)(2,1)S(1)}, bf16[640,128]{1,0:T(8,128)(2,1)S(1)}, u32[]{:S(2)}, u32[]{:S(2)}) collective-permute-start(bf16[640,128]{1,0:T(8,128)(2,1)S(1)} %get-tuple-element.34.grad_ref.refs_0_), channel_id=1, source_target_pairs={{0,1},{1,0},{2,3},{3,2},{4,5},{5,4},{6,7},{7,6},{8,9},{9,8},{10,11... | collective-permute-start | bytes 491528 | tf_op jit(solution)/shard_map/ppermute | solution.py:243
  29.9 6.0 %collective-permute-start.8 = (bf16[640,128]{1,0:T(8,128)(2,1)S(1)}, bf16[640,128]{1,0:T(8,128)(2,1)S(1)}, u32[]{:S(2)}, u32[]{:S(2)}) collective-permute-start(bf16[640,128]{1,0:T(8,128)(2,1)S(1)} %get-tuple-element.34.grad_ref.refs_0_), channel_id=1, source_target_pairs={{0,2},{1,3},{2,0},{3,1},{4,6},{5,7},{6,4},{7,5},{8,10},{9,11},{10,... | collective-permute-start | bytes 491528 | tf_op jit(solution)/shard_map/ppermute | solution.py:243
  36.4 1.5 %collective-permute-start.11 = (bf16[768,128]{1,0:T(8,128)(2,1)S(1)}, bf16[768,128]{1,0:T(8,128)(2,1)S(1)}, u32[]{:S(2)}, u32[]{:S(2)}) collective-permute-start(bf16[768,128]{1,0:T(8,128)(2,1)S(1)} %backward_sent.1.own_ref), channel_id=1, source_target_pairs={{0,8},{8,0},{16,24},{24,16},{1,9},{9,1},{17,25},{25,17},{2,10},{10... | collective-permute-start | bytes 589832 | tf_op jit(solution)/shard_map/ppermute | solution.py:243
  37.9 4.9 %collective-permute-start.12 = (bf16[384,128]{1,0:T(8,128)(2,1)S(1)}, bf16[384,128]{1,0:T(8,128)(2,1)S(1)}, u32[]{:S(2)}, u32[]{:S(2)}) collective-permute-start(bf16[384,128]{1,0:T(8,128)(2,1)S(1)} %get-tuple-element.36.own_ref), channel_id=1, source_target_pairs={{0,16},{8,24},{16,0},{24,8},{1,17},{9,25},{17,1},{25,9},{2,18},{10... | collective-permute-start | bytes 294920 | tf_op jit(solution)/shard_map/ppermute | solution.py:243

commit v6 on v5

--- a/solution.py
+++ b/solution.py
@@ -198,11 +198,15 @@
     total_ref[...] = columns_of(dense_ref, [grad_ref], 0, slice(0, total_ref.shape[1]))
 
 
+def backward_more(group, dense_ref, grad_ref, before_ref, total_ref):
+    total_ref[...] = columns_of(dense_ref, [grad_ref], group, slice(0, total_ref.shape[1])) + before_ref[...]
+
+
 def backward_sent(dense_ref, total_ref, *refs):
     grads, send_ref = refs[:-1], refs[-1]
     width, kept = total_ref.shape[0], total_ref.shape[1] // 2
     columns = slice(kept, 2 * kept)
-    send_ref[:kept, :] = (columns_of(dense_ref, grads[1:], 1, columns) + total_ref[:, columns]).T.astype(BF16)
+    send_ref[:kept, :] = (columns_of(dense_ref, grads[1:2], 1, columns) + total_ref[:, columns]).T.astype(BF16)
     term = pair_sums([grad[-width:, :].astype(F32) for grad in grads])
     high = term.astype(BF16)
     send_ref[kept : kept + width, :] = high
@@ -304,9 +308,12 @@
 
         flops = 2 * rows * cols * width // len(grads)
         total = some(backward_own, (width, cols), F32, flops, "backward_own", grads[0])
+        for m in range(len(grads) - 1, 1, -1):
+            more = functools.partial(backward_more, m)
+            total = some(more, (width, cols), F32, flops, "backward_more", grads[m], total)
         flops = 2 * rows * cols * width // 2
         send = some(backward_sent, (cols // 2 + 2 * width, width), BF16, flops, "backward_sent", total, *grads)
-        return send, some(backward_kept, (cols // 2, width), F32, flops, "backward_kept", total, *grads[1:])
+        return send, some(backward_kept, (cols // 2, width), F32, flops, "backward_kept", total, *grads[1:2])
 
 
 class TiledBlock:

time: 43.8 us -> 43.6 us (level)
  waiting for transfers between devices: 17 us -> 16.5 us
    ppermute x13, waiting for transfers between devices: 17 us -> 16.5 us  [swap(): return lax.ppermute(x, axis, [(i, i ^ mask) for i in range(n)])]
    pallas_call x3 -> x5, Pallas kernels: 1.3 us -> 1.66 us  [some(): kernel_call(kernel, [(shape, dtype, True)], flops, name, [VM] * (1 + len(...]
  transfers between devices with their start and end apart: 13 -> 13, of which waited for: 10 -> 10; matrix products, arithmetic and copies ran while one was open for 0% -> 0% of each run, Pallas kernels for 10% -> 11%
where the time goes in v6:
time: 43.6 us; the launch traced here: 43.5 us
  starting transfers between devices  18.7 us (43%)
  waiting for transfers between devices  16.5 us (38%)
  Pallas kernels  6.8 us (16%)
  between operations  1.42 us (3%)
    ppermute x13, starting transfers between devices, swap(): return lax.ppermute(x, axis, [(i, i ^ mask) for i in range(n)])  18.7 us
    ppermute x13, waiting for transfers between devices, swap(): return lax.ppermute(x, axis, [(i, i ^ mask) for i in range(n)])  16.5 us
    pallas_call x5, Pallas kernels, some(): kernel_call(kernel, [(shape, dtype, True)], flops, name, [VM] * (1 + len(...  1.66 us
    pallas_call x3, Pallas kernels, some(): kernel_call(kernel, outs, flops, name, [VM] * (1 + len(given)))  1.58 us
    pallas_call x1, Pallas kernels, __init__(): kernel_call(functools.partial(densify, row_of, col_of, DENSIFY_PARTS), [(...  1.36 us
  transfers between devices with their start and end apart: 13, of which 10 were waited for; matrix products, arithmetic and copies ran while one was open for 0% of the time, Pallas kernels for 11%

profile of v6, /device:TPU:0, one launch (start us, length us, event | category | flops | bytes accessed | tf_op | source)
XLA Modules:
  0.0 43.5 jit_solution(2288574886879148388)
XLA Ops:
  0.6 0.0 copy-start.1
  0.6 3.0 %collective-permute-start = (bf16[256,128]{1,0:T(8,128)(2,1)}, bf16[256,128]{1,0:T(8,128)(2,1)S(1)}, u32[]{:S(2)}, u32[]{:S(2)}) collective-permute-start(bf16[256,128]{1,0:T(8,128)(2,1)} %refs_0_.3), channel_id=1, source_target_pairs={{0,16},{8,24},{16,0},{24,8},{1,17},{9,25},{17,1},{25,9},{2,18},{10... | collective-permute-start | bytes 196616 | tf_op jit(solution)/shard_map/ppermute | solution.py:247
  3.7 0.0 collective-permute-start.1
  4.3 1.4 %densify.1.dense_ref = bf16[2176,1024]{1,0:T(8,128)(2,1)S(1)} custom-call(bf16[1,1,44,128,128]{4,3,2,1,0:T(8,128)(2,1)} %tiles_ref.1, s32[1,1,44]{2,1,0:T(1,128)} %slots_ref.1, s32[1,1]{1,0:T(1,128)S(6)} %copy.9.count_ref), custom_call_target="tpu_custom_call" | custom-call | bytes 4456448 | tf_op jit(solution)/shard_map/densify/pallas_call | solution.py:252
  5.7 0.0 copy-start.2
  5.7 0.4 collective-permute-done.refs_1_
  6.1 0.2 collective-permute-start.2
  6.3 0.0 collective-permute-done.1.refs_2_
  6.3 0.0 copy-done.1
  6.3 0.8 %forward_early.1.total_ref = f32[1536,128]{1,0:T(8,128)S(1)} custom-call(bf16[2176,1024]{1,0:T(8,128)(2,1)S(1)} %densify.1.dense_ref, bf16[256,128]{1,0:T(8,128)(2,1)S(1)} %copy-done.1, bf16[256,128]{1,0:T(8,128)(2,1)S(1)} %collective-permute-done.refs_1_, bf16[256,128]{1,0:T(8,128)(2,1)S(1)} %collective-permute-done.1.refs_2_), custom_call_target="tpu_custom_call" | custom-call | flops 301989888 | bytes 786432 | tf_op jit(solution)/shard_map/forward_early/pallas_call | solution.py:279
  7.1 0.0 copy-start
  7.1 0.3 collective-permute-done.2.refs_3_.piece_ref
  7.4 0.4 forward_sent.1
  7.8 2.1 %collective-permute-start.3 = (bf16[512,128]{1,0:T(8,128)(2,1)S(1)}, bf16[512,128]{1,0:T(8,128)(2,1)S(1)}, u32[]{:S(2)}, u32[]{:S(2)}) collective-permute-start(bf16[512,128]{1,0:T(8,128)(2,1)S(1)} %get-tuple-element.26), channel_id=1, source_target_pairs={{0,2},{1,3},{2,0},{3,1},{4,6},{5,7},{6,4},{7,5},{8,10},{9,11},{10,... | collective-permute-start | bytes 393224 | tf_op jit(solution)/shard_map/ppermute | solution.py:247
  9.9 1.5 %collective-permute-start.4 = (bf16[512,128]{1,0:T(8,128)(2,1)S(1)}, bf16[512,128]{1,0:T(8,128)(2,1)S(1)}, u32[]{:S(2)}, u32[]{:S(2)}) collective-permute-start(bf16[512,128]{1,0:T(8,128)(2,1)S(1)} %get-tuple-element.27), channel_id=1, source_target_pairs={{0,1},{1,0},{2,3},{3,2},{4,5},{5,4},{6,7},{7,6},{8,9},{9,8},{10,11... | collective-permute-start | bytes 393224 | tf_op jit(solution)/shard_map/ppermute | solution.py:247
  11.4 0.0 collective-permute-start.5
  11.4 0.0 copy-done.2
  11.4 4.0 %collective-permute-start.6 = (bf16[256,128]{1,0:T(8,128)(2,1)S(1)}, bf16[256,128]{1,0:T(8,128)(2,1)S(1)}, u32[]{:S(2)}, u32[]{:S(2)}) collective-permute-start(bf16[256,128]{1,0:T(8,128)(2,1)S(1)} %copy-done.2), channel_id=1, source_target_pairs={{0,6},{1,7},{2,4},{3,5},{4,2},{5,3},{6,0},{7,1},{8,14},{9,15},{10,... | collective-permute-start | bytes 196616 | tf_op jit(solution)/shard_map/ppermute | solution.py:247
  15.4 0.4 %forward_own.1 = f32[512,128]{1,0:T(8,128)S(1)} custom-call(bf16[2176,1024]{1,0:T(8,128)(2,1)S(1)} %densify.1.dense_ref, bf16[256,128]{1,0:T(8,128)(2,1)S(1)} %copy-done.1, bf16[256,128]{1,0:T(8,128)(2,1)S(1)} %collective-permute-done.refs_1_, bf16[256,128]{1,0:T(8,128)(2,1)S(1)} %collective-permute-done.1.refs_2_, ...), custom_call_target="tpu_custom_call" | custom-call | flops 134217728 | bytes 262144 | tf_op jit(solution)/shard_map/forward_own/pallas_call | solution.py:279
  15.9 0.0 collective-permute-done.3
  15.9 2.1 %collective-permute-done.4 = bf16[512,128]{1,0:T(8,128)(2,1)S(1)} collective-permute-done((bf16[512,128]{1,0:T(8,128)(2,1)S(1)}, bf16[512,128]{1,0:T(8,128)(2,1)S(1)}, u32[]{:S(2)}, u32[]{:S(2)}) %collective-permute-start.4) | collective-permute-done | bytes 131104 | tf_op jit(solution)/shard_map/ppermute | solution.py:247
  18.0 0.0 collective-permute-done.5
  18.0 0.1 add_convert_fusion.left_ref
  18.1 2.1 %collective-permute-done.6.refs_1_ = bf16[256,128]{1,0:T(8,128)(2,1)S(1)} collective-permute-done((bf16[256,128]{1,0:T(8,128)(2,1)S(1)}, bf16[256,128]{1,0:T(8,128)(2,1)S(1)}, u32[]{:S(2)}, u32[]{:S(2)}) %collective-permute-start.6) | collective-permute-done | bytes 65568 | tf_op jit(solution)/shard_map/ppermute | solution.py:247
  20.2 2.6 %collective-permute-start.7 = (bf16[512,128]{1,0:T(8,128)(2,1)S(1)}, bf16[512,128]{1,0:T(8,128)(2,1)S(1)}, u32[]{:S(2)}, u32[]{:S(2)}) collective-permute-start(bf16[512,128]{1,0:T(8,128)(2,1)S(1)} %add_convert_fusion.left_ref), channel_id=1, source_target_pairs={{0,6},{1,7},{2,4},{3,5},{4,2},{5,3},{6,0},{7,1},{8,14},{9,15},{10,... | collective-permute-start | bytes 393224 | tf_op jit(solution)/shard_map/ppermute | solution.py:247
  22.8 0.0 copy-done
  22.8 0.2 project.1.first_ref
  22.9 4.1 %collective-permute-done.7.right_ref = bf16[512,128]{1,0:T(8,128)(2,1)S(1)} collective-permute-done((bf16[512,128]{1,0:T(8,128)(2,1)S(1)}, bf16[512,128]{1,0:T(8,128)(2,1)S(1)}, u32[]{:S(2)}, u32[]{:S(2)}) %collective-permute-start.7) | collective-permute-done | bytes 131104 | tf_op jit(solution)/shard_map/ppermute | solution.py:247
  27.0 0.6 %middle.1 = (bf16[640,128]{1,0:T(8,128)(2,1)S(1)}, bf16[256,128]{1,0:T(8,128)(2,1)S(1)}) custom-call(f32[512,128]{1,0:T(8,128)S(1)} %project.1.first_ref, bf16[512,128]{1,0:T(8,128)(2,1)S(1)} %add_convert_fusion.left_ref, bf16[512,128]{1,0:T(8,128)(2,1)S(1)} %collective-permute-done.7.right_ref, bf16[128,128]{1,0:T(8,128)(2,1)S(1)} %copy-done, ...), custom_call_target="tpu_custom_call" | custom-call | flops 50331648 | bytes 229376 | tf_op jit(solution)/shard_map/middle/pallas_call | solution.py:390
  27.6 0.3 collective-permute-start.9
  27.9 2.0 %collective-permute-start.8 = (bf16[640,128]{1,0:T(8,128)(2,1)S(1)}, bf16[640,128]{1,0:T(8,128)(2,1)S(1)}, u32[]{:S(2)}, u32[]{:S(2)}) collective-permute-start(bf16[640,128]{1,0:T(8,128)(2,1)S(1)} %get-tuple-element.34.grad_ref.refs_0_), channel_id=1, source_target_pairs={{0,1},{1,0},{2,3},{3,2},{4,5},{5,4},{6,7},{7,6},{8,9},{9,8},{10,11... | collective-permute-start | bytes 491528 | tf_op jit(solution)/shard_map/ppermute | solution.py:247
  29.9 1.2 %collective-permute-start.10 = (bf16[640,128]{1,0:T(8,128)(2,1)S(1)}, bf16[640,128]{1,0:T(8,128)(2,1)S(1)}, u32[]{:S(2)}, u32[]{:S(2)}) collective-permute-start(bf16[640,128]{1,0:T(8,128)(2,1)S(1)} %get-tuple-element.34.grad_ref.refs_0_), channel_id=1, source_target_pairs={{0,2},{1,3},{2,0},{3,1},{4,6},{5,7},{6,4},{7,5},{8,10},{9,11},{10,... | collective-permute-start | bytes 491528 | tf_op jit(solution)/shard_map/ppermute | solution.py:247
  31.2 0.3 backward_own.1.before_ref
  31.5 2.7 %collective-permute-done.9.grad_ref.refs_3_ = bf16[640,128]{1,0:T(8,128)(2,1)S(1)} collective-permute-done((bf16[640,128]{1,0:T(8,128)(2,1)S(1)}, bf16[640,128]{1,0:T(8,128)(2,1)S(1)}, u32[]{:S(2)}, u32[]{:S(2)}) %collective-permute-start.9) | collective-permute-done | bytes 163872 | tf_op jit(solution)/shard_map/ppermute | solution.py:247
  34.2 0.3 backward_more.2.before_ref
  34.5 0.5 %collective-permute-done.8.grad_ref.refs_2_ = bf16[640,128]{1,0:T(8,128)(2,1)S(1)} collective-permute-done((bf16[640,128]{1,0:T(8,128)(2,1)S(1)}, bf16[640,128]{1,0:T(8,128)(2,1)S(1)}, u32[]{:S(2)}, u32[]{:S(2)}) %collective-permute-start.8) | collective-permute-done | bytes 163872 | tf_op jit(solution)/shard_map/ppermute | solution.py:247
  35.0 0.3 backward_more.3.total_ref
  35.3 0.6 %collective-permute-done.10.refs_0_.refs_1_ = bf16[640,128]{1,0:T(8,128)(2,1)S(1)} collective-permute-done((bf16[640,128]{1,0:T(8,128)(2,1)S(1)}, bf16[640,128]{1,0:T(8,128)(2,1)S(1)}, u32[]{:S(2)}, u32[]{:S(2)}) %collective-permute-start.10) | collective-permute-done | bytes 163872 | tf_op jit(solution)/shard_map/ppermute | solution.py:247
  35.9 0.3 backward_sent.1.own_ref
  36.2 0.1 collective-permute-start.11
  36.3 0.4 backward_kept.1.keep_ref
  36.6 1.1 %collective-permute-done.11.other_ref = bf16[768,128]{1,0:T(8,128)(2,1)S(1)} collective-permute-done((bf16[768,128]{1,0:T(8,128)(2,1)S(1)}, bf16[768,128]{1,0:T(8,128)(2,1)S(1)}, u32[]{:S(2)}, u32[]{:S(2)}) %collective-permute-start.11) | collective-permute-done | bytes 196640 | tf_op jit(solution)/shard_map/ppermute | solution.py:247
  37.8 1.6 %collective-permute-start.12 = (bf16[384,128]{1,0:T(8,128)(2,1)S(1)}, bf16[384,128]{1,0:T(8,128)(2,1)S(1)}, u32[]{:S(2)}, u32[]{:S(2)}) collective-permute-start(bf16[384,128]{1,0:T(8,128)(2,1)S(1)} %get-tuple-element.36.own_ref), channel_id=1, source_target_pairs={{0,16},{8,24},{16,0},{24,8},{1,17},{9,25},{17,1},{25,9},{2,18},{10... | collective-permute-start | bytes 294920 | tf_op jit(solution)/shard_map/ppermute | solution.py:247
  39.3 0.6 %emit.1 = bf16[256,128]{1,0:T(8,128)(2,1)} custom-call(bf16[256,128]{1,0:T(8,128)(2,1)S(1)} %get-tuple-element.33.given_ref), custom_call_target="tpu_custom_call" | custom-call | bytes 65536 | tf_op jit(solution)/shard_map/emit/pallas_call | solution.py:397
  40.0 2.7 %collective-permute-done.12.other_ref = bf16[384,128]{1,0:T(8,128)(2,1)S(1)} collective-permute-done((bf16[384,128]{1,0:T(8,128)(2,1)S(1)}, bf16[384,128]{1,0:T(8,128)(2,1)S(1)}, u32[]{:S(2)}, u32[]{:S(2)}) %collective-permute-start.12) | collective-permute-done | bytes 98336 | tf_op jit(solution)/shard_map/ppermute | solution.py:247
  42.7 0.8 %finish.1 = (bf16[256,128]{1,0:T(8,128)(2,1)}, f32[128,128]{1,0:T(8,128)}) custom-call(f32[256,128]{1,0:T(8,128)S(1)} %get-tuple-element.35.keep_ref, bf16[384,128]{1,0:T(8,128)(2,1)S(1)} %get-tuple-element.36.own_ref, bf16[384,128]{1,0:T(8,128)(2,1)S(1)} %collective-permute-done.12.other_ref, bf16[128,128]{1,0:T(8,128)(2,1)S(1)} %copy-done), custom_call_target="tpu_custom_call" | custom-call | flops 8388608 | bytes 131072 | tf_op jit(solution)/shard_map/finish/pallas_call | solution.py:414
  (1 shorter events, 0.0 us)
Async XLA Ops:
  0.6 5.7 %copy-start.1 = (bf16[256,128]{1,0:T(8,128)(2,1)S(1)}, bf16[256,128]{1,0:T(8,128)(2,1)}, u32[]{:S(2)}) copy-start(bf16[256,128]{1,0:T(8,128)(2,1)} %refs_0_.3) | copy-start | bytes 196612
  0.6 5.5 %collective-permute-start = (bf16[256,128]{1,0:T(8,128)(2,1)}, bf16[256,128]{1,0:T(8,128)(2,1)S(1)}, u32[]{:S(2)}, u32[]{:S(2)}) collective-permute-start(bf16[256,128]{1,0:T(8,128)(2,1)} %refs_0_.3), channel_id=1, source_target_pairs={{0,16},{8,24},{16,0},{24,8},{1,17},{9,25},{17,1},{25,9},{2,18},{10... | collective-permute-start | bytes 196616 | tf_op jit(solution)/shard_map/ppermute | solution.py:247
  3.7 2.6 %collective-permute-start.1 = (bf16[256,128]{1,0:T(8,128)(2,1)}, bf16[256,128]{1,0:T(8,128)(2,1)S(1)}, u32[]{:S(2)}, u32[]{:S(2)}) collective-permute-start(bf16[256,128]{1,0:T(8,128)(2,1)} %refs_0_.3), channel_id=1, source_target_pairs={{0,8},{8,0},{16,24},{24,16},{1,9},{9,1},{17,25},{25,17},{2,10},{10... | collective-permute-start | bytes 196616 | tf_op jit(solution)/shard_map/ppermute | solution.py:247
  5.7 5.7 %copy-start.2 = (bf16[256,128]{1,0:T(8,128)(2,1)S(1)}, bf16[256,128]{1,0:T(8,128)(2,1)}, u32[]{:S(2)}) copy-start(bf16[256,128]{1,0:T(8,128)(2,1)} %refs_0_.4) | copy-start | bytes 196612
  6.1 1.3 %collective-permute-start.2 = (bf16[256,128]{1,0:T(8,128)(2,1)S(1)}, bf16[256,128]{1,0:T(8,128)(2,1)S(1)}, u32[]{:S(2)}, u32[]{:S(2)}) collective-permute-start(bf16[256,128]{1,0:T(8,128)(2,1)S(1)} %collective-permute-done.refs_1_), channel_id=1, source_target_pairs={{0,8},{8,0},{16,24},{24,16},{1,9},{9,1},{17,25},{25,17},{2,10},{10... | collective-permute-start | bytes 196616 | tf_op jit(solution)/shard_map/ppermute | solution.py:247
  7.1 15.7 %copy-start = (bf16[128,128]{1,0:T(8,128)(2,1)S(1)}, bf16[128,128]{1,0:T(8,128)(2,1)}, u32[]{:S(2)}) copy-start(bf16[128,128]{1,0:T(8,128)(2,1)} %weight_ref.5) | copy-start | bytes 98308
  7.8 8.1 %collective-permute-start.3 = (bf16[512,128]{1,0:T(8,128)(2,1)S(1)}, bf16[512,128]{1,0:T(8,128)(2,1)S(1)}, u32[]{:S(2)}, u32[]{:S(2)}) collective-permute-start(bf16[512,128]{1,0:T(8,128)(2,1)S(1)} %get-tuple-element.26), channel_id=1, source_target_pairs={{0,2},{1,3},{2,0},{3,1},{4,6},{5,7},{6,4},{7,5},{8,10},{9,11},{10,... | collective-permute-start | bytes 393224 | tf_op jit(solution)/shard_map/ppermute | solution.py:247
  9.9 8.1 %collective-permute-start.4 = (bf16[512,128]{1,0:T(8,128)(2,1)S(1)}, bf16[512,128]{1,0:T(8,128)(2,1)S(1)}, u32[]{:S(2)}, u32[]{:S(2)}) collective-permute-start(bf16[512,128]{1,0:T(8,128)(2,1)S(1)} %get-tuple-element.27), channel_id=1, source_target_pairs={{0,1},{1,0},{2,3},{3,2},{4,5},{5,4},{6,7},{7,6},{8,9},{9,8},{10,11... | collective-permute-start | bytes 393224 | tf_op jit(solution)/shard_map/ppermute | solution.py:247
  11.4 6.6 %collective-permute-start.5 = (bf16[512,128]{1,0:T(8,128)(2,1)S(1)}, bf16[512,128]{1,0:T(8,128)(2,1)S(1)}, u32[]{:S(2)}, u32[]{:S(2)}) collective-permute-start(bf16[512,128]{1,0:T(8,128)(2,1)S(1)} %get-tuple-element.28), channel_id=1, source_target_pairs={{0,3},{1,2},{2,1},{3,0},{4,7},{5,6},{6,5},{7,4},{8,11},{9,10},{10,... | collective-permute-start | bytes 393224 | tf_op jit(solution)/shard_map/ppermute | solution.py:247
  11.4 8.7 %collective-permute-start.6 = (bf16[256,128]{1,0:T(8,128)(2,1)S(1)}, bf16[256,128]{1,0:T(8,128)(2,1)S(1)}, u32[]{:S(2)}, u32[]{:S(2)}) collective-permute-start(bf16[256,128]{1,0:T(8,128)(2,1)S(1)} %copy-done.2), channel_id=1, source_target_pairs={{0,6},{1,7},{2,4},{3,5},{4,2},{5,3},{6,0},{7,1},{8,14},{9,15},{10,... | collective-permute-start | bytes 196616 | tf_op jit(solution)/shard_map/ppermute | solution.py:247
  20.2 6.9 %collective-permute-start.7 = (bf16[512,128]{1,0:T(8,128)(2,1)S(1)}, bf16[512,128]{1,0:T(8,128)(2,1)S(1)}, u32[]{:S(2)}, u32[]{:S(2)}) collective-permute-start(bf16[512,128]{1,0:T(8,128)(2,1)S(1)} %add_convert_fusion.left_ref), channel_id=1, source_target_pairs={{0,6},{1,7},{2,4},{3,5},{4,2},{5,3},{6,0},{7,1},{8,14},{9,15},{10,... | collective-permute-start | bytes 393224 | tf_op jit(solution)/shard_map/ppermute | solution.py:247
  27.6 6.6 %collective-permute-start.9 = (bf16[640,128]{1,0:T(8,128)(2,1)S(1)}, bf16[640,128]{1,0:T(8,128)(2,1)S(1)}, u32[]{:S(2)}, u32[]{:S(2)}) collective-permute-start(bf16[640,128]{1,0:T(8,128)(2,1)S(1)} %get-tuple-element.34.grad_ref.refs_0_), channel_id=1, source_target_pairs={{0,3},{1,2},{2,1},{3,0},{4,7},{5,6},{6,5},{7,4},{8,11},{9,10},{10,... | collective-permute-start | bytes 491528 | tf_op jit(solution)/shard_map/ppermute | solution.py:247
  27.9 7.1 %collective-permute-start.8 = (bf16[640,128]{1,0:T(8,128)(2,1)S(1)}, bf16[640,128]{1,0:T(8,128)(2,1)S(1)}, u32[]{:S(2)}, u32[]{:S(2)}) collective-permute-start(bf16[640,128]{1,0:T(8,128)(2,1)S(1)} %get-tuple-element.34.grad_ref.refs_0_), channel_id=1, source_target_pairs={{0,1},{1,0},{2,3},{3,2},{4,5},{5,4},{6,7},{7,6},{8,9},{9,8},{10,11... | collective-permute-start | bytes 491528 | tf_op jit(solution)/shard_map/ppermute | solution.py:247
  29.9 6.0 %collective-permute-start.10 = (bf16[640,128]{1,0:T(8,128)(2,1)S(1)}, bf16[640,128]{1,0:T(8,128)(2,1)S(1)}, u32[]{:S(2)}, u32[]{:S(2)}) collective-permute-start(bf16[640,128]{1,0:T(8,128)(2,1)S(1)} %get-tuple-element.34.grad_ref.refs_0_), channel_id=1, source_target_pairs={{0,2},{1,3},{2,0},{3,1},{4,6},{5,7},{6,4},{7,5},{8,10},{9,11},{10,... | collective-permute-start | bytes 491528 | tf_op jit(solution)/shard_map/ppermute | solution.py:247
  36.2 1.5 %collective-permute-start.11 = (bf16[768,128]{1,0:T(8,128)(2,1)S(1)}, bf16[768,128]{1,0:T(8,128)(2,1)S(1)}, u32[]{:S(2)}, u32[]{:S(2)}) collective-permute-start(bf16[768,128]{1,0:T(8,128)(2,1)S(1)} %backward_sent.1.own_ref), channel_id=1, source_target_pairs={{0,8},{8,0},{16,24},{24,16},{1,9},{9,1},{17,25},{25,17},{2,10},{10... | collective-permute-start | bytes 589832 | tf_op jit(solution)/shard_map/ppermute | solution.py:247
  37.8 4.9 %collective-permute-start.12 = (bf16[384,128]{1,0:T(8,128)(2,1)S(1)}, bf16[384,128]{1,0:T(8,128)(2,1)S(1)}, u32[]{:S(2)}, u32[]{:S(2)}) collective-permute-start(bf16[384,128]{1,0:T(8,128)(2,1)S(1)} %get-tuple-element.36.own_ref), channel_id=1, source_target_pairs={{0,16},{8,24},{16,0},{24,8},{1,17},{9,25},{17,1},{25,9},{2,18},{10... | collective-permute-start | bytes 294920 | tf_op jit(solution)/shard_map/ppermute | solution.py:247
